TPU v7x, 32 devices: a whole 2x2x4 slice. The times are simulated.
32 devices in a mesh: pipe: 4 (over y, x), dp: 8 (over z, core).
Axes of the slice: x: 2, y: 2, z: 4, core: 2. Of those that a mesh axis runs over, the one named last changes fastest.
Arguments:
- new_input: bfloat16 [4, 1024, 8192], P('pipe', 'dp'), may hold values from -400 to 400
- new_gain: bfloat16 [4, 8192], P('pipe'), may hold values from 0.5 to 1.5
- queries: bfloat16 [4, 1024, 4096], P('pipe', 'dp'), may hold values from -5 to 5
- new_keys: bfloat16 [4, 1024, 512], P('pipe', 'dp'), may hold values from -5 to 5
- context_grad: bfloat16 [4, 1024, 4096], P('pipe', 'dp'), may hold values from -0.08984375 to 0.08984375
- segment_ids: int32 [4, 1024], P('pipe', 'dp'), may hold values from 0 to 15, never falling along the last dimension, each value on 1 to 128 neighbouring positions
- frozen_input: bfloat16 [4, 1024, 8192], P('pipe', 'dp'), may hold values from -400 to 400
- frozen_gain: bfloat16 [4, 8192], P('pipe'), may hold values from 0.5 to 1.5
- output_grad: bfloat16 [4, 1024, 8192], P('pipe', 'dp'), may hold values from -6 to 6
- kv_grad: bfloat16 [4, 1024, 1024], P('pipe', 'dp'), may hold values from -18 to 18
- kv_weight: bfloat16 [4, 8192, 1024], P('pipe', 'dp'), may hold values from -0.0625 to 0.0625
Outputs:
- cot_below: bfloat16 [4, 1024, 8192], P('pipe', 'dp')
- value_grad: float32 [4, 8192, 512], P('pipe', 'dp')
Inputs may be any that keep to these rules, and one draw needn't show every extreme that they name: `segment_ids`: within a section the numbers never fall; every number of 0 to 15 appears, on 1 to 128 positions in a row, one on exactly 128.
All inputs are finite; a program needn't handle non-finite values.
Results may differ from a plain program's by a relative error of at most 0.0056.
Values may be sent and summed in bfloat16 or wider, within the bound.
No kernel may reach another device: no remote copies, remote signals or barrier semaphores. Data moves between devices by JAX's collectives and lax.ppermute only.
A program may use at most 128 MiB of HBM per device.

v0:
```python
import functools
import math

import jax
import jax.numpy as jnp
from jax import lax
from jax.experimental import pallas as pl
from jax.experimental.pallas import tpu as pltpu
from jax.sharding import PartitionSpec as P

HEAD = 128
CORES = 2
MIB = 1 << 20

norm_eps = 1e-05
masked_value = -1e30

whole = pl.BlockSpec(memory_space=pl.ANY)
scalars = pl.BlockSpec(memory_space=pltpu.SMEM)


def from_behind(array, axis, by):
    length = lax.axis_size(axis)
    pairs = [(i, i + by) for i in range(length) if 0 <= i + by < length]
    return lax.ppermute(array, axis, pairs)


def along_chips(array, by, first=0):
    length = lax.axis_size("dp")
    pairs = [
        (line * length + i, line * length + ((i + by * CORES) % length if line >= first else i ^ 1))
        for line in range(lax.axis_size("pipe")) for i in range(length)
    ]
    return lax.ppermute(array, ("pipe", "dp"), pairs)


def between_lines(array, source, target):
    length = lax.axis_size("dp")
    pairs = [(source * length + i, target * length + i) for i in range(length)]
    return lax.ppermute(array, ("pipe", "dp"), pairs)


def on_line(array, by, line):
    length = lax.axis_size("dp")
    pairs = [(line * length + i, line * length + (i + by * CORES) % length) for i in range(length)]
    return lax.ppermute(array, ("pipe", "dp"), pairs)


def swap_cores(array):
    length = lax.axis_size("dp")
    return lax.ppermute(array, "dp", [(i, i ^ 1) for i in range(length)])


def call(body, name, flops, nbytes, vmem=24, **kwargs):
    return pl.pallas_call(
        body,
        name=name,
        compiler_params=pltpu.CompilerParams(vmem_limit_bytes=vmem * MIB),
        cost_estimate=pl.CostEstimate(flops=flops, bytes_accessed=nbytes, transcendentals=0),
        **kwargs,
    )


def part_columns(chip, half, core, width):
    owner = chip * CORES + (core if half == 0 else CORES - 1 - core)
    return pl.ds(pl.multiple_of(owner * width, width), width)


def norm_kernel(chips, ahead, place_ref, x_ref, gain_ref, cot_ref, *rest):
    out_refs = rest[-len(ahead):]
    chip, core = place_ref[0], place_ref[1]
    values = x_ref[...].astype(jnp.float32)
    inverse = lax.rsqrt(jnp.mean(values * values, axis=-1, keepdims=True) + norm_eps)
    front = cot_ref.shape[1]
    width = (out_refs[0].shape[1] - front) // CORES
    for by, out_ref in zip(ahead, out_refs):
        to = lax.rem(chip + by, chips)
        out_ref[:, :front] = cot_ref[...]
        for half in range(CORES):
            cols = part_columns(to, half, core, width)
            out_ref[:, front + half * width:front + (half + 1) * width] = (
                x_ref[:, cols].astype(jnp.float32) * inverse * gain_ref[:, cols].astype(jnp.float32)
            ).astype(out_ref.dtype)


def normalize(place, rows, gain, cot, chips, ahead, start, count, after):
    width = rows.shape[1]
    front = cot.shape[1]
    block = math.gcd(math.gcd(start, count), 32)
    first = start // block
    out_width = front + width // chips
    return list(call(
        functools.partial(norm_kernel, chips, ahead), "norm_forward",
        4 * count * width, 2 * count * width + 2 * count * out_width * len(ahead),
        grid=(count // block,),
        in_specs=[
            scalars,
            pl.BlockSpec((block, width), lambda i: (first + i, 0)),
            pl.BlockSpec((1, width), lambda i: (0, 0)),
            pl.BlockSpec((block, front), lambda i: (first + i, 0)),
        ] + [whole] * len(after),
        out_specs=[pl.BlockSpec((block, out_width), lambda i: (i, 0))] * len(ahead),
        out_shape=[jax.ShapeDtypeStruct((count, out_width), jnp.bfloat16)] * len(ahead),
    )(place, rows, gain, cot, *after))


def stack_kernel(count, *refs):
    at = 0
    for ref in refs[:count]:
        refs[-1][at:at + ref.shape[0]] = ref[...]
        at += ref.shape[0]


def stack_rows(arrays, after):
    width = arrays[0].shape[1]
    tall = sum(array.shape[0] for array in arrays)
    return call(
        functools.partial(stack_kernel, len(arrays)), "stack_rows", 0, 4 * tall * width,
        grid=(1,),
        in_specs=[pl.BlockSpec(array.shape, lambda i: (0, 0)) for array in arrays] + [whole] * len(after),
        out_specs=pl.BlockSpec((tall, width), lambda i: (0, 0)),
        out_shape=jax.ShapeDtypeStruct((tall, width), arrays[0].dtype),
    )(*arrays, *after)


def attend_kernel(query_ref, key_ref, grad_ref, row_seg_ref, col_seg_ref, out_ref):
    tokens = key_ref.shape[0]
    group = query_ref.shape[1] // HEAD
    at_query = lax.broadcasted_iota(jnp.int32, (tokens, tokens), 0)
    at_key = lax.broadcasted_iota(jnp.int32, (tokens, tokens), 1)
    visible = (col_seg_ref[...] == row_seg_ref[...]) & (at_key <= at_query)
    keys = key_ref[...]
    total = jnp.zeros((tokens, HEAD), jnp.float32)
    for head in range(group):
        cols = slice(head * HEAD, (head + 1) * HEAD)
        scores = lax.dot_general(
            query_ref[:, cols], keys, (((1,), (1,)), ((), ())),
            preferred_element_type=jnp.float32,
        ) / math.sqrt(HEAD)
        masked = jnp.where(visible, scores, masked_value)
        highest = jnp.max(masked, axis=-1, keepdims=True)
        weights = jnp.where(visible, jnp.exp(masked - highest), 0.0)
        attention = (weights / jnp.sum(weights, axis=-1, keepdims=True)).astype(jnp.bfloat16)
        total += lax.dot_general(
            attention, grad_ref[:, cols], (((0,), (0,)), ((), ())),
            preferred_element_type=jnp.float32,
        )
    out_ref[...] = total.astype(out_ref.dtype)


def attend(queries, keys, grads, segments):
    tokens, kv_width = keys.shape
    heads = kv_width // HEAD
    wide = queries.shape[1] // heads
    return call(
        attend_kernel, "attend",
        4 * tokens * tokens * queries.shape[1], 4 * tokens * queries.shape[1],
        grid=(heads,),
        in_specs=[
            pl.BlockSpec((tokens, wide), lambda i: (0, i)),
            pl.BlockSpec((tokens, HEAD), lambda i: (0, i)),
            pl.BlockSpec((tokens, wide), lambda i: (0, i)),
            pl.BlockSpec((1, tokens), lambda i: (0, 0)),
            pl.BlockSpec((tokens, 1), lambda i: (0, 0)),
        ],
        out_specs=pl.BlockSpec((tokens, HEAD), lambda i: (0, i)),
        out_shape=jax.ShapeDtypeStruct((tokens, kv_width), jnp.bfloat16),
    )(queries, keys, grads, segments, segments.reshape(tokens, 1))


def project_kernel(chips, steps, cuts, own_ref, other_ref, *rest):
    row_refs, out_refs, gathered = rest[:chips], rest[-chips * (len(cuts) - 1) - 1:-1], rest[-1]
    taken, depth = row_refs[0].shape
    step = pl.program_id(0)

    @pl.when(step == 0)
    def _():
        for by in range(chips):
            gathered[by] = row_refs[by][...]

    def multiply(weight_ref):
        product = lax.dot_general(
            gathered[...].reshape(chips * taken, depth), weight_ref[...], (((1,), (1,)), ((), ())),
            preferred_element_type=jnp.float32,
        ).astype(jnp.bfloat16)
        for part, (start, end) in enumerate(zip(cuts, cuts[1:])):
            for by in range(chips):
                out_refs[part * chips + by][...] = product[by * taken + start:by * taken + end]

    @pl.when(step < steps)
    def _():
        multiply(own_ref)

    @pl.when(step >= steps)
    def _():
        multiply(other_ref)


def project(rows, own, other, cuts, after):
    chips = len(rows)
    taken, depth = rows[0].shape
    width = own.shape[0]
    block = min(width, 512)
    steps = width // block
    counts = [end - start for start, end in zip(cuts, cuts[1:]) for by in range(chips)]
    results = list(call(
        functools.partial(project_kernel, chips, steps, cuts), "project",
        4 * chips * taken * depth * width, 2 * (chips * taken * (depth + 2 * width) + 2 * width * depth),
        grid=(CORES * steps,),
        in_specs=[
            pl.BlockSpec((block, depth), lambda i: (jnp.minimum(i, steps - 1), 0)),
            pl.BlockSpec((block, depth), lambda i: (jnp.maximum(i - steps, 0), 0)),
        ] + [pl.BlockSpec((taken, depth), lambda i: (0, 0))] * chips + [whole] * len(after),
        out_specs=[pl.BlockSpec((count, block), lambda i: (0, i)) for count in counts],
        out_shape=[jax.ShapeDtypeStruct((count, CORES * width), jnp.bfloat16) for count in counts],
        scratch_shapes=[pltpu.VMEM((chips, taken, depth), jnp.bfloat16)],
    )(own, other, *rows, *after))
    return [results[at:at + chips] for at in range(0, len(results), chips)]


def backward_kernel(chips, place_ref, x_ref, gain_ref, grad_ref, *rest):
    cot_refs, out_ref = rest[:chips], rest[-1]
    chip, core = place_ref[0], place_ref[1]
    values = x_ref[...].astype(jnp.float32)
    width = cot_refs[0].shape[1] // CORES
    inverse = lax.rsqrt(jnp.mean(values * values, axis=-1, keepdims=True) + norm_eps)
    inner = jnp.zeros_like(inverse)

    def parts():
        for by, cot_ref in enumerate(cot_refs):
            source = lax.rem(chip + chips - by, chips)
            for half in range(CORES):
                cols = part_columns(source, half, core, width)
                cot = cot_ref[:, half * width:(half + 1) * width].astype(jnp.float32)
                yield cols, gain_ref[:, cols].astype(jnp.float32) * cot

    for cols, scaled in parts():
        inner += jnp.sum(x_ref[:, cols].astype(jnp.float32) * scaled, axis=-1, keepdims=True)
    factor = inverse * inverse * inverse * (inner / x_ref.shape[1])
    for cols, scaled in parts():
        out_ref[:, cols] = (
            grad_ref[:, cols].astype(jnp.float32)
            + inverse * scaled
            - x_ref[:, cols].astype(jnp.float32) * factor
        ).astype(out_ref.dtype)


def norm_backward(place, cots, rows, gain, grads, start, after):
    tokens, width = rows.shape
    taken, part_width = cots[0].shape
    block = math.gcd(math.gcd(start, taken), 32)
    first = start // block
    return call(
        functools.partial(backward_kernel, len(cots)), "norm_backward",
        10 * taken * width, 8 * taken * width,
        grid=(taken // block,),
        in_specs=[
            scalars,
            pl.BlockSpec((block, width), lambda i: (first + i, 0)),
            pl.BlockSpec((1, width), lambda i: (0, 0)),
            pl.BlockSpec((block, width), lambda i: (first + i, 0)),
        ] + [pl.BlockSpec((block, part_width), lambda i: (i, 0))] * len(cots) + [whole] * len(after),
        out_specs=pl.BlockSpec((block, width), lambda i: (i, 0)),
        out_shape=jax.ShapeDtypeStruct((taken, width), jnp.bfloat16),
    )(place, rows, gain, grads, *cots, *after)


def outer_kernel(groups, sums, halves, *refs):
    arrays = sum(groups)
    cots, columns, terms = refs[:arrays], refs[arrays:2 * arrays], refs[2 * arrays:2 * arrays + sums]
    total, at = None, 0
    for size in groups:
        column, cot = columns[at][...], cots[at][...]
        for more in range(at + 1, at + size):
            column, cot = column + columns[more][...], cot + cots[more][...]
        at += size
        product = lax.dot_general(
            column, cot, (((0,), (0,)), ((), ())), preferred_element_type=jnp.float32
        )
        total = product if total is None else total + product
    for term in terms:
        total += term[...].astype(jnp.float32)
    if halves:
        lower, upper = refs[2 * arrays + sums:2 * arrays + sums + 2]
        in_lower = pl.program_id(0) < pl.num_programs(0) // 2
        total += jnp.where(in_lower, lower[...], upper[...]).astype(jnp.float32)
    refs[-1][...] = total.astype(refs[-1].dtype)


def outer(groups, cot_width, half, before, dtype, part=0, parts=1, halves=(), after=()):
    payloads = [payload for group in groups for payload in group]
    wide = payloads[0].shape[1]
    width = (wide - cot_width) // CORES
    block = math.gcd(math.gcd(width // 2, 256), cot_width)
    steps = width // parts // block
    skip = part * steps
    first = (cot_width + half * width) // block + skip
    middle = steps // 2
    tokens = sum(payload.shape[0] for payload in payloads)
    return call(
        functools.partial(outer_kernel, [len(group) for group in groups], len(before), len(halves)), "outer",
        2 * tokens * width * cot_width, 2 * tokens * width + 4 * width * cot_width,
        grid=(steps,),
        in_specs=[pl.BlockSpec((payload.shape[0], cot_width), lambda i: (0, 0)) for payload in payloads]
        + [pl.BlockSpec((payload.shape[0], block), lambda i: (0, first + i)) for payload in payloads]
        + [pl.BlockSpec((block, cot_width), lambda i: (skip + i, 0)) for term in before]
        + [
            pl.BlockSpec((block, cot_width), lambda i: (jnp.minimum(i, middle - 1), 0)),
            pl.BlockSpec((block, cot_width), lambda i: (jnp.maximum(i - middle, 0), 0)),
        ][:len(halves)]
        + [whole] * len(after),
        out_specs=pl.BlockSpec((block, cot_width), lambda i: (i, 0)),
        out_shape=jax.ShapeDtypeStruct((width // parts, cot_width), dtype),
    )(*payloads, *payloads, *before, *halves, *after)


def shards(
    new_input,
    new_gain,
    queries,
    new_keys,
    context_grad,
    segment_ids,
    frozen_input,
    frozen_gain,
    output_grad,
    kv_grad,
    kv_weight,
):
    chips = lax.axis_size("dp") // CORES
    sections = lax.axis_size("pipe")
    tokens, kv_width = new_keys.shape[1:]
    at = lax.axis_index("dp")
    place = jnp.stack([at // CORES, at % CORES]).astype(jnp.int32)
    middle = chips // 2
    near = [by for by in range(1, chips) if by != middle]
    spread = tokens // 4

    rows = [kv_grad[0]] + [along_chips(kv_grad[0], chips - by, 1) for by in range(1, chips)]
    other_weight = swap_cores(kv_weight[0])
    value_cot = attend(queries[0], new_keys[0], context_grad[0], segment_ids)

    apply = functools.partial(normalize, place, new_input[0], new_gain, value_cot, chips)
    shared = apply([middle], 0, spread, [other_weight])[0]
    brought = [between_lines(shared, section, 0) for section in range(1, sections)]
    early = apply([0] + near[:1], 0, tokens, rows[1:])
    columns = [early[0]] + [along_chips(block, by) for block, by in zip(early[1:], near)]
    joint = stack_rows([shared] + brought, early[:1])
    moved = on_line(joint, middle, 0)
    returned = [moved[:spread]] + [
        between_lines(moved[section * spread:(section + 1) * spread], 0, section) for section in range(1, sections)
    ]

    cuts = [0, tokens * 5 // 8, tokens]
    parts = project(rows, kv_weight[0], other_weight, cuts, [joint])
    arrived = [
        [part[0]] + [along_chips(part[by], by, 1) for by in range(1, chips)] for part in parts
    ]
    backward = functools.partial(norm_backward, place, rows=frozen_input[0], gain=frozen_gain, grads=output_grad[0])
    above = backward(arrived[0], start=cuts[0], after=columns[1:])
    kept = apply([middle], spread, tokens - spread, [above] + [arrived[1][by] for by in near])
    late = apply(near[1:], 0, tokens, kept)
    above = [above, backward(arrived[1], start=cuts[1], after=late[:1])]
    below = [from_behind(half, "pipe", -1) for half in above]
    cot_below = stack_rows(below, [])

    groups = [[column] for column in columns] + [returned]
    last = [[along_chips(block, by)] for block, by in zip(late + kept, near[1:] + [middle])]
    sums = [outer(groups, kv_width, half, [], jnp.float32, after=above[1:]) for half in range(CORES)]
    given = [
        outer(last, kv_width, 1, sums[1:], jnp.bfloat16, part, 2, after=sums[:1]) for part in range(2)
    ]
    taken = [swap_cores(part) for part in given]
    grad = outer(last, kv_width, 0, sums[:1], jnp.float32, halves=taken, after=[cot_below])
    return (cot_below[None], grad[None])


def solution(mesh):
    placed = (
        P("pipe", "dp", None),
        P("pipe", None),
        P("pipe", "dp", None),
        P("pipe", "dp", None),
        P("pipe", "dp", None),
        P("pipe", "dp"),
        P("pipe", "dp", None),
        P("pipe", None),
        P("pipe", "dp", None),
        P("pipe", "dp", None),
        P("pipe", "dp", None),
    )
    return jax.shard_map(
        shards,
        mesh=mesh,
        in_specs=placed,
        out_specs=(P("pipe", "dp", None), P("pipe", "dp", None)),
        check_vma=False,
    )
```

profile of v0, /device:TPU:10, one launch (start us, length us, event | category | flops | bytes accessed | tf_op | source)
XLA Modules:
  0.0 141.0 jit_solution(12803258349543433222)
XLA Ops:
  0.7 0.5 collective-permute-start.1
  1.2 2.6 %collective-permute-start.2 = (bf16[128,1024]{1,0:T(8,128)(2,1)}, bf16[128,1024]{1,0:T(8,128)(2,1)S(1)}, u32[]{:S(2)}, u32[]{:S(2)}) collective-permute-start(bf16[128,1024]{1,0:T(8,128)(2,1)} %bitcast.29), channel_id=1, source_target_pairs={{0,1},{1,0},{2,3},{3,2},{4,5},{5,4},{6,7},{7,6},{8,12},{9,13},{10,... | collective-permute-start | bytes 786440 | tf_op jit(solution)/shard_map/ppermute | solution.py:34
  3.8 2.5 %collective-permute-start.3 = (bf16[128,1024]{1,0:T(8,128)(2,1)}, bf16[128,1024]{1,0:T(8,128)(2,1)S(1)}, u32[]{:S(2)}, u32[]{:S(2)}) collective-permute-start(bf16[128,1024]{1,0:T(8,128)(2,1)} %bitcast.30), channel_id=1, source_target_pairs={{0,1},{1,0},{2,3},{3,2},{4,5},{5,4},{6,7},{7,6},{8,10},{9,11},{10,... | collective-permute-start | bytes 786440 | tf_op jit(solution)/shard_map/ppermute | solution.py:34
  6.3 0.8 copy.13.col_seg_ref
  7.1 1.2 copy-done.4
  8.3 1.2 copy-done.5
  9.5 0.9 copy-done.8
  10.4 0.7 copy-done.9
  11.1 4.5 %attend.1.cot_ref = bf16[128,512]{1,0:T(8,128)(2,1)S(1)} custom-call(bf16[128,4096]{1,0:T(8,128)(2,1)S(1)} %bitcast.22, bf16[128,512]{1,0:T(8,128)(2,1)S(1)} %bitcast.24, bf16[128,4096]{1,0:T(8,128)(2,1)S(1)} %bitcast.23, s32[1,128]{1,0:T(1,128)S(1)} %copy-done.9, s32[128,1]{1,0:T(8,128)S(1)} %copy.13.col_seg_ref), custom_call_target="tpu_custom_call" | custom-call | flops 268435456 | bytes 2097152 | tf_op jit(solution)/shard_map/attend/pallas_call | solution.py:155
  15.6 0.1 pad_add_fusion.place_ref
  15.6 0.8 norm_forward.4.refs_0_
  16.4 1.4 %collective-permute-start.4 = (bf16[32,2560]{1,0:T(8,128)(2,1)S(1)}, bf16[32,2560]{1,0:T(8,128)(2,1)S(1)}, u32[]{:S(2)}, u32[]{:S(2)}) collective-permute-start(bf16[32,2560]{1,0:T(8,128)(2,1)S(1)} %norm_forward.4.refs_0_), channel_id=1, source_target_pairs={{8,0},{9,1},{10,2},{11,3},{12,4},{13,5},{14,6},{15,7}} | collective-permute-start | bytes 491528 | tf_op jit(solution)/shard_map/ppermute | solution.py:40
  17.9 0.7 collective-permute-start.5
  18.6 0.7 collective-permute-start.6
  19.2 2.8 %collective-permute-done.2.rest_1_.rest_2_ = bf16[128,1024]{1,0:T(8,128)(2,1)S(1)} collective-permute-done((bf16[128,1024]{1,0:T(8,128)(2,1)}, bf16[128,1024]{1,0:T(8,128)(2,1)S(1)}, u32[]{:S(2)}, u32[]{:S(2)}) %collective-permute-start.2) | collective-permute-done | bytes 262176 | tf_op jit(solution)/shard_map/ppermute | solution.py:34
  22.1 4.8 %collective-permute-done.3.rest_2_.rest_3_ = bf16[128,1024]{1,0:T(8,128)(2,1)S(1)} collective-permute-done((bf16[128,1024]{1,0:T(8,128)(2,1)}, bf16[128,1024]{1,0:T(8,128)(2,1)S(1)}, u32[]{:S(2)}, u32[]{:S(2)}) %collective-permute-start.3) | collective-permute-done | bytes 262176 | tf_op jit(solution)/shard_map/ppermute | solution.py:34
  26.9 1.5 %norm_forward.5 = (bf16[128,2560]{1,0:T(8,128)(2,1)S(1)}, bf16[128,2560]{1,0:T(8,128)(2,1)S(1)}) custom-call(s32[2]{0:T(128)S(1)} %pad_add_fusion.place_ref, bf16[128,8192]{1,0:T(8,128)(2,1)S(1)} %bitcast.14, bf16[1,8192]{1,0:T(2,128)(2,1)S(1)} %copy-done.6, bf16[128,512]{1,0:T(8,128)(2,1)S(1)} %attend.1.cot_ref, ...), custom_call_target="tpu_custom_call" | custom-call | flops 4194304 | bytes 3407872 | tf_op jit(solution)/shard_map/norm_forward/pallas_call | solution.py:92
  28.5 2.4 %collective-permute-start.10 = (bf16[128,2560]{1,0:T(8,128)(2,1)S(1)}, bf16[128,2560]{1,0:T(8,128)(2,1)S(1)}, u32[]{:S(2)}, u32[]{:S(2)}) collective-permute-start(bf16[128,2560]{1,0:T(8,128)(2,1)S(1)} %get-tuple-element.17), channel_id=1, source_target_pairs={{0,2},{1,3},{2,4},{3,5},{4,6},{5,7},{6,0},{7,1},{8,10},{9,11},{10,... | collective-permute-start | bytes 1966088 | tf_op jit(solution)/shard_map/ppermute | solution.py:34
  31.0 0.8 collective-permute-start.18
  31.9 5.4 %project.1 = (bf16[80,2048]{1,0:T(8,128)(2,1)S(1)}, bf16[80,2048]{1,0:T(8,128)(2,1)S(1)}, bf16[80,2048]{1,0:T(8,128)(2,1)S(1)}, bf16[80,2048]{1,0:T(8,128)(2,1)S...) custom-call(bf16[1024,1024]{1,0:T(8,128)(2,1)S(1)} %bitcast.27, ...), custom_call_target="tpu_custom_call" | custom-call | flops 2147483648 | bytes 7340032 | tf_op jit(solution)/shard_map/project/pallas_call | solution.py:206
  37.2 0.1 collective-permute-start.7
  37.3 2.0 %collective-permute-start.8 = (bf16[80,2048]{1,0:T(8,128)(2,1)S(1)}, bf16[80,2048]{1,0:T(8,128)(2,1)S(1)}, u32[]{:S(2)}, u32[]{:S(2)}) collective-permute-start(bf16[80,2048]{1,0:T(8,128)(2,1)S(1)} %get-tuple-element.15), channel_id=1, source_target_pairs={{0,1},{1,0},{2,3},{3,2},{4,5},{5,4},{6,7},{7,6},{8,12},{9,13},{10,... | collective-permute-start | bytes 983048 | tf_op jit(solution)/shard_map/ppermute | solution.py:34
  39.3 1.0 collective-permute-start.9
  40.4 5.8 %collective-permute-done.10.rest_4_.refs_1_.refs_7_ = bf16[128,2560]{1,0:T(8,128)(2,1)S(1)} collective-permute-done((bf16[128,2560]{1,0:T(8,128)(2,1)S(1)}, bf16[128,2560]{1,0:T(8,128)(2,1)S(1)}, u32[]{:S(2)}, u32[]{:S(2)}) %collective-permute-start.10) | collective-permute-done | bytes 655392 | tf_op jit(solution)/shard_map/ppermute | solution.py:34
  46.2 2.4 %collective-permute-start.12 = (bf16[48,2048]{1,0:T(8,128)(2,1)S(1)}, bf16[48,2048]{1,0:T(8,128)(2,1)S(1)}, u32[]{:S(2)}, u32[]{:S(2)}) collective-permute-start(bf16[48,2048]{1,0:T(8,128)(2,1)S(1)} %get-tuple-element.19), channel_id=1, source_target_pairs={{0,1},{1,0},{2,3},{3,2},{4,5},{5,4},{6,7},{7,6},{8,10},{9,11},{10,... | collective-permute-start | bytes 589832 | tf_op jit(solution)/shard_map/ppermute | solution.py:34
  48.6 18.6 %collective-permute-done.7.rest_1_ = bf16[80,2048]{1,0:T(8,128)(2,1)S(1)} collective-permute-done((bf16[80,2048]{1,0:T(8,128)(2,1)S(1)}, bf16[80,2048]{1,0:T(8,128)(2,1)S(1)}, u32[]{:S(2)}, u32[]{:S(2)}) %collective-permute-start.7) | collective-permute-done | bytes 327712 | tf_op jit(solution)/shard_map/ppermute | solution.py:34
  67.2 15.4 %collective-permute-done.8.rest_2_ = bf16[80,2048]{1,0:T(8,128)(2,1)S(1)} collective-permute-done((bf16[80,2048]{1,0:T(8,128)(2,1)S(1)}, bf16[80,2048]{1,0:T(8,128)(2,1)S(1)}, u32[]{:S(2)}, u32[]{:S(2)}) %collective-permute-start.8) | collective-permute-done | bytes 327712 | tf_op jit(solution)/shard_map/ppermute | solution.py:34
  82.6 3.4 %collective-permute-start.13 = (bf16[48,2048]{1,0:T(8,128)(2,1)S(1)}, bf16[48,2048]{1,0:T(8,128)(2,1)S(1)}, u32[]{:S(2)}, u32[]{:S(2)}) collective-permute-start(bf16[48,2048]{1,0:T(8,128)(2,1)S(1)} %get-tuple-element.20), channel_id=1, source_target_pairs={{0,1},{1,0},{2,3},{3,2},{4,5},{5,4},{6,7},{7,6},{8,12},{9,13},{10,... | collective-permute-start | bytes 589832 | tf_op jit(solution)/shard_map/ppermute | solution.py:34
  86.0 2.5 %norm_backward.2.rest_0_ = bf16[80,8192]{1,0:T(8,128)(2,1)S(1)} custom-call(s32[2]{0:T(128)S(1)} %pad_add_fusion.place_ref, bf16[128,8192]{1,0:T(8,128)(2,1)S(1)} %bitcast.17, bf16[1,8192]{1,0:T(2,128)(2,1)S(1)} %copy-done.7, bf16[128,8192]{1,0:T(8,128)(2,1)S(1)} %bitcast.19, bf16[80,2048]{1,0:T(8,128)(2,1)S(1)} %get-tuple-element.13.rest_0_, ...), custom_call_target="tpu_custom_call" | custom-call | flops 6553600 | bytes 5242880 | tf_op jit(solution)/shard_map/norm_backward/pallas_call | solution.py:253
  88.5 1.9 %collective-permute-start.11 = (bf16[80,8192]{1,0:T(8,128)(2,1)S(1)}, bf16[80,8192]{1,0:T(8,128)(2,1)S(1)}, u32[]{:S(2)}, u32[]{:S(2)}) collective-permute-start(bf16[80,8192]{1,0:T(8,128)(2,1)S(1)} %norm_backward.2.rest_0_), channel_id=1, source_target_pairs={{8,0},{16,8},{24,16},{9,1},{17,9},{25,17},{10,2},{18,10},{26,18},{... | collective-permute-start | bytes 3932168 | tf_op jit(solution)/shard_map/ppermute | solution.py:25
  90.5 1.3 norm_forward.6.rest_0_
  91.8 1.5 %norm_forward.7.rest_4_ = bf16[128,2560]{1,0:T(8,128)(2,1)S(1)} custom-call(s32[2]{0:T(128)S(1)} %pad_add_fusion.place_ref, bf16[128,8192]{1,0:T(8,128)(2,1)S(1)} %bitcast.16, bf16[1,8192]{1,0:T(2,128)(2,1)S(1)} %copy-done.6, bf16[128,512]{1,0:T(8,128)(2,1)S(1)} %attend.1.cot_ref, bf16[96,2560]{1,0:T(8,128)(2,1)S(1)} %norm_forward.6.rest_0_), custom_call_target="tpu_custom_call" | custom-call | flops 4194304 | bytes 2752512 | tf_op jit(solution)/shard_map/norm_forward/pallas_call | solution.py:92
  93.3 0.3 collective-permute-start.16
  93.7 1.3 collective-permute-start.19
  95.0 19.8 %collective-permute-done.13.rest_2_ = bf16[48,2048]{1,0:T(8,128)(2,1)S(1)} collective-permute-done((bf16[48,2048]{1,0:T(8,128)(2,1)S(1)}, bf16[48,2048]{1,0:T(8,128)(2,1)S(1)}, u32[]{:S(2)}, u32[]{:S(2)}) %collective-permute-start.13) | collective-permute-done | bytes 196640 | tf_op jit(solution)/shard_map/ppermute | solution.py:34
  114.7 0.7 collective-permute-start.20
  115.4 0.7 collective-permute-start.21
  116.1 1.7 %norm_backward.3.refs_12_ = bf16[48,8192]{1,0:T(8,128)(2,1)S(1)} custom-call(s32[2]{0:T(128)S(1)} %pad_add_fusion.place_ref, bf16[128,8192]{1,0:T(8,128)(2,1)S(1)} %bitcast.18, bf16[1,8192]{1,0:T(2,128)(2,1)S(1)} %copy-done.7, bf16[128,8192]{1,0:T(8,128)(2,1)S(1)} %bitcast.20, bf16[48,2048]{1,0:T(8,128)(2,1)S(1)} %get-tuple-element.18.rest_0_, ...), custom_call_target="tpu_custom_call" | custom-call | flops 3932160 | bytes 3145728 | tf_op jit(solution)/shard_map/norm_backward/pallas_call | solution.py:253
  117.8 6.1 %collective-permute-start.15 = (bf16[48,8192]{1,0:T(8,128)(2,1)S(1)}, bf16[48,8192]{1,0:T(8,128)(2,1)S(1)}, u32[]{:S(2)}, u32[]{:S(2)}) collective-permute-start(bf16[48,8192]{1,0:T(8,128)(2,1)S(1)} %norm_backward.3.refs_12_), channel_id=1, source_target_pairs={{8,0},{16,8},{24,16},{9,1},{17,9},{25,17},{10,2},{18,10},{26,18},{... | collective-permute-start | bytes 2359304 | tf_op jit(solution)/shard_map/ppermute | solution.py:25
  124.0 1.8 %outer.6.refs_4_ = f32[1024,512]{1,0:T(8,128)S(1)} custom-call(bf16[128,2560]{1,0:T(8,128)(2,1)S(1)} %get-tuple-element.12.refs_4_.refs_0_.refs_6_, bf16[128,2560]{1,0:T(8,128)(2,1)S(1)} %collective-permute-done.10.rest_4_.refs_1_.refs_7_, bf16[32,2560]{1,0:T(8,128)(2,1)S(1)} %get-tuple-element.25.refs_2_.refs_8_, ...), custom_call_target="tpu_custom_call" | custom-call | flops 402653184 | bytes 2883584 | tf_op jit(solution)/shard_map/outer/pallas_call | solution.py:300
  125.8 1.8 %outer.5.refs_5_.refs_4_ = f32[1024,512]{1,0:T(8,128)S(1)} custom-call(bf16[128,2560]{1,0:T(8,128)(2,1)S(1)} %get-tuple-element.12.refs_4_.refs_0_.refs_6_, bf16[128,2560]{1,0:T(8,128)(2,1)S(1)} %collective-permute-done.10.rest_4_.refs_1_.refs_7_, bf16[32,2560]{1,0:T(8,128)(2,1)S(1)} %get-tuple-element.25.refs_2_.refs_8_, ...), custom_call_target="tpu_custom_call" | custom-call | flops 402653184 | bytes 2883584 | tf_op jit(solution)/shard_map/outer/pallas_call | solution.py:300
  127.7 0.7 outer.8
  128.5 0.7 outer.7
  129.3 0.5 collective-permute-start.22
  129.8 5.5 %collective-permute-done.15.refs_1_ = bf16[48,8192]{1,0:T(8,128)(2,1)S(1)} collective-permute-done((bf16[48,8192]{1,0:T(8,128)(2,1)S(1)}, bf16[48,8192]{1,0:T(8,128)(2,1)S(1)}, u32[]{:S(2)}, u32[]{:S(2)}) %collective-permute-start.15) | collective-permute-done | bytes 786464 | tf_op jit(solution)/shard_map/ppermute | solution.py:25
  135.3 1.5 %stack_rows.3.refs_7_ = bf16[128,8192]{1,0:T(8,128)(2,1)} custom-call(bf16[80,8192]{1,0:T(8,128)(2,1)S(1)} %collective-permute-done.11.refs_0_, bf16[48,8192]{1,0:T(8,128)(2,1)S(1)} %collective-permute-done.15.refs_1_), custom_call_target="tpu_custom_call" | custom-call | bytes 4194304 | tf_op jit(solution)/shard_map/stack_rows/pallas_call | solution.py:117
  136.8 1.6 %copy-done.3 = bf16[128,8192]{1,0:T(8,128)(2,1)S(1)} copy-done((bf16[128,8192]{1,0:T(8,128)(2,1)S(1)}, bf16[128,8192]{1,0:T(8,128)(2,1)}, u32[]{:S(2)}) %copy-start.3) | copy-done | bytes 2097176
  138.4 2.6 %outer.9 = f32[1024,512]{1,0:T(8,128)} custom-call(bf16[128,2560]{1,0:T(8,128)(2,1)S(1)} %collective-permute-done.16.refs_0_.refs_2_, bf16[96,2560]{1,0:T(8,128)(2,1)S(1)} %collective-permute-done.17.refs_1_.refs_3_, bf16[128,2560]{1,0:T(8,128)(2,1)S(1)} %collective-permute-done.16.refs_0_.refs_2_, ...), custom_call_target="tpu_custom_call" | custom-call | flops 234881024 | bytes 2555904 | tf_op jit(solution)/shard_map/outer/pallas_call | solution.py:300
  (42 shorter events, 0.4 us)
Async XLA Ops:
  0.6 15.0 %copy-start = (bf16[1,128,8192]{2,1,0:T(8,128)(2,1)S(1)}, bf16[1,128,8192]{2,1,0:T(8,128)(2,1)}, u32[]{:S(2)}) copy-start(bf16[1,128,8192]{2,1,0:T(8,128)(2,1)} %param.11) | copy-start | bytes 6291460
  0.6 15.0 %collective-permute-start = (bf16[1024,1024]{1,0:T(8,128)(2,1)}, bf16[1024,1024]{1,0:T(8,128)(2,1)}, u32[]{:S(2)}, u32[]{:S(2)}) collective-permute-start(bf16[1024,1024]{1,0:T(8,128)(2,1)} %bitcast.26), channel_id=1, source_target_pairs={{0,1},{1,0},{2,3},{3,2},{4,5},{5,4},{6,7},{7,6},{8,9},{9,8},{10,11... | collective-permute-start | bytes 6291464 | tf_op jit(solution)/shard_map/ppermute | solution.py:51
  0.7 17.8 %collective-permute-start.1 = (bf16[128,1024]{1,0:T(8,128)(2,1)}, bf16[128,1024]{1,0:T(8,128)(2,1)S(1)}, u32[]{:S(2)}, u32[]{:S(2)}) collective-permute-start(bf16[128,1024]{1,0:T(8,128)(2,1)} %bitcast.28), channel_id=1, source_target_pairs={{0,1},{1,0},{2,3},{3,2},{4,5},{5,4},{6,7},{7,6},{8,14},{9,15},{10,... | collective-permute-start | bytes 786440 | tf_op jit(solution)/shard_map/ppermute | solution.py:34
  1.2 20.8 %collective-permute-start.2 = (bf16[128,1024]{1,0:T(8,128)(2,1)}, bf16[128,1024]{1,0:T(8,128)(2,1)S(1)}, u32[]{:S(2)}, u32[]{:S(2)}) collective-permute-start(bf16[128,1024]{1,0:T(8,128)(2,1)} %bitcast.29), channel_id=1, source_target_pairs={{0,1},{1,0},{2,3},{3,2},{4,5},{5,4},{6,7},{7,6},{8,12},{9,13},{10,... | collective-permute-start | bytes 786440 | tf_op jit(solution)/shard_map/ppermute | solution.py:34
  3.8 23.1 %collective-permute-start.3 = (bf16[128,1024]{1,0:T(8,128)(2,1)}, bf16[128,1024]{1,0:T(8,128)(2,1)S(1)}, u32[]{:S(2)}, u32[]{:S(2)}) collective-permute-start(bf16[128,1024]{1,0:T(8,128)(2,1)} %bitcast.30), channel_id=1, source_target_pairs={{0,1},{1,0},{2,3},{3,2},{4,5},{5,4},{6,7},{7,6},{8,10},{9,11},{10,... | collective-permute-start | bytes 786440 | tf_op jit(solution)/shard_map/ppermute | solution.py:34
  7.1 1.2 copy-start.4
  8.3 1.2 copy-start.5
  9.5 0.9 copy-start.8
  10.4 0.7 copy-start.9
  11.1 4.6 %copy-start.6 = (bf16[1,8192]{1,0:T(2,128)(2,1)S(1)}, bf16[1,8192]{1,0:T(2,128)(2,1)}, u32[]{:S(2)}) copy-start(bf16[1,8192]{1,0:T(2,128)(2,1)} %gain_ref.10) | copy-start | bytes 49156
  16.4 15.4 %copy-start.10 = (bf16[1,1024,1024]{2,1,0:T(8,128)(2,1)S(1)}, bf16[1,1024,1024]{2,1,0:T(8,128)(2,1)}, u32[]{:S(2)}) copy-start(bf16[1,1024,1024]{2,1,0:T(8,128)(2,1)} %param.21) | copy-start | bytes 6291460
  16.4 15.4 %copy-start.11 = (bf16[1,128,1024]{2,1,0:T(8,128)(2,1)S(1)}, bf16[1,128,1024]{2,1,0:T(8,128)(2,1)}, u32[]{:S(2)}) copy-start(bf16[1,128,1024]{2,1,0:T(8,128)(2,1)} %param.20) | copy-start | bytes 786436
  16.4 14.5 %collective-permute-start.4 = (bf16[32,2560]{1,0:T(8,128)(2,1)S(1)}, bf16[32,2560]{1,0:T(8,128)(2,1)S(1)}, u32[]{:S(2)}, u32[]{:S(2)}) collective-permute-start(bf16[32,2560]{1,0:T(8,128)(2,1)S(1)} %norm_forward.4.refs_0_), channel_id=1, source_target_pairs={{8,0},{9,1},{10,2},{11,3},{12,4},{13,5},{14,6},{15,7}} | collective-permute-start | bytes 491528 | tf_op jit(solution)/shard_map/ppermute | solution.py:40
  17.9 13.0 %collective-permute-start.5 = (bf16[32,2560]{1,0:T(8,128)(2,1)S(1)}, bf16[32,2560]{1,0:T(8,128)(2,1)S(1)}, u32[]{:S(2)}, u32[]{:S(2)}) collective-permute-start(bf16[32,2560]{1,0:T(8,128)(2,1)S(1)} %norm_forward.4.refs_0_), channel_id=1, source_target_pairs={{16,0},{17,1},{18,2},{19,3},{20,4},{21,5},{22,6},{23,7}} | collective-permute-start | bytes 491528 | tf_op jit(solution)/shard_map/ppermute | solution.py:40
  18.6 12.3 %collective-permute-start.6 = (bf16[32,2560]{1,0:T(8,128)(2,1)S(1)}, bf16[32,2560]{1,0:T(8,128)(2,1)S(1)}, u32[]{:S(2)}, u32[]{:S(2)}) collective-permute-start(bf16[32,2560]{1,0:T(8,128)(2,1)S(1)} %norm_forward.4.refs_0_), channel_id=1, source_target_pairs={{24,0},{25,1},{26,2},{27,3},{28,4},{29,5},{30,6},{31,7}} | collective-permute-start | bytes 491528 | tf_op jit(solution)/shard_map/ppermute | solution.py:40
  28.5 17.7 %collective-permute-start.10 = (bf16[128,2560]{1,0:T(8,128)(2,1)S(1)}, bf16[128,2560]{1,0:T(8,128)(2,1)S(1)}, u32[]{:S(2)}, u32[]{:S(2)}) collective-permute-start(bf16[128,2560]{1,0:T(8,128)(2,1)S(1)} %get-tuple-element.17), channel_id=1, source_target_pairs={{0,2},{1,3},{2,4},{3,5},{4,6},{5,7},{6,0},{7,1},{8,10},{9,11},{10,... | collective-permute-start | bytes 1966088 | tf_op jit(solution)/shard_map/ppermute | solution.py:34
  31.0 55.0 %copy-start.1 = (bf16[1,128,8192]{2,1,0:T(8,128)(2,1)S(1)}, bf16[1,128,8192]{2,1,0:T(8,128)(2,1)}, u32[]{:S(2)}) copy-start(bf16[1,128,8192]{2,1,0:T(8,128)(2,1)} %param.17) | copy-start | bytes 6291460
  31.0 55.0 %copy-start.2 = (bf16[1,128,8192]{2,1,0:T(8,128)(2,1)S(1)}, bf16[1,128,8192]{2,1,0:T(8,128)(2,1)}, u32[]{:S(2)}) copy-start(bf16[1,128,8192]{2,1,0:T(8,128)(2,1)} %param.19) | copy-start | bytes 6291460
  31.0 55.0 %copy-start.7 = (bf16[1,8192]{1,0:T(2,128)(2,1)S(1)}, bf16[1,8192]{1,0:T(2,128)(2,1)}, u32[]{:S(2)}) copy-start(bf16[1,8192]{1,0:T(2,128)(2,1)} %gain_ref.11) | copy-start | bytes 49156
  31.0 62.6 %collective-permute-start.18 = (bf16[128,2560]{1,0:T(8,128)(2,1)S(1)}, bf16[128,2560]{1,0:T(8,128)(2,1)S(1)}, u32[]{:S(2)}, u32[]{:S(2)}) collective-permute-start(bf16[128,2560]{1,0:T(8,128)(2,1)S(1)} %stack_rows.2.rest_4_), channel_id=1, source_target_pairs={{0,4},{1,5},{2,6},{3,7},{4,0},{5,1},{6,2},{7,3}} | collective-permute-start | bytes 1966088 | tf_op jit(solution)/shard_map/ppermute | solution.py:46
  37.2 29.9 %collective-permute-start.7 = (bf16[80,2048]{1,0:T(8,128)(2,1)S(1)}, bf16[80,2048]{1,0:T(8,128)(2,1)S(1)}, u32[]{:S(2)}, u32[]{:S(2)}) collective-permute-start(bf16[80,2048]{1,0:T(8,128)(2,1)S(1)} %get-tuple-element.14), channel_id=1, source_target_pairs={{0,1},{1,0},{2,3},{3,2},{4,5},{5,4},{6,7},{7,6},{8,10},{9,11},{10,... | collective-permute-start | bytes 983048 | tf_op jit(solution)/shard_map/ppermute | solution.py:34
  37.3 45.3 %collective-permute-start.8 = (bf16[80,2048]{1,0:T(8,128)(2,1)S(1)}, bf16[80,2048]{1,0:T(8,128)(2,1)S(1)}, u32[]{:S(2)}, u32[]{:S(2)}) collective-permute-start(bf16[80,2048]{1,0:T(8,128)(2,1)S(1)} %get-tuple-element.15), channel_id=1, source_target_pairs={{0,1},{1,0},{2,3},{3,2},{4,5},{5,4},{6,7},{7,6},{8,12},{9,13},{10,... | collective-permute-start | bytes 983048 | tf_op jit(solution)/shard_map/ppermute | solution.py:34
  39.3 46.7 %collective-permute-start.9 = (bf16[80,2048]{1,0:T(8,128)(2,1)S(1)}, bf16[80,2048]{1,0:T(8,128)(2,1)S(1)}, u32[]{:S(2)}, u32[]{:S(2)}) collective-permute-start(bf16[80,2048]{1,0:T(8,128)(2,1)S(1)} %get-tuple-element.16), channel_id=1, source_target_pairs={{0,1},{1,0},{2,3},{3,2},{4,5},{5,4},{6,7},{7,6},{8,14},{9,15},{10,... | collective-permute-start | bytes 983048 | tf_op jit(solution)/shard_map/ppermute | solution.py:34
  46.2 44.3 %collective-permute-start.12 = (bf16[48,2048]{1,0:T(8,128)(2,1)S(1)}, bf16[48,2048]{1,0:T(8,128)(2,1)S(1)}, u32[]{:S(2)}, u32[]{:S(2)}) collective-permute-start(bf16[48,2048]{1,0:T(8,128)(2,1)S(1)} %get-tuple-element.19), channel_id=1, source_target_pairs={{0,1},{1,0},{2,3},{3,2},{4,5},{5,4},{6,7},{7,6},{8,10},{9,11},{10,... | collective-permute-start | bytes 589832 | tf_op jit(solution)/shard_map/ppermute | solution.py:34
  67.2 23.3 %collective-permute-start.14 = (bf16[48,2048]{1,0:T(8,128)(2,1)S(1)}, bf16[48,2048]{1,0:T(8,128)(2,1)S(1)}, u32[]{:S(2)}, u32[]{:S(2)}) collective-permute-start(bf16[48,2048]{1,0:T(8,128)(2,1)S(1)} %get-tuple-element.21), channel_id=1, source_target_pairs={{0,1},{1,0},{2,3},{3,2},{4,5},{5,4},{6,7},{7,6},{8,14},{9,15},{10,... | collective-permute-start | bytes 589832 | tf_op jit(solution)/shard_map/ppermute | solution.py:34
  82.6 32.1 %collective-permute-start.13 = (bf16[48,2048]{1,0:T(8,128)(2,1)S(1)}, bf16[48,2048]{1,0:T(8,128)(2,1)S(1)}, u32[]{:S(2)}, u32[]{:S(2)}) collective-permute-start(bf16[48,2048]{1,0:T(8,128)(2,1)S(1)} %get-tuple-element.20), channel_id=1, source_target_pairs={{0,1},{1,0},{2,3},{3,2},{4,5},{5,4},{6,7},{7,6},{8,12},{9,13},{10,... | collective-permute-start | bytes 589832 | tf_op jit(solution)/shard_map/ppermute | solution.py:34
  88.5 46.8 %collective-permute-start.11 = (bf16[80,8192]{1,0:T(8,128)(2,1)S(1)}, bf16[80,8192]{1,0:T(8,128)(2,1)S(1)}, u32[]{:S(2)}, u32[]{:S(2)}) collective-permute-start(bf16[80,8192]{1,0:T(8,128)(2,1)S(1)} %norm_backward.2.rest_0_), channel_id=1, source_target_pairs={{8,0},{16,8},{24,16},{9,1},{17,9},{25,17},{10,2},{18,10},{26,18},{... | collective-permute-start | bytes 3932168 | tf_op jit(solution)/shard_map/ppermute | solution.py:25
  91.8 35.9 %collective-permute-start.17 = (bf16[96,2560]{1,0:T(8,128)(2,1)S(1)}, bf16[96,2560]{1,0:T(8,128)(2,1)S(1)}, u32[]{:S(2)}, u32[]{:S(2)}) collective-permute-start(bf16[96,2560]{1,0:T(8,128)(2,1)S(1)} %norm_forward.6.rest_0_), channel_id=1, source_target_pairs={{0,4},{1,5},{2,6},{3,7},{4,0},{5,1},{6,2},{7,3},{8,12},{9,13},{10,... | collective-permute-start | bytes 1474568 | tf_op jit(solution)/shard_map/ppermute | solution.py:34
  93.3 34.4 %collective-permute-start.16 = (bf16[128,2560]{1,0:T(8,128)(2,1)S(1)}, bf16[128,2560]{1,0:T(8,128)(2,1)S(1)}, u32[]{:S(2)}, u32[]{:S(2)}) collective-permute-start(bf16[128,2560]{1,0:T(8,128)(2,1)S(1)} %norm_forward.7.rest_4_), channel_id=1, source_target_pairs={{0,6},{1,7},{2,0},{3,1},{4,2},{5,3},{6,4},{7,5},{8,14},{9,15},{10,... | collective-permute-start | bytes 1966088 | tf_op jit(solution)/shard_map/ppermute | solution.py:34
  93.7 21.7 %collective-permute-start.19 = (bf16[32,2560]{1,0:T(8,128)(2,1)S(1)}, bf16[32,2560]{1,0:T(8,128)(2,1)S(1)}, u32[]{:S(2)}, u32[]{:S(2)}) collective-permute-start(bf16[32,2560]{1,0:T(8,128)(2,1)S(1)} %get-tuple-element.24), channel_id=1, source_target_pairs={{0,8},{1,9},{2,10},{3,11},{4,12},{5,13},{6,14},{7,15}} | collective-permute-start | bytes 491528 | tf_op jit(solution)/shard_map/ppermute | solution.py:40
  114.7 3.1 %collective-permute-start.20 = (bf16[32,2560]{1,0:T(8,128)(2,1)S(1)}, bf16[32,2560]{1,0:T(8,128)(2,1)S(1)}, u32[]{:S(2)}, u32[]{:S(2)}) collective-permute-start(bf16[32,2560]{1,0:T(8,128)(2,1)S(1)} %get-tuple-element.23), channel_id=1, source_target_pairs={{0,16},{1,17},{2,18},{3,19},{4,20},{5,21},{6,22},{7,23}} | collective-permute-start | bytes 491528 | tf_op jit(solution)/shard_map/ppermute | solution.py:40
  115.4 8.6 %collective-permute-start.21 = (bf16[32,2560]{1,0:T(8,128)(2,1)S(1)}, bf16[32,2560]{1,0:T(8,128)(2,1)S(1)}, u32[]{:S(2)}, u32[]{:S(2)}) collective-permute-start(bf16[32,2560]{1,0:T(8,128)(2,1)S(1)} %get-tuple-element.22), channel_id=1, source_target_pairs={{0,24},{1,25},{2,26},{3,27},{4,28},{5,29},{6,30},{7,31}} | collective-permute-start | bytes 491528 | tf_op jit(solution)/shard_map/ppermute | solution.py:40
  117.8 17.5 %collective-permute-start.15 = (bf16[48,8192]{1,0:T(8,128)(2,1)S(1)}, bf16[48,8192]{1,0:T(8,128)(2,1)S(1)}, u32[]{:S(2)}, u32[]{:S(2)}) collective-permute-start(bf16[48,8192]{1,0:T(8,128)(2,1)S(1)} %norm_backward.3.refs_12_), channel_id=1, source_target_pairs={{8,0},{16,8},{24,16},{9,1},{17,9},{25,17},{10,2},{18,10},{26,18},{... | collective-permute-start | bytes 2359304 | tf_op jit(solution)/shard_map/ppermute | solution.py:25
  128.4 8.3 %collective-permute-start.23 = (bf16[512,512]{1,0:T(8,128)(2,1)S(1)}, bf16[512,512]{1,0:T(8,128)(2,1)S(1)}, u32[]{:S(2)}, u32[]{:S(2)}) collective-permute-start(bf16[512,512]{1,0:T(8,128)(2,1)S(1)} %outer.8), channel_id=1, source_target_pairs={{0,1},{1,0},{2,3},{3,2},{4,5},{5,4},{6,7},{7,6},{8,9},{9,8},{10,11... | collective-permute-start | bytes 1572872 | tf_op jit(solution)/shard_map/ppermute | solution.py:51
  129.3 7.5 %collective-permute-start.22 = (bf16[512,512]{1,0:T(8,128)(2,1)S(1)}, bf16[512,512]{1,0:T(8,128)(2,1)S(1)}, u32[]{:S(2)}, u32[]{:S(2)}) collective-permute-start(bf16[512,512]{1,0:T(8,128)(2,1)S(1)} %outer.7), channel_id=1, source_target_pairs={{0,1},{1,0},{2,3},{3,2},{4,5},{5,4},{6,7},{7,6},{8,9},{9,8},{10,11... | collective-permute-start | bytes 1572872 | tf_op jit(solution)/shard_map/ppermute | solution.py:51
  136.8 1.6 %copy-start.3 = (bf16[128,8192]{1,0:T(8,128)(2,1)S(1)}, bf16[128,8192]{1,0:T(8,128)(2,1)}, u32[]{:S(2)}) copy-start(bf16[128,8192]{1,0:T(8,128)(2,1)} %stack_rows.3.refs_7_) | copy-start | bytes 6291460
where the time goes:
time: 143 us; the launch traced here: 141 us
  waiting for transfers between devices  72.8 us (51%)
  starting transfers between devices  32.2 us (23%)
  Pallas kernels  28.5 us (20%)
  local copies, waits for them, and re-layouts  6.44 us (5%)
    ppermute x12, waiting for transfers between devices, along_chips(): return lax.ppermute(array, ('pipe', 'dp'), pairs)  67.3 us
    ppermute x12, starting transfers between devices, along_chips(): return lax.ppermute(array, ('pipe', 'dp'), pairs)  17.2 us
    ppermute x2, starting transfers between devices, from_behind(): return lax.ppermute(array, axis, pairs)  8.05 us
    pallas_call x5, Pallas kernels, outer(): call(functools.partial(outer_kernel, [len(group) for group in groups], le...  7.8 us
    unnamed x24, local copies, waits for them, and re-layouts  5.63 us
    ppermute x2, waiting for transfers between devices, from_behind(): return lax.ppermute(array, axis, pairs)  5.49 us
    ppermute x6, starting transfers between devices, between_lines(): return lax.ppermute(array, ('pipe', 'dp'), pairs)  5.4 us
    pallas_call x1, Pallas kernels, project(): call(functools.partial(project_kernel, chips, steps, cuts), 'project', 4...  5.38 us
  transfers between devices with their start and end apart: 24, of which 7 were waited for; matrix products, arithmetic and copies ran while one was open for 1% of the time, Pallas kernels for 18%

commit v1 on v0

--- a/solution.py
+++ b/solution.py
@@ -25,25 +25,9 @@
     return lax.ppermute(array, axis, pairs)
 
 
-def along_chips(array, by, first=0):
+def along_chips(array, by):
     length = lax.axis_size("dp")
-    pairs = [
-        (line * length + i, line * length + ((i + by * CORES) % length if line >= first else i ^ 1))
-        for line in range(lax.axis_size("pipe")) for i in range(length)
-    ]
-    return lax.ppermute(array, ("pipe", "dp"), pairs)
-
-
-def between_lines(array, source, target):
-    length = lax.axis_size("dp")
-    pairs = [(source * length + i, target * length + i) for i in range(length)]
-    return lax.ppermute(array, ("pipe", "dp"), pairs)
-
-
-def on_line(array, by, line):
-    length = lax.axis_size("dp")
-    pairs = [(line * length + i, line * length + (i + by * CORES) % length) for i in range(length)]
-    return lax.ppermute(array, ("pipe", "dp"), pairs)
+    return lax.ppermute(array, "dp", [(i, (i + by * CORES) % length) for i in range(length)])
 
 
 def swap_cores(array):
@@ -328,44 +312,32 @@
     kv_weight,
 ):
     chips = lax.axis_size("dp") // CORES
-    sections = lax.axis_size("pipe")
     tokens, kv_width = new_keys.shape[1:]
     at = lax.axis_index("dp")
     place = jnp.stack([at // CORES, at % CORES]).astype(jnp.int32)
     middle = chips // 2
     near = [by for by in range(1, chips) if by != middle]
-    spread = tokens // 4
-
-    rows = [kv_grad[0]] + [along_chips(kv_grad[0], chips - by, 1) for by in range(1, chips)]
+
+    rows = [kv_grad[0]] + [along_chips(kv_grad[0], chips - by) for by in range(1, chips)]
     other_weight = swap_cores(kv_weight[0])
     value_cot = attend(queries[0], new_keys[0], context_grad[0], segment_ids)
 
     apply = functools.partial(normalize, place, new_input[0], new_gain, value_cot, chips)
-    shared = apply([middle], 0, spread, [other_weight])[0]
-    brought = [between_lines(shared, section, 0) for section in range(1, sections)]
     early = apply([0] + near[:1], 0, tokens, rows[1:])
     columns = [early[0]] + [along_chips(block, by) for block, by in zip(early[1:], near)]
-    joint = stack_rows([shared] + brought, early[:1])
-    moved = on_line(joint, middle, 0)
-    returned = [moved[:spread]] + [
-        between_lines(moved[section * spread:(section + 1) * spread], 0, section) for section in range(1, sections)
-    ]
 
     cuts = [0, tokens * 5 // 8, tokens]
-    parts = project(rows, kv_weight[0], other_weight, cuts, [joint])
-    arrived = [
-        [part[0]] + [along_chips(part[by], by, 1) for by in range(1, chips)] for part in parts
-    ]
+    parts = project(rows, kv_weight[0], other_weight, cuts, early[:1])
+    arrived = [[part[0]] + [along_chips(part[by], by) for by in range(1, chips)] for part in parts]
     backward = functools.partial(norm_backward, place, rows=frozen_input[0], gain=frozen_gain, grads=output_grad[0])
     above = backward(arrived[0], start=cuts[0], after=columns[1:])
-    kept = apply([middle], spread, tokens - spread, [above] + [arrived[1][by] for by in near])
-    late = apply(near[1:], 0, tokens, kept)
+    late = apply(near[1:] + [middle], 0, tokens, [above] + arrived[1][1:])
     above = [above, backward(arrived[1], start=cuts[1], after=late[:1])]
     below = [from_behind(half, "pipe", -1) for half in above]
     cot_below = stack_rows(below, [])
 
-    groups = [[column] for column in columns] + [returned]
-    last = [[along_chips(block, by)] for block, by in zip(late + kept, near[1:] + [middle])]
+    last = [[along_chips(block, by)] for block, by in zip(late, near[1:] + [middle])]
+    groups = [[column] for column in columns]
     sums = [outer(groups, kv_width, half, [], jnp.float32, after=above[1:]) for half in range(CORES)]
     given = [
         outer(last, kv_width, 1, sums[1:], jnp.bfloat16, part, 2, after=sums[:1]) for part in range(2)

time: 143 us -> 148 us (1.035)
  the two profiles are of different devices: /device:TPU:10 before, /device:TPU:0 now
where the time goes in v1:
time: 148 us
  waiting for transfers between devices  71 us (48%)
  starting transfers between devices  44.1 us (30%)
  Pallas kernels  25.5 us (17%)
  local copies, waits for them, and re-layouts  6.39 us (4%)
    ppermute x12, waiting for transfers between devices, along_chips(): lax.ppermute(array, 'dp', [(i, (i + by * CORES) % length) for i in range(...  70.9 us
    ppermute x12, starting transfers between devices, along_chips(): lax.ppermute(array, 'dp', [(i, (i + by * CORES) % length) for i in range(...  40.4 us
    pallas_call x5, Pallas kernels, outer(): call(functools.partial(outer_kernel, [len(group) for group in groups], le...  7 us
    unnamed x24, local copies, waits for them, and re-layouts  5.63 us
    pallas_call x1, Pallas kernels, project(): call(functools.partial(project_kernel, chips, steps, cuts), 'project', 4...  5.17 us
    pallas_call x1, Pallas kernels, attend(): call(attend_kernel, 'attend', 4 * tokens * tokens * queries.shape[1], 4 *...  4.47 us
    pallas_call x2, Pallas kernels, norm_backward(): call(functools.partial(backward_kernel, len(cots)), 'norm_backward', 10 *...  4.25 us
    pallas_call x2, Pallas kernels, normalize(): call(functools.partial(norm_kernel, chips, ahead), 'norm_forward', 4 * co...  3.11 us
  transfers between devices with their start and end apart: 17, of which 7 were waited for; matrix products, arithmetic and copies ran while one was open for 1% of the time, Pallas kernels for 15%

profile of v1, /device:TPU:0, one launch (start us, length us, event | category | flops | bytes accessed | tf_op | source)
XLA Modules:
  0.0 147.9 jit_solution(2060908479806297401)
XLA Ops:
  0.6 0.5 collective-permute-start
  1.2 4.7 %collective-permute-start.1 = (bf16[128,1024]{1,0:T(8,128)(2,1)}, bf16[128,1024]{1,0:T(8,128)(2,1)S(1)}, u32[]{:S(2)}, u32[]{:S(2)}) collective-permute-start(bf16[128,1024]{1,0:T(8,128)(2,1)} %bitcast.26), channel_id=1, source_target_pairs={{0,6},{1,7},{2,0},{3,1},{4,2},{5,3},{6,4},{7,5},{8,14},{9,15},{10,... | collective-permute-start | bytes 786440 | tf_op jit(solution)/shard_map/ppermute | solution.py:30
  5.8 1.0 collective-permute-start.3
  6.8 0.8 copy.13.col_seg_ref
  7.6 0.0 copy-start.4
  7.6 1.2 copy-done.4
  8.8 1.2 copy-done.5
  10.1 0.9 copy-done.8
  11.0 0.7 copy-done.9
  11.6 4.5 %attend.1.cot_ref = bf16[128,512]{1,0:T(8,128)(2,1)S(1)} custom-call(bf16[128,4096]{1,0:T(8,128)(2,1)S(1)} %bitcast.20, bf16[128,512]{1,0:T(8,128)(2,1)S(1)} %bitcast.22, bf16[128,4096]{1,0:T(8,128)(2,1)S(1)} %bitcast.21, s32[1,128]{1,0:T(1,128)S(1)} %copy-done.9, s32[128,1]{1,0:T(8,128)S(1)} %copy.13.col_seg_ref), custom_call_target="tpu_custom_call" | custom-call | flops 268435456 | bytes 2097152 | tf_op jit(solution)/shard_map/attend/pallas_call | solution.py:139
  16.1 0.0 copy-start.10
  16.1 0.0 copy-start.11
  16.1 0.1 pad_add_fusion.place_ref
  16.2 12.7 %collective-permute-done.2.rest_1_.rest_2_ = bf16[128,1024]{1,0:T(8,128)(2,1)S(1)} collective-permute-done((bf16[128,1024]{1,0:T(8,128)(2,1)}, bf16[128,1024]{1,0:T(8,128)(2,1)S(1)}, u32[]{:S(2)}, u32[]{:S(2)}) %collective-permute-start.2) | collective-permute-done | bytes 262176 | tf_op jit(solution)/shard_map/ppermute | solution.py:30
  29.0 1.6 %norm_forward.2 = (bf16[128,2560]{1,0:T(8,128)(2,1)S(1)}, bf16[128,2560]{1,0:T(8,128)(2,1)S(1)}) custom-call(s32[2]{0:T(128)S(1)} %pad_add_fusion.place_ref, bf16[128,8192]{1,0:T(8,128)(2,1)S(1)} %bitcast.14, bf16[1,8192]{1,0:T(2,128)(2,1)S(1)} %copy-done.6, bf16[128,512]{1,0:T(8,128)(2,1)S(1)} %attend.1.cot_ref, ...), custom_call_target="tpu_custom_call" | custom-call | flops 4194304 | bytes 3407872 | tf_op jit(solution)/shard_map/norm_forward/pallas_call | solution.py:76
  30.5 1.0 collective-permute-start.7
  31.6 0.0 copy-start.2
  31.6 0.0 copy-start.3
  31.6 0.0 copy-start.7
  31.6 5.2 %project.1 = (bf16[80,2048]{1,0:T(8,128)(2,1)S(1)}, bf16[80,2048]{1,0:T(8,128)(2,1)S(1)}, bf16[80,2048]{1,0:T(8,128)(2,1)S(1)}, bf16[80,2048]{1,0:T(8,128)(2,1)S...) custom-call(bf16[1024,1024]{1,0:T(8,128)(2,1)S(1)} %bitcast.25, ...), custom_call_target="tpu_custom_call" | custom-call | flops 2147483648 | bytes 7340032 | tf_op jit(solution)/shard_map/project/pallas_call | solution.py:190
  36.8 2.4 %collective-permute-start.4 = (bf16[80,2048]{1,0:T(8,128)(2,1)S(1)}, bf16[80,2048]{1,0:T(8,128)(2,1)S(1)}, u32[]{:S(2)}, u32[]{:S(2)}) collective-permute-start(bf16[80,2048]{1,0:T(8,128)(2,1)S(1)} %get-tuple-element.16), channel_id=1, source_target_pairs={{0,2},{1,3},{2,4},{3,5},{4,6},{5,7},{6,0},{7,1},{8,10},{9,11},{10,... | collective-permute-start | bytes 983048 | tf_op jit(solution)/shard_map/ppermute | solution.py:30
  39.2 1.1 collective-permute-start.5
  40.3 1.4 collective-permute-start.6
  41.6 1.0 collective-permute-start.10
  42.7 7.5 %collective-permute-done.7.rest_4_.refs_1_.refs_3_ = bf16[128,2560]{1,0:T(8,128)(2,1)S(1)} collective-permute-done((bf16[128,2560]{1,0:T(8,128)(2,1)S(1)}, bf16[128,2560]{1,0:T(8,128)(2,1)S(1)}, u32[]{:S(2)}, u32[]{:S(2)}) %collective-permute-start.7) | collective-permute-done | bytes 655392 | tf_op jit(solution)/shard_map/ppermute | solution.py:30
  50.2 0.2 collective-permute-start.11
  50.5 6.7 %collective-permute-done.4.rest_1_ = bf16[80,2048]{1,0:T(8,128)(2,1)S(1)} collective-permute-done((bf16[80,2048]{1,0:T(8,128)(2,1)S(1)}, bf16[80,2048]{1,0:T(8,128)(2,1)S(1)}, u32[]{:S(2)}, u32[]{:S(2)}) %collective-permute-start.4) | collective-permute-done | bytes 327712 | tf_op jit(solution)/shard_map/ppermute | solution.py:30
  57.2 21.4 %collective-permute-start.9 = (bf16[48,2048]{1,0:T(8,128)(2,1)S(1)}, bf16[48,2048]{1,0:T(8,128)(2,1)S(1)}, u32[]{:S(2)}, u32[]{:S(2)}) collective-permute-start(bf16[48,2048]{1,0:T(8,128)(2,1)S(1)} %get-tuple-element.21), channel_id=1, source_target_pairs={{0,2},{1,3},{2,4},{3,5},{4,6},{5,7},{6,0},{7,1},{8,10},{9,11},{10,... | collective-permute-start | bytes 589832 | tf_op jit(solution)/shard_map/ppermute | solution.py:30
  78.6 2.5 %norm_backward.2.rest_0_ = bf16[80,8192]{1,0:T(8,128)(2,1)S(1)} custom-call(s32[2]{0:T(128)S(1)} %pad_add_fusion.place_ref, bf16[128,8192]{1,0:T(8,128)(2,1)S(1)} %bitcast.16, bf16[1,8192]{1,0:T(2,128)(2,1)S(1)} %copy-done.7, bf16[128,8192]{1,0:T(8,128)(2,1)S(1)} %bitcast.18, bf16[80,2048]{1,0:T(8,128)(2,1)S(1)} %get-tuple-element.15.rest_0_, ...), custom_call_target="tpu_custom_call" | custom-call | flops 6553600 | bytes 5242880 | tf_op jit(solution)/shard_map/norm_backward/pallas_call | solution.py:237
  81.2 1.3 collective-permute-start.8
  82.5 7.1 %collective-permute-done.10.rest_2_ = bf16[48,2048]{1,0:T(8,128)(2,1)S(1)} collective-permute-done((bf16[48,2048]{1,0:T(8,128)(2,1)S(1)}, bf16[48,2048]{1,0:T(8,128)(2,1)S(1)}, u32[]{:S(2)}, u32[]{:S(2)}) %collective-permute-start.10) | collective-permute-done | bytes 196640 | tf_op jit(solution)/shard_map/ppermute | solution.py:30
  89.6 1.5 %norm_forward.3 = (bf16[128,2560]{1,0:T(8,128)(2,1)S(1)}, bf16[128,2560]{1,0:T(8,128)(2,1)S(1)}) custom-call(s32[2]{0:T(128)S(1)} %pad_add_fusion.place_ref, bf16[128,8192]{1,0:T(8,128)(2,1)S(1)} %bitcast.15, bf16[1,8192]{1,0:T(2,128)(2,1)S(1)} %copy-done.6, bf16[128,512]{1,0:T(8,128)(2,1)S(1)} %attend.1.cot_ref, bf16[80,8192]{1,0:T(8,128)(2,1)S(1)} %norm_backward.2.rest_0_, ...), custom_call_target="tpu_custom_call" | custom-call | flops 4194304 | bytes 3407872 | tf_op jit(solution)/shard_map/norm_forward/pallas_call | solution.py:76
  91.1 3.5 %collective-permute-start.13 = (bf16[128,2560]{1,0:T(8,128)(2,1)S(1)}, bf16[128,2560]{1,0:T(8,128)(2,1)S(1)}, u32[]{:S(2)}, u32[]{:S(2)}) collective-permute-start(bf16[128,2560]{1,0:T(8,128)(2,1)S(1)} %get-tuple-element.24.rest_4_), channel_id=1, source_target_pairs={{0,6},{1,7},{2,0},{3,1},{4,2},{5,3},{6,4},{7,5},{8,14},{9,15},{10,... | collective-permute-start | bytes 1966088 | tf_op jit(solution)/shard_map/ppermute | solution.py:30
  94.7 2.7 %collective-permute-start.14 = (bf16[128,2560]{1,0:T(8,128)(2,1)S(1)}, bf16[128,2560]{1,0:T(8,128)(2,1)S(1)}, u32[]{:S(2)}, u32[]{:S(2)}) collective-permute-start(bf16[128,2560]{1,0:T(8,128)(2,1)S(1)} %get-tuple-element.25), channel_id=1, source_target_pairs={{0,4},{1,5},{2,6},{3,7},{4,0},{5,1},{6,2},{7,3},{8,12},{9,13},{10,... | collective-permute-start | bytes 1966088 | tf_op jit(solution)/shard_map/ppermute | solution.py:30
  97.3 1.7 %norm_backward.3.refs_4_ = bf16[48,8192]{1,0:T(8,128)(2,1)S(1)} custom-call(s32[2]{0:T(128)S(1)} %pad_add_fusion.place_ref, bf16[128,8192]{1,0:T(8,128)(2,1)S(1)} %bitcast.17, bf16[1,8192]{1,0:T(2,128)(2,1)S(1)} %copy-done.7, bf16[128,8192]{1,0:T(8,128)(2,1)S(1)} %bitcast.19, bf16[48,2048]{1,0:T(8,128)(2,1)S(1)} %get-tuple-element.20.rest_0_, ...), custom_call_target="tpu_custom_call" | custom-call | flops 3932160 | bytes 3145728 | tf_op jit(solution)/shard_map/norm_backward/pallas_call | solution.py:237
  99.1 1.3 collective-permute-start.12
  100.4 1.4 outer.6.refs_4_
  101.8 1.4 outer.5.refs_5_.refs_4_
  103.3 7.5 %collective-permute-done.13.refs_0_.refs_2_ = bf16[128,2560]{1,0:T(8,128)(2,1)S(1)} collective-permute-done((bf16[128,2560]{1,0:T(8,128)(2,1)S(1)}, bf16[128,2560]{1,0:T(8,128)(2,1)S(1)}, u32[]{:S(2)}, u32[]{:S(2)}) %collective-permute-start.13) | collective-permute-done | bytes 655392 | tf_op jit(solution)/shard_map/ppermute | solution.py:30
  110.8 29.3 %collective-permute-done.14.refs_1_.refs_3_ = bf16[128,2560]{1,0:T(8,128)(2,1)S(1)} collective-permute-done((bf16[128,2560]{1,0:T(8,128)(2,1)S(1)}, bf16[128,2560]{1,0:T(8,128)(2,1)S(1)}, u32[]{:S(2)}, u32[]{:S(2)}) %collective-permute-start.14) | collective-permute-done | bytes 655392 | tf_op jit(solution)/shard_map/ppermute | solution.py:30
  140.1 0.7 outer.8
  140.8 0.1 collective-permute-start.16
  140.9 0.8 outer.7
  141.6 0.5 collective-permute-start.15
  142.2 1.5 stack_rows.1.refs_7_
  143.6 0.1 collective-permute-done.15.refs_5_
  143.7 1.6 %copy-done = bf16[128,8192]{1,0:T(8,128)(2,1)S(1)} copy-done((bf16[128,8192]{1,0:T(8,128)(2,1)S(1)}, bf16[128,8192]{1,0:T(8,128)(2,1)}, u32[]{:S(2)}) %copy-start) | copy-done | bytes 2097176
  145.3 2.6 %outer.9 = f32[1024,512]{1,0:T(8,128)} custom-call(bf16[128,2560]{1,0:T(8,128)(2,1)S(1)} %collective-permute-done.13.refs_0_.refs_2_, bf16[128,2560]{1,0:T(8,128)(2,1)S(1)} %collective-permute-done.14.refs_1_.refs_3_, bf16[128,2560]{1,0:T(8,128)(2,1)S(1)} %collective-permute-done.13.refs_0_.refs_2_, ...), custom_call_target="tpu_custom_call" | custom-call | flops 268435456 | bytes 2621440 | tf_op jit(solution)/shard_map/outer/pallas_call | solution.py:284
  (24 shorter events, 0.1 us)
Async XLA Ops:
  0.6 28.3 %copy-start.1 = (bf16[1,128,8192]{2,1,0:T(8,128)(2,1)S(1)}, bf16[1,128,8192]{2,1,0:T(8,128)(2,1)}, u32[]{:S(2)}) copy-start(bf16[1,128,8192]{2,1,0:T(8,128)(2,1)} %param.11) | copy-start | bytes 6291460
  0.6 30.9 %collective-permute-start = (bf16[1024,1024]{1,0:T(8,128)(2,1)}, bf16[1024,1024]{1,0:T(8,128)(2,1)}, u32[]{:S(2)}, u32[]{:S(2)}) collective-permute-start(bf16[1024,1024]{1,0:T(8,128)(2,1)} %bitcast.24), channel_id=1, source_target_pairs={{0,1},{1,0},{2,3},{3,2},{4,5},{5,4},{6,7},{7,6},{8,9},{9,8},{10,11... | collective-permute-start | bytes 6291464 | tf_op jit(solution)/shard_map/ppermute | solution.py:35
  1.2 15.1 %collective-permute-start.1 = (bf16[128,1024]{1,0:T(8,128)(2,1)}, bf16[128,1024]{1,0:T(8,128)(2,1)S(1)}, u32[]{:S(2)}, u32[]{:S(2)}) collective-permute-start(bf16[128,1024]{1,0:T(8,128)(2,1)} %bitcast.26), channel_id=1, source_target_pairs={{0,6},{1,7},{2,0},{3,1},{4,2},{5,3},{6,4},{7,5},{8,14},{9,15},{10,... | collective-permute-start | bytes 786440 | tf_op jit(solution)/shard_map/ppermute | solution.py:30
  5.8 23.1 %collective-permute-start.2 = (bf16[128,1024]{1,0:T(8,128)(2,1)}, bf16[128,1024]{1,0:T(8,128)(2,1)S(1)}, u32[]{:S(2)}, u32[]{:S(2)}) collective-permute-start(bf16[128,1024]{1,0:T(8,128)(2,1)} %bitcast.27), channel_id=1, source_target_pairs={{0,4},{1,5},{2,6},{3,7},{4,0},{5,1},{6,2},{7,3},{8,12},{9,13},{10,... | collective-permute-start | bytes 786440 | tf_op jit(solution)/shard_map/ppermute | solution.py:30
  5.8 23.1 %collective-permute-start.3 = (bf16[128,1024]{1,0:T(8,128)(2,1)}, bf16[128,1024]{1,0:T(8,128)(2,1)S(1)}, u32[]{:S(2)}, u32[]{:S(2)}) collective-permute-start(bf16[128,1024]{1,0:T(8,128)(2,1)} %bitcast.28), channel_id=1, source_target_pairs={{0,2},{1,3},{2,4},{3,5},{4,6},{5,7},{6,0},{7,1},{8,10},{9,11},{10,... | collective-permute-start | bytes 786440 | tf_op jit(solution)/shard_map/ppermute | solution.py:30
  7.6 1.2 copy-start.4
  8.8 1.2 copy-start.5
  10.1 0.9 copy-start.8
  11.0 0.7 copy-start.9
  11.6 17.3 %copy-start.6 = (bf16[1,8192]{1,0:T(2,128)(2,1)S(1)}, bf16[1,8192]{1,0:T(2,128)(2,1)}, u32[]{:S(2)}) copy-start(bf16[1,8192]{1,0:T(2,128)(2,1)} %gain_ref.6) | copy-start | bytes 49156
  16.1 15.5 %copy-start.10 = (bf16[1,1024,1024]{2,1,0:T(8,128)(2,1)S(1)}, bf16[1,1024,1024]{2,1,0:T(8,128)(2,1)}, u32[]{:S(2)}) copy-start(bf16[1,1024,1024]{2,1,0:T(8,128)(2,1)} %param.21) | copy-start | bytes 6291460
  16.1 15.4 %copy-start.11 = (bf16[1,128,1024]{2,1,0:T(8,128)(2,1)S(1)}, bf16[1,128,1024]{2,1,0:T(8,128)(2,1)}, u32[]{:S(2)}) copy-start(bf16[1,128,1024]{2,1,0:T(8,128)(2,1)} %param.20) | copy-start | bytes 786436
  30.5 19.7 %collective-permute-start.7 = (bf16[128,2560]{1,0:T(8,128)(2,1)S(1)}, bf16[128,2560]{1,0:T(8,128)(2,1)S(1)}, u32[]{:S(2)}, u32[]{:S(2)}) collective-permute-start(bf16[128,2560]{1,0:T(8,128)(2,1)S(1)} %get-tuple-element.19), channel_id=1, source_target_pairs={{0,2},{1,3},{2,4},{3,5},{4,6},{5,7},{6,0},{7,1},{8,10},{9,11},{10,... | collective-permute-start | bytes 1966088 | tf_op jit(solution)/shard_map/ppermute | solution.py:30
  31.6 47.1 %copy-start.2 = (bf16[1,128,8192]{2,1,0:T(8,128)(2,1)S(1)}, bf16[1,128,8192]{2,1,0:T(8,128)(2,1)}, u32[]{:S(2)}) copy-start(bf16[1,128,8192]{2,1,0:T(8,128)(2,1)} %param.17) | copy-start | bytes 6291460
  31.6 47.0 %copy-start.3 = (bf16[1,128,8192]{2,1,0:T(8,128)(2,1)S(1)}, bf16[1,128,8192]{2,1,0:T(8,128)(2,1)}, u32[]{:S(2)}) copy-start(bf16[1,128,8192]{2,1,0:T(8,128)(2,1)} %param.19) | copy-start | bytes 6291460
  31.6 47.0 %copy-start.7 = (bf16[1,8192]{1,0:T(2,128)(2,1)S(1)}, bf16[1,8192]{1,0:T(2,128)(2,1)}, u32[]{:S(2)}) copy-start(bf16[1,8192]{1,0:T(2,128)(2,1)} %gain_ref.7) | copy-start | bytes 49156
  36.8 20.4 %collective-permute-start.4 = (bf16[80,2048]{1,0:T(8,128)(2,1)S(1)}, bf16[80,2048]{1,0:T(8,128)(2,1)S(1)}, u32[]{:S(2)}, u32[]{:S(2)}) collective-permute-start(bf16[80,2048]{1,0:T(8,128)(2,1)S(1)} %get-tuple-element.16), channel_id=1, source_target_pairs={{0,2},{1,3},{2,4},{3,5},{4,6},{5,7},{6,0},{7,1},{8,10},{9,11},{10,... | collective-permute-start | bytes 983048 | tf_op jit(solution)/shard_map/ppermute | solution.py:30
  39.2 39.4 %collective-permute-start.5 = (bf16[80,2048]{1,0:T(8,128)(2,1)S(1)}, bf16[80,2048]{1,0:T(8,128)(2,1)S(1)}, u32[]{:S(2)}, u32[]{:S(2)}) collective-permute-start(bf16[80,2048]{1,0:T(8,128)(2,1)S(1)} %get-tuple-element.17), channel_id=1, source_target_pairs={{0,4},{1,5},{2,6},{3,7},{4,0},{5,1},{6,2},{7,3},{8,12},{9,13},{10,... | collective-permute-start | bytes 983048 | tf_op jit(solution)/shard_map/ppermute | solution.py:30
  40.3 38.4 %collective-permute-start.6 = (bf16[80,2048]{1,0:T(8,128)(2,1)S(1)}, bf16[80,2048]{1,0:T(8,128)(2,1)S(1)}, u32[]{:S(2)}, u32[]{:S(2)}) collective-permute-start(bf16[80,2048]{1,0:T(8,128)(2,1)S(1)} %get-tuple-element.18), channel_id=1, source_target_pairs={{0,6},{1,7},{2,0},{3,1},{4,2},{5,3},{6,4},{7,5},{8,14},{9,15},{10,... | collective-permute-start | bytes 983048 | tf_op jit(solution)/shard_map/ppermute | solution.py:30
  41.6 47.9 %collective-permute-start.10 = (bf16[48,2048]{1,0:T(8,128)(2,1)S(1)}, bf16[48,2048]{1,0:T(8,128)(2,1)S(1)}, u32[]{:S(2)}, u32[]{:S(2)}) collective-permute-start(bf16[48,2048]{1,0:T(8,128)(2,1)S(1)} %get-tuple-element.22), channel_id=1, source_target_pairs={{0,4},{1,5},{2,6},{3,7},{4,0},{5,1},{6,2},{7,3},{8,12},{9,13},{10,... | collective-permute-start | bytes 589832 | tf_op jit(solution)/shard_map/ppermute | solution.py:30
  50.2 39.4 %collective-permute-start.11 = (bf16[48,2048]{1,0:T(8,128)(2,1)S(1)}, bf16[48,2048]{1,0:T(8,128)(2,1)S(1)}, u32[]{:S(2)}, u32[]{:S(2)}) collective-permute-start(bf16[48,2048]{1,0:T(8,128)(2,1)S(1)} %get-tuple-element.23), channel_id=1, source_target_pairs={{0,6},{1,7},{2,0},{3,1},{4,2},{5,3},{6,4},{7,5},{8,14},{9,15},{10,... | collective-permute-start | bytes 589832 | tf_op jit(solution)/shard_map/ppermute | solution.py:30
  57.2 32.4 %collective-permute-start.9 = (bf16[48,2048]{1,0:T(8,128)(2,1)S(1)}, bf16[48,2048]{1,0:T(8,128)(2,1)S(1)}, u32[]{:S(2)}, u32[]{:S(2)}) collective-permute-start(bf16[48,2048]{1,0:T(8,128)(2,1)S(1)} %get-tuple-element.21), channel_id=1, source_target_pairs={{0,2},{1,3},{2,4},{3,5},{4,6},{5,7},{6,0},{7,1},{8,10},{9,11},{10,... | collective-permute-start | bytes 589832 | tf_op jit(solution)/shard_map/ppermute | solution.py:30
  81.2 61.0 %collective-permute-start.8 = (bf16[80,8192]{1,0:T(8,128)(2,1)S(1)}, bf16[80,8192]{1,0:T(8,128)(2,1)S(1)}, u32[]{:S(2)}, u32[]{:S(2)}) collective-permute-start(bf16[80,8192]{1,0:T(8,128)(2,1)S(1)} %norm_backward.2.rest_0_), channel_id=1, source_target_pairs={{8,0},{16,8},{24,16},{9,1},{17,9},{25,17},{10,2},{18,10},{26,18},{... | collective-permute-start | bytes 3932168 | tf_op jit(solution)/shard_map/ppermute | solution.py:25
  91.1 19.6 %collective-permute-start.13 = (bf16[128,2560]{1,0:T(8,128)(2,1)S(1)}, bf16[128,2560]{1,0:T(8,128)(2,1)S(1)}, u32[]{:S(2)}, u32[]{:S(2)}) collective-permute-start(bf16[128,2560]{1,0:T(8,128)(2,1)S(1)} %get-tuple-element.24.rest_4_), channel_id=1, source_target_pairs={{0,6},{1,7},{2,0},{3,1},{4,2},{5,3},{6,4},{7,5},{8,14},{9,15},{10,... | collective-permute-start | bytes 1966088 | tf_op jit(solution)/shard_map/ppermute | solution.py:30
  94.7 45.4 %collective-permute-start.14 = (bf16[128,2560]{1,0:T(8,128)(2,1)S(1)}, bf16[128,2560]{1,0:T(8,128)(2,1)S(1)}, u32[]{:S(2)}, u32[]{:S(2)}) collective-permute-start(bf16[128,2560]{1,0:T(8,128)(2,1)S(1)} %get-tuple-element.25), channel_id=1, source_target_pairs={{0,4},{1,5},{2,6},{3,7},{4,0},{5,1},{6,2},{7,3},{8,12},{9,13},{10,... | collective-permute-start | bytes 1966088 | tf_op jit(solution)/shard_map/ppermute | solution.py:30
  99.1 43.1 %collective-permute-start.12 = (bf16[48,8192]{1,0:T(8,128)(2,1)S(1)}, bf16[48,8192]{1,0:T(8,128)(2,1)S(1)}, u32[]{:S(2)}, u32[]{:S(2)}) collective-permute-start(bf16[48,8192]{1,0:T(8,128)(2,1)S(1)} %norm_backward.3.refs_4_), channel_id=1, source_target_pairs={{8,0},{16,8},{24,16},{9,1},{17,9},{25,17},{10,2},{18,10},{26,18},{... | collective-permute-start | bytes 2359304 | tf_op jit(solution)/shard_map/ppermute | solution.py:25
  140.8 2.8 %collective-permute-start.16 = (bf16[512,512]{1,0:T(8,128)(2,1)S(1)}, bf16[512,512]{1,0:T(8,128)(2,1)S(1)}, u32[]{:S(2)}, u32[]{:S(2)}) collective-permute-start(bf16[512,512]{1,0:T(8,128)(2,1)S(1)} %outer.8), channel_id=1, source_target_pairs={{0,1},{1,0},{2,3},{3,2},{4,5},{5,4},{6,7},{7,6},{8,9},{9,8},{10,11... | collective-permute-start | bytes 1572872 | tf_op jit(solution)/shard_map/ppermute | solution.py:35
  141.6 2.1 %collective-permute-start.15 = (bf16[512,512]{1,0:T(8,128)(2,1)S(1)}, bf16[512,512]{1,0:T(8,128)(2,1)S(1)}, u32[]{:S(2)}, u32[]{:S(2)}) collective-permute-start(bf16[512,512]{1,0:T(8,128)(2,1)S(1)} %outer.7), channel_id=1, source_target_pairs={{0,1},{1,0},{2,3},{3,2},{4,5},{5,4},{6,7},{7,6},{8,9},{9,8},{10,11... | collective-permute-start | bytes 1572872 | tf_op jit(solution)/shard_map/ppermute | solution.py:35
  143.7 1.6 %copy-start = (bf16[128,8192]{1,0:T(8,128)(2,1)S(1)}, bf16[128,8192]{1,0:T(8,128)(2,1)}, u32[]{:S(2)}) copy-start(bf16[128,8192]{1,0:T(8,128)(2,1)} %stack_rows.1.refs_7_) | copy-start | bytes 6291460

commit v2 on v0

--- a/solution.py
+++ b/solution.py
@@ -371,7 +371,7 @@
         outer(last, kv_width, 1, sums[1:], jnp.bfloat16, part, 2, after=sums[:1]) for part in range(2)
     ]
     taken = [swap_cores(part) for part in given]
-    grad = outer(last, kv_width, 0, sums[:1], jnp.float32, halves=taken, after=[cot_below])
+    grad = outer(last, kv_width, 0, sums[:1], jnp.float32, halves=taken)
     return (cot_below[None], grad[None])
 
 

time: 143 us -> 139 us (0.972)
  waiting for transfers between devices: 72.8 us -> 70.2 us
  local copies, waits for them, and re-layouts: 6.44 us -> 4.85 us
    ppermute x2, waiting for transfers between devices: 5.49 us -> 1.32 us  [from_behind(): return lax.ppermute(array, axis, pairs)]
    unnamed x24 -> x22, local copies, waits for them, and re-layouts: 5.63 us -> 4.04 us
    ppermute x3, waiting for transfers between devices: 0.01 us -> 1.54 us  [swap_cores(): return lax.ppermute(array, 'dp', [(i, i ^ 1) for i in range(length)])]
  transfers between devices with their start and end apart: 24 -> 24, of which waited for: 7 -> 9; matrix products, arithmetic and copies ran while one was open for 1% -> 1% of each run, Pallas kernels for 18% -> 20%
where the time goes in v2:
time: 139 us; the launch traced here: 137 us
  waiting for transfers between devices  70.2 us (51%)
  starting transfers between devices  32.2 us (23%)
  Pallas kernels  28.5 us (21%)
  local copies, waits for them, and re-layouts  4.85 us (3%)
    ppermute x12, waiting for transfers between devices, along_chips(): return lax.ppermute(array, ('pipe', 'dp'), pairs)  67.3 us
    ppermute x12, starting transfers between devices, along_chips(): return lax.ppermute(array, ('pipe', 'dp'), pairs)  17.2 us
    ppermute x2, starting transfers between devices, from_behind(): return lax.ppermute(array, axis, pairs)  8.05 us
    pallas_call x5, Pallas kernels, outer(): call(functools.partial(outer_kernel, [len(group) for group in groups], le...  7.79 us
    ppermute x6, starting transfers between devices, between_lines(): return lax.ppermute(array, ('pipe', 'dp'), pairs)  5.4 us
    pallas_call x1, Pallas kernels, project(): call(functools.partial(project_kernel, chips, steps, cuts), 'project', 4...  5.38 us
    pallas_call x4, Pallas kernels, normalize(): call(functools.partial(norm_kernel, chips, ahead), 'norm_forward', 4 * co...  5.06 us
    pallas_call x1, Pallas kernels, attend(): call(attend_kernel, 'attend', 4 * tokens * tokens * queries.shape[1], 4 *...  4.48 us
  transfers between devices with their start and end apart: 24, of which 9 were waited for; matrix products, arithmetic and copies ran while one was open for 1% of the time, Pallas kernels for 20%

profile of v2, /device:TPU:10, one launch (start us, length us, event | category | flops | bytes accessed | tf_op | source)
XLA Modules:
  0.0 136.8 jit_solution(17047853530613434623)
XLA Ops:
  0.7 0.5 collective-permute-start.1
  1.2 2.6 %collective-permute-start.2 = (bf16[128,1024]{1,0:T(8,128)(2,1)}, bf16[128,1024]{1,0:T(8,128)(2,1)S(1)}, u32[]{:S(2)}, u32[]{:S(2)}) collective-permute-start(bf16[128,1024]{1,0:T(8,128)(2,1)} %bitcast.28), channel_id=1, source_target_pairs={{0,1},{1,0},{2,3},{3,2},{4,5},{5,4},{6,7},{7,6},{8,12},{9,13},{10,... | collective-permute-start | bytes 786440 | tf_op jit(solution)/shard_map/ppermute | solution.py:34
  3.8 2.5 %collective-permute-start.3 = (bf16[128,1024]{1,0:T(8,128)(2,1)}, bf16[128,1024]{1,0:T(8,128)(2,1)S(1)}, u32[]{:S(2)}, u32[]{:S(2)}) collective-permute-start(bf16[128,1024]{1,0:T(8,128)(2,1)} %bitcast.29), channel_id=1, source_target_pairs={{0,1},{1,0},{2,3},{3,2},{4,5},{5,4},{6,7},{7,6},{8,10},{9,11},{10,... | collective-permute-start | bytes 786440 | tf_op jit(solution)/shard_map/ppermute | solution.py:34
  6.3 0.8 copy.13.col_seg_ref
  7.1 1.2 copy-done.3
  8.3 1.2 copy-done.4
  9.5 0.9 copy-done.7
  10.4 0.7 copy-done.8
  11.1 4.5 %attend.1.cot_ref = bf16[128,512]{1,0:T(8,128)(2,1)S(1)} custom-call(bf16[128,4096]{1,0:T(8,128)(2,1)S(1)} %bitcast.21, bf16[128,512]{1,0:T(8,128)(2,1)S(1)} %bitcast.23, bf16[128,4096]{1,0:T(8,128)(2,1)S(1)} %bitcast.22, s32[1,128]{1,0:T(1,128)S(1)} %copy-done.8, s32[128,1]{1,0:T(8,128)S(1)} %copy.13.col_seg_ref), custom_call_target="tpu_custom_call" | custom-call | flops 268435456 | bytes 2097152 | tf_op jit(solution)/shard_map/attend/pallas_call | solution.py:155
  15.6 0.8 norm_forward.4.refs_0_
  16.4 1.4 %collective-permute-start.4 = (bf16[32,2560]{1,0:T(8,128)(2,1)S(1)}, bf16[32,2560]{1,0:T(8,128)(2,1)S(1)}, u32[]{:S(2)}, u32[]{:S(2)}) collective-permute-start(bf16[32,2560]{1,0:T(8,128)(2,1)S(1)} %norm_forward.4.refs_0_), channel_id=1, source_target_pairs={{8,0},{9,1},{10,2},{11,3},{12,4},{13,5},{14,6},{15,7}} | collective-permute-start | bytes 491528 | tf_op jit(solution)/shard_map/ppermute | solution.py:40
  17.9 0.7 collective-permute-start.5
  18.6 0.7 collective-permute-start.6
  19.2 2.8 %collective-permute-done.2.rest_1_.rest_2_ = bf16[128,1024]{1,0:T(8,128)(2,1)S(1)} collective-permute-done((bf16[128,1024]{1,0:T(8,128)(2,1)}, bf16[128,1024]{1,0:T(8,128)(2,1)S(1)}, u32[]{:S(2)}, u32[]{:S(2)}) %collective-permute-start.2) | collective-permute-done | bytes 262176 | tf_op jit(solution)/shard_map/ppermute | solution.py:34
  22.1 4.8 %collective-permute-done.3.rest_2_.rest_3_ = bf16[128,1024]{1,0:T(8,128)(2,1)S(1)} collective-permute-done((bf16[128,1024]{1,0:T(8,128)(2,1)}, bf16[128,1024]{1,0:T(8,128)(2,1)S(1)}, u32[]{:S(2)}, u32[]{:S(2)}) %collective-permute-start.3) | collective-permute-done | bytes 262176 | tf_op jit(solution)/shard_map/ppermute | solution.py:34
  26.9 1.5 %norm_forward.5 = (bf16[128,2560]{1,0:T(8,128)(2,1)S(1)}, bf16[128,2560]{1,0:T(8,128)(2,1)S(1)}) custom-call(s32[2]{0:T(128)S(1)} %pad_add_fusion.place_ref, bf16[128,8192]{1,0:T(8,128)(2,1)S(1)} %bitcast.14, bf16[1,8192]{1,0:T(2,128)(2,1)S(1)} %copy-done.5, bf16[128,512]{1,0:T(8,128)(2,1)S(1)} %attend.1.cot_ref, ...), custom_call_target="tpu_custom_call" | custom-call | flops 4194304 | bytes 3407872 | tf_op jit(solution)/shard_map/norm_forward/pallas_call | solution.py:92
  28.5 2.4 %collective-permute-start.10 = (bf16[128,2560]{1,0:T(8,128)(2,1)S(1)}, bf16[128,2560]{1,0:T(8,128)(2,1)S(1)}, u32[]{:S(2)}, u32[]{:S(2)}) collective-permute-start(bf16[128,2560]{1,0:T(8,128)(2,1)S(1)} %get-tuple-element.17), channel_id=1, source_target_pairs={{0,2},{1,3},{2,4},{3,5},{4,6},{5,7},{6,0},{7,1},{8,10},{9,11},{10,... | collective-permute-start | bytes 1966088 | tf_op jit(solution)/shard_map/ppermute | solution.py:34
  31.0 0.8 collective-permute-start.18
  31.9 5.4 %project.1 = (bf16[80,2048]{1,0:T(8,128)(2,1)S(1)}, bf16[80,2048]{1,0:T(8,128)(2,1)S(1)}, bf16[80,2048]{1,0:T(8,128)(2,1)S(1)}, bf16[80,2048]{1,0:T(8,128)(2,1)S...) custom-call(bf16[1024,1024]{1,0:T(8,128)(2,1)S(1)} %bitcast.26, ...), custom_call_target="tpu_custom_call" | custom-call | flops 2147483648 | bytes 7340032 | tf_op jit(solution)/shard_map/project/pallas_call | solution.py:206
  37.2 0.1 collective-permute-start.7
  37.3 2.0 %collective-permute-start.8 = (bf16[80,2048]{1,0:T(8,128)(2,1)S(1)}, bf16[80,2048]{1,0:T(8,128)(2,1)S(1)}, u32[]{:S(2)}, u32[]{:S(2)}) collective-permute-start(bf16[80,2048]{1,0:T(8,128)(2,1)S(1)} %get-tuple-element.15), channel_id=1, source_target_pairs={{0,1},{1,0},{2,3},{3,2},{4,5},{5,4},{6,7},{7,6},{8,12},{9,13},{10,... | collective-permute-start | bytes 983048 | tf_op jit(solution)/shard_map/ppermute | solution.py:34
  39.3 1.0 collective-permute-start.9
  40.4 5.8 %collective-permute-done.10.rest_4_.refs_1_.refs_7_ = bf16[128,2560]{1,0:T(8,128)(2,1)S(1)} collective-permute-done((bf16[128,2560]{1,0:T(8,128)(2,1)S(1)}, bf16[128,2560]{1,0:T(8,128)(2,1)S(1)}, u32[]{:S(2)}, u32[]{:S(2)}) %collective-permute-start.10) | collective-permute-done | bytes 655392 | tf_op jit(solution)/shard_map/ppermute | solution.py:34
  46.2 2.4 %collective-permute-start.12 = (bf16[48,2048]{1,0:T(8,128)(2,1)S(1)}, bf16[48,2048]{1,0:T(8,128)(2,1)S(1)}, u32[]{:S(2)}, u32[]{:S(2)}) collective-permute-start(bf16[48,2048]{1,0:T(8,128)(2,1)S(1)} %get-tuple-element.19), channel_id=1, source_target_pairs={{0,1},{1,0},{2,3},{3,2},{4,5},{5,4},{6,7},{7,6},{8,10},{9,11},{10,... | collective-permute-start | bytes 589832 | tf_op jit(solution)/shard_map/ppermute | solution.py:34
  48.6 18.6 %collective-permute-done.7.rest_1_ = bf16[80,2048]{1,0:T(8,128)(2,1)S(1)} collective-permute-done((bf16[80,2048]{1,0:T(8,128)(2,1)S(1)}, bf16[80,2048]{1,0:T(8,128)(2,1)S(1)}, u32[]{:S(2)}, u32[]{:S(2)}) %collective-permute-start.7) | collective-permute-done | bytes 327712 | tf_op jit(solution)/shard_map/ppermute | solution.py:34
  67.2 15.4 %collective-permute-done.8.rest_2_ = bf16[80,2048]{1,0:T(8,128)(2,1)S(1)} collective-permute-done((bf16[80,2048]{1,0:T(8,128)(2,1)S(1)}, bf16[80,2048]{1,0:T(8,128)(2,1)S(1)}, u32[]{:S(2)}, u32[]{:S(2)}) %collective-permute-start.8) | collective-permute-done | bytes 327712 | tf_op jit(solution)/shard_map/ppermute | solution.py:34
  82.6 3.4 %collective-permute-start.13 = (bf16[48,2048]{1,0:T(8,128)(2,1)S(1)}, bf16[48,2048]{1,0:T(8,128)(2,1)S(1)}, u32[]{:S(2)}, u32[]{:S(2)}) collective-permute-start(bf16[48,2048]{1,0:T(8,128)(2,1)S(1)} %get-tuple-element.20), channel_id=1, source_target_pairs={{0,1},{1,0},{2,3},{3,2},{4,5},{5,4},{6,7},{7,6},{8,12},{9,13},{10,... | collective-permute-start | bytes 589832 | tf_op jit(solution)/shard_map/ppermute | solution.py:34
  86.0 2.5 %norm_backward.2.rest_0_ = bf16[80,8192]{1,0:T(8,128)(2,1)S(1)} custom-call(s32[2]{0:T(128)S(1)} %pad_add_fusion.place_ref, bf16[128,8192]{1,0:T(8,128)(2,1)S(1)} %bitcast.17, bf16[1,8192]{1,0:T(2,128)(2,1)S(1)} %copy-done.6, bf16[128,8192]{1,0:T(8,128)(2,1)S(1)} %bitcast.19, bf16[80,2048]{1,0:T(8,128)(2,1)S(1)} %get-tuple-element.13.rest_0_, ...), custom_call_target="tpu_custom_call" | custom-call | flops 6553600 | bytes 5242880 | tf_op jit(solution)/shard_map/norm_backward/pallas_call | solution.py:253
  88.5 1.9 %collective-permute-start.11 = (bf16[80,8192]{1,0:T(8,128)(2,1)S(1)}, bf16[80,8192]{1,0:T(8,128)(2,1)S(1)}, u32[]{:S(2)}, u32[]{:S(2)}) collective-permute-start(bf16[80,8192]{1,0:T(8,128)(2,1)S(1)} %norm_backward.2.rest_0_), channel_id=1, source_target_pairs={{8,0},{16,8},{24,16},{9,1},{17,9},{25,17},{10,2},{18,10},{26,18},{... | collective-permute-start | bytes 3932168 | tf_op jit(solution)/shard_map/ppermute | solution.py:25
  90.5 1.3 norm_forward.6.rest_0_
  91.8 1.5 %norm_forward.7.rest_4_ = bf16[128,2560]{1,0:T(8,128)(2,1)S(1)} custom-call(s32[2]{0:T(128)S(1)} %pad_add_fusion.place_ref, bf16[128,8192]{1,0:T(8,128)(2,1)S(1)} %bitcast.16, bf16[1,8192]{1,0:T(2,128)(2,1)S(1)} %copy-done.5, bf16[128,512]{1,0:T(8,128)(2,1)S(1)} %attend.1.cot_ref, bf16[96,2560]{1,0:T(8,128)(2,1)S(1)} %norm_forward.6.rest_0_), custom_call_target="tpu_custom_call" | custom-call | flops 4194304 | bytes 2752512 | tf_op jit(solution)/shard_map/norm_forward/pallas_call | solution.py:92
  93.3 0.3 collective-permute-start.16
  93.7 1.3 collective-permute-start.19
  95.0 19.8 %collective-permute-done.13.rest_2_ = bf16[48,2048]{1,0:T(8,128)(2,1)S(1)} collective-permute-done((bf16[48,2048]{1,0:T(8,128)(2,1)S(1)}, bf16[48,2048]{1,0:T(8,128)(2,1)S(1)}, u32[]{:S(2)}, u32[]{:S(2)}) %collective-permute-start.13) | collective-permute-done | bytes 196640 | tf_op jit(solution)/shard_map/ppermute | solution.py:34
  114.7 0.7 collective-permute-start.20
  115.4 0.7 collective-permute-start.21
  116.1 1.7 %norm_backward.3.refs_12_ = bf16[48,8192]{1,0:T(8,128)(2,1)S(1)} custom-call(s32[2]{0:T(128)S(1)} %pad_add_fusion.place_ref, bf16[128,8192]{1,0:T(8,128)(2,1)S(1)} %bitcast.18, bf16[1,8192]{1,0:T(2,128)(2,1)S(1)} %copy-done.6, bf16[128,8192]{1,0:T(8,128)(2,1)S(1)} %bitcast.20, bf16[48,2048]{1,0:T(8,128)(2,1)S(1)} %get-tuple-element.18.rest_0_, ...), custom_call_target="tpu_custom_call" | custom-call | flops 3932160 | bytes 3145728 | tf_op jit(solution)/shard_map/norm_backward/pallas_call | solution.py:253
  117.8 6.1 %collective-permute-start.15 = (bf16[48,8192]{1,0:T(8,128)(2,1)S(1)}, bf16[48,8192]{1,0:T(8,128)(2,1)S(1)}, u32[]{:S(2)}, u32[]{:S(2)}) collective-permute-start(bf16[48,8192]{1,0:T(8,128)(2,1)S(1)} %norm_backward.3.refs_12_), channel_id=1, source_target_pairs={{8,0},{16,8},{24,16},{9,1},{17,9},{25,17},{10,2},{18,10},{26,18},{... | collective-permute-start | bytes 2359304 | tf_op jit(solution)/shard_map/ppermute | solution.py:25
  124.0 1.8 %outer.6.refs_4_ = f32[1024,512]{1,0:T(8,128)S(1)} custom-call(bf16[128,2560]{1,0:T(8,128)(2,1)S(1)} %get-tuple-element.12.refs_4_.refs_0_.refs_6_, bf16[128,2560]{1,0:T(8,128)(2,1)S(1)} %collective-permute-done.10.rest_4_.refs_1_.refs_7_, bf16[32,2560]{1,0:T(8,128)(2,1)S(1)} %get-tuple-element.25.refs_2_.refs_8_, ...), custom_call_target="tpu_custom_call" | custom-call | flops 402653184 | bytes 2883584 | tf_op jit(solution)/shard_map/outer/pallas_call | solution.py:300
  125.8 1.8 %outer.5.refs_5_.refs_4_ = f32[1024,512]{1,0:T(8,128)S(1)} custom-call(bf16[128,2560]{1,0:T(8,128)(2,1)S(1)} %get-tuple-element.12.refs_4_.refs_0_.refs_6_, bf16[128,2560]{1,0:T(8,128)(2,1)S(1)} %collective-permute-done.10.rest_4_.refs_1_.refs_7_, bf16[32,2560]{1,0:T(8,128)(2,1)S(1)} %get-tuple-element.25.refs_2_.refs_8_, ...), custom_call_target="tpu_custom_call" | custom-call | flops 402653184 | bytes 2883584 | tf_op jit(solution)/shard_map/outer/pallas_call | solution.py:300
  127.7 0.7 outer.8
  128.5 0.7 outer.7
  129.3 0.5 collective-permute-start.22
  129.8 0.6 collective-permute-done.23.refs_6_
  130.4 0.9 collective-permute-done.22.refs_5_
  131.4 2.6 %outer.9 = f32[1024,512]{1,0:T(8,128)} custom-call(bf16[128,2560]{1,0:T(8,128)(2,1)S(1)} %collective-permute-done.16.refs_0_.refs_2_, bf16[96,2560]{1,0:T(8,128)(2,1)S(1)} %collective-permute-done.17.refs_1_.refs_3_, bf16[128,2560]{1,0:T(8,128)(2,1)S(1)} %collective-permute-done.16.refs_0_.refs_2_, ...), custom_call_target="tpu_custom_call" | custom-call | flops 234881024 | bytes 2555904 | tf_op jit(solution)/shard_map/outer/pallas_call | solution.py:300
  134.0 1.3 collective-permute-done.15.refs_1_
  135.3 1.5 %stack_rows.3 = bf16[128,8192]{1,0:T(8,128)(2,1)} custom-call(bf16[80,8192]{1,0:T(8,128)(2,1)S(1)} %collective-permute-done.11.refs_0_, bf16[48,8192]{1,0:T(8,128)(2,1)S(1)} %collective-permute-done.15.refs_1_), custom_call_target="tpu_custom_call" | custom-call | bytes 4194304 | tf_op jit(solution)/shard_map/stack_rows/pallas_call | solution.py:117
  (40 shorter events, 0.5 us)
Async XLA Ops:
  0.6 15.0 %copy-start = (bf16[1,128,8192]{2,1,0:T(8,128)(2,1)S(1)}, bf16[1,128,8192]{2,1,0:T(8,128)(2,1)}, u32[]{:S(2)}) copy-start(bf16[1,128,8192]{2,1,0:T(8,128)(2,1)} %param.11) | copy-start | bytes 6291460
  0.6 15.0 %collective-permute-start = (bf16[1024,1024]{1,0:T(8,128)(2,1)}, bf16[1024,1024]{1,0:T(8,128)(2,1)}, u32[]{:S(2)}, u32[]{:S(2)}) collective-permute-start(bf16[1024,1024]{1,0:T(8,128)(2,1)} %bitcast.25), channel_id=1, source_target_pairs={{0,1},{1,0},{2,3},{3,2},{4,5},{5,4},{6,7},{7,6},{8,9},{9,8},{10,11... | collective-permute-start | bytes 6291464 | tf_op jit(solution)/shard_map/ppermute | solution.py:51
  0.7 17.8 %collective-permute-start.1 = (bf16[128,1024]{1,0:T(8,128)(2,1)}, bf16[128,1024]{1,0:T(8,128)(2,1)S(1)}, u32[]{:S(2)}, u32[]{:S(2)}) collective-permute-start(bf16[128,1024]{1,0:T(8,128)(2,1)} %bitcast.27), channel_id=1, source_target_pairs={{0,1},{1,0},{2,3},{3,2},{4,5},{5,4},{6,7},{7,6},{8,14},{9,15},{10,... | collective-permute-start | bytes 786440 | tf_op jit(solution)/shard_map/ppermute | solution.py:34
  1.2 20.8 %collective-permute-start.2 = (bf16[128,1024]{1,0:T(8,128)(2,1)}, bf16[128,1024]{1,0:T(8,128)(2,1)S(1)}, u32[]{:S(2)}, u32[]{:S(2)}) collective-permute-start(bf16[128,1024]{1,0:T(8,128)(2,1)} %bitcast.28), channel_id=1, source_target_pairs={{0,1},{1,0},{2,3},{3,2},{4,5},{5,4},{6,7},{7,6},{8,12},{9,13},{10,... | collective-permute-start | bytes 786440 | tf_op jit(solution)/shard_map/ppermute | solution.py:34
  3.8 23.1 %collective-permute-start.3 = (bf16[128,1024]{1,0:T(8,128)(2,1)}, bf16[128,1024]{1,0:T(8,128)(2,1)S(1)}, u32[]{:S(2)}, u32[]{:S(2)}) collective-permute-start(bf16[128,1024]{1,0:T(8,128)(2,1)} %bitcast.29), channel_id=1, source_target_pairs={{0,1},{1,0},{2,3},{3,2},{4,5},{5,4},{6,7},{7,6},{8,10},{9,11},{10,... | collective-permute-start | bytes 786440 | tf_op jit(solution)/shard_map/ppermute | solution.py:34
  7.1 1.2 copy-start.3
  8.3 1.2 copy-start.4
  9.5 0.9 copy-start.7
  10.4 0.7 copy-start.8
  11.1 4.6 %copy-start.5 = (bf16[1,8192]{1,0:T(2,128)(2,1)S(1)}, bf16[1,8192]{1,0:T(2,128)(2,1)}, u32[]{:S(2)}) copy-start(bf16[1,8192]{1,0:T(2,128)(2,1)} %gain_ref.10) | copy-start | bytes 49156
  16.4 15.4 %copy-start.9 = (bf16[1,1024,1024]{2,1,0:T(8,128)(2,1)S(1)}, bf16[1,1024,1024]{2,1,0:T(8,128)(2,1)}, u32[]{:S(2)}) copy-start(bf16[1,1024,1024]{2,1,0:T(8,128)(2,1)} %param.21) | copy-start | bytes 6291460
  16.4 15.4 %copy-start.10 = (bf16[1,128,1024]{2,1,0:T(8,128)(2,1)S(1)}, bf16[1,128,1024]{2,1,0:T(8,128)(2,1)}, u32[]{:S(2)}) copy-start(bf16[1,128,1024]{2,1,0:T(8,128)(2,1)} %param.20) | copy-start | bytes 786436
  16.4 14.5 %collective-permute-start.4 = (bf16[32,2560]{1,0:T(8,128)(2,1)S(1)}, bf16[32,2560]{1,0:T(8,128)(2,1)S(1)}, u32[]{:S(2)}, u32[]{:S(2)}) collective-permute-start(bf16[32,2560]{1,0:T(8,128)(2,1)S(1)} %norm_forward.4.refs_0_), channel_id=1, source_target_pairs={{8,0},{9,1},{10,2},{11,3},{12,4},{13,5},{14,6},{15,7}} | collective-permute-start | bytes 491528 | tf_op jit(solution)/shard_map/ppermute | solution.py:40
  17.9 13.0 %collective-permute-start.5 = (bf16[32,2560]{1,0:T(8,128)(2,1)S(1)}, bf16[32,2560]{1,0:T(8,128)(2,1)S(1)}, u32[]{:S(2)}, u32[]{:S(2)}) collective-permute-start(bf16[32,2560]{1,0:T(8,128)(2,1)S(1)} %norm_forward.4.refs_0_), channel_id=1, source_target_pairs={{16,0},{17,1},{18,2},{19,3},{20,4},{21,5},{22,6},{23,7}} | collective-permute-start | bytes 491528 | tf_op jit(solution)/shard_map/ppermute | solution.py:40
  18.6 12.3 %collective-permute-start.6 = (bf16[32,2560]{1,0:T(8,128)(2,1)S(1)}, bf16[32,2560]{1,0:T(8,128)(2,1)S(1)}, u32[]{:S(2)}, u32[]{:S(2)}) collective-permute-start(bf16[32,2560]{1,0:T(8,128)(2,1)S(1)} %norm_forward.4.refs_0_), channel_id=1, source_target_pairs={{24,0},{25,1},{26,2},{27,3},{28,4},{29,5},{30,6},{31,7}} | collective-permute-start | bytes 491528 | tf_op jit(solution)/shard_map/ppermute | solution.py:40
  28.5 17.7 %collective-permute-start.10 = (bf16[128,2560]{1,0:T(8,128)(2,1)S(1)}, bf16[128,2560]{1,0:T(8,128)(2,1)S(1)}, u32[]{:S(2)}, u32[]{:S(2)}) collective-permute-start(bf16[128,2560]{1,0:T(8,128)(2,1)S(1)} %get-tuple-element.17), channel_id=1, source_target_pairs={{0,2},{1,3},{2,4},{3,5},{4,6},{5,7},{6,0},{7,1},{8,10},{9,11},{10,... | collective-permute-start | bytes 1966088 | tf_op jit(solution)/shard_map/ppermute | solution.py:34
  31.0 55.0 %copy-start.1 = (bf16[1,128,8192]{2,1,0:T(8,128)(2,1)S(1)}, bf16[1,128,8192]{2,1,0:T(8,128)(2,1)}, u32[]{:S(2)}) copy-start(bf16[1,128,8192]{2,1,0:T(8,128)(2,1)} %param.17) | copy-start | bytes 6291460
  31.0 55.0 %copy-start.2 = (bf16[1,128,8192]{2,1,0:T(8,128)(2,1)S(1)}, bf16[1,128,8192]{2,1,0:T(8,128)(2,1)}, u32[]{:S(2)}) copy-start(bf16[1,128,8192]{2,1,0:T(8,128)(2,1)} %param.19) | copy-start | bytes 6291460
  31.0 55.0 %copy-start.6 = (bf16[1,8192]{1,0:T(2,128)(2,1)S(1)}, bf16[1,8192]{1,0:T(2,128)(2,1)}, u32[]{:S(2)}) copy-start(bf16[1,8192]{1,0:T(2,128)(2,1)} %gain_ref.11) | copy-start | bytes 49156
  31.0 62.6 %collective-permute-start.18 = (bf16[128,2560]{1,0:T(8,128)(2,1)S(1)}, bf16[128,2560]{1,0:T(8,128)(2,1)S(1)}, u32[]{:S(2)}, u32[]{:S(2)}) collective-permute-start(bf16[128,2560]{1,0:T(8,128)(2,1)S(1)} %stack_rows.2.rest_4_), channel_id=1, source_target_pairs={{0,4},{1,5},{2,6},{3,7},{4,0},{5,1},{6,2},{7,3}} | collective-permute-start | bytes 1966088 | tf_op jit(solution)/shard_map/ppermute | solution.py:46
  37.2 29.9 %collective-permute-start.7 = (bf16[80,2048]{1,0:T(8,128)(2,1)S(1)}, bf16[80,2048]{1,0:T(8,128)(2,1)S(1)}, u32[]{:S(2)}, u32[]{:S(2)}) collective-permute-start(bf16[80,2048]{1,0:T(8,128)(2,1)S(1)} %get-tuple-element.14), channel_id=1, source_target_pairs={{0,1},{1,0},{2,3},{3,2},{4,5},{5,4},{6,7},{7,6},{8,10},{9,11},{10,... | collective-permute-start | bytes 983048 | tf_op jit(solution)/shard_map/ppermute | solution.py:34
  37.3 45.3 %collective-permute-start.8 = (bf16[80,2048]{1,0:T(8,128)(2,1)S(1)}, bf16[80,2048]{1,0:T(8,128)(2,1)S(1)}, u32[]{:S(2)}, u32[]{:S(2)}) collective-permute-start(bf16[80,2048]{1,0:T(8,128)(2,1)S(1)} %get-tuple-element.15), channel_id=1, source_target_pairs={{0,1},{1,0},{2,3},{3,2},{4,5},{5,4},{6,7},{7,6},{8,12},{9,13},{10,... | collective-permute-start | bytes 983048 | tf_op jit(solution)/shard_map/ppermute | solution.py:34
  39.3 46.7 %collective-permute-start.9 = (bf16[80,2048]{1,0:T(8,128)(2,1)S(1)}, bf16[80,2048]{1,0:T(8,128)(2,1)S(1)}, u32[]{:S(2)}, u32[]{:S(2)}) collective-permute-start(bf16[80,2048]{1,0:T(8,128)(2,1)S(1)} %get-tuple-element.16), channel_id=1, source_target_pairs={{0,1},{1,0},{2,3},{3,2},{4,5},{5,4},{6,7},{7,6},{8,14},{9,15},{10,... | collective-permute-start | bytes 983048 | tf_op jit(solution)/shard_map/ppermute | solution.py:34
  46.2 44.3 %collective-permute-start.12 = (bf16[48,2048]{1,0:T(8,128)(2,1)S(1)}, bf16[48,2048]{1,0:T(8,128)(2,1)S(1)}, u32[]{:S(2)}, u32[]{:S(2)}) collective-permute-start(bf16[48,2048]{1,0:T(8,128)(2,1)S(1)} %get-tuple-element.19), channel_id=1, source_target_pairs={{0,1},{1,0},{2,3},{3,2},{4,5},{5,4},{6,7},{7,6},{8,10},{9,11},{10,... | collective-permute-start | bytes 589832 | tf_op jit(solution)/shard_map/ppermute | solution.py:34
  67.2 23.3 %collective-permute-start.14 = (bf16[48,2048]{1,0:T(8,128)(2,1)S(1)}, bf16[48,2048]{1,0:T(8,128)(2,1)S(1)}, u32[]{:S(2)}, u32[]{:S(2)}) collective-permute-start(bf16[48,2048]{1,0:T(8,128)(2,1)S(1)} %get-tuple-element.21), channel_id=1, source_target_pairs={{0,1},{1,0},{2,3},{3,2},{4,5},{5,4},{6,7},{7,6},{8,14},{9,15},{10,... | collective-permute-start | bytes 589832 | tf_op jit(solution)/shard_map/ppermute | solution.py:34
  82.6 32.1 %collective-permute-start.13 = (bf16[48,2048]{1,0:T(8,128)(2,1)S(1)}, bf16[48,2048]{1,0:T(8,128)(2,1)S(1)}, u32[]{:S(2)}, u32[]{:S(2)}) collective-permute-start(bf16[48,2048]{1,0:T(8,128)(2,1)S(1)} %get-tuple-element.20), channel_id=1, source_target_pairs={{0,1},{1,0},{2,3},{3,2},{4,5},{5,4},{6,7},{7,6},{8,12},{9,13},{10,... | collective-permute-start | bytes 589832 | tf_op jit(solution)/shard_map/ppermute | solution.py:34
  88.5 46.8 %collective-permute-start.11 = (bf16[80,8192]{1,0:T(8,128)(2,1)S(1)}, bf16[80,8192]{1,0:T(8,128)(2,1)S(1)}, u32[]{:S(2)}, u32[]{:S(2)}) collective-permute-start(bf16[80,8192]{1,0:T(8,128)(2,1)S(1)} %norm_backward.2.rest_0_), channel_id=1, source_target_pairs={{8,0},{16,8},{24,16},{9,1},{17,9},{25,17},{10,2},{18,10},{26,18},{... | collective-permute-start | bytes 3932168 | tf_op jit(solution)/shard_map/ppermute | solution.py:25
  91.8 35.9 %collective-permute-start.17 = (bf16[96,2560]{1,0:T(8,128)(2,1)S(1)}, bf16[96,2560]{1,0:T(8,128)(2,1)S(1)}, u32[]{:S(2)}, u32[]{:S(2)}) collective-permute-start(bf16[96,2560]{1,0:T(8,128)(2,1)S(1)} %norm_forward.6.rest_0_), channel_id=1, source_target_pairs={{0,4},{1,5},{2,6},{3,7},{4,0},{5,1},{6,2},{7,3},{8,12},{9,13},{10,... | collective-permute-start | bytes 1474568 | tf_op jit(solution)/shard_map/ppermute | solution.py:34
  93.3 34.4 %collective-permute-start.16 = (bf16[128,2560]{1,0:T(8,128)(2,1)S(1)}, bf16[128,2560]{1,0:T(8,128)(2,1)S(1)}, u32[]{:S(2)}, u32[]{:S(2)}) collective-permute-start(bf16[128,2560]{1,0:T(8,128)(2,1)S(1)} %norm_forward.7.rest_4_), channel_id=1, source_target_pairs={{0,6},{1,7},{2,0},{3,1},{4,2},{5,3},{6,4},{7,5},{8,14},{9,15},{10,... | collective-permute-start | bytes 1966088 | tf_op jit(solution)/shard_map/ppermute | solution.py:34
  93.7 21.7 %collective-permute-start.19 = (bf16[32,2560]{1,0:T(8,128)(2,1)S(1)}, bf16[32,2560]{1,0:T(8,128)(2,1)S(1)}, u32[]{:S(2)}, u32[]{:S(2)}) collective-permute-start(bf16[32,2560]{1,0:T(8,128)(2,1)S(1)} %get-tuple-element.24), channel_id=1, source_target_pairs={{0,8},{1,9},{2,10},{3,11},{4,12},{5,13},{6,14},{7,15}} | collective-permute-start | bytes 491528 | tf_op jit(solution)/shard_map/ppermute | solution.py:40
  114.7 3.1 %collective-permute-start.20 = (bf16[32,2560]{1,0:T(8,128)(2,1)S(1)}, bf16[32,2560]{1,0:T(8,128)(2,1)S(1)}, u32[]{:S(2)}, u32[]{:S(2)}) collective-permute-start(bf16[32,2560]{1,0:T(8,128)(2,1)S(1)} %get-tuple-element.23), channel_id=1, source_target_pairs={{0,16},{1,17},{2,18},{3,19},{4,20},{5,21},{6,22},{7,23}} | collective-permute-start | bytes 491528 | tf_op jit(solution)/shard_map/ppermute | solution.py:40
  115.4 8.6 %collective-permute-start.21 = (bf16[32,2560]{1,0:T(8,128)(2,1)S(1)}, bf16[32,2560]{1,0:T(8,128)(2,1)S(1)}, u32[]{:S(2)}, u32[]{:S(2)}) collective-permute-start(bf16[32,2560]{1,0:T(8,128)(2,1)S(1)} %get-tuple-element.22), channel_id=1, source_target_pairs={{0,24},{1,25},{2,26},{3,27},{4,28},{5,29},{6,30},{7,31}} | collective-permute-start | bytes 491528 | tf_op jit(solution)/shard_map/ppermute | solution.py:40
  117.8 17.5 %collective-permute-start.15 = (bf16[48,8192]{1,0:T(8,128)(2,1)S(1)}, bf16[48,8192]{1,0:T(8,128)(2,1)S(1)}, u32[]{:S(2)}, u32[]{:S(2)}) collective-permute-start(bf16[48,8192]{1,0:T(8,128)(2,1)S(1)} %norm_backward.3.refs_12_), channel_id=1, source_target_pairs={{8,0},{16,8},{24,16},{9,1},{17,9},{25,17},{10,2},{18,10},{26,18},{... | collective-permute-start | bytes 2359304 | tf_op jit(solution)/shard_map/ppermute | solution.py:25
  128.4 2.0 %collective-permute-start.23 = (bf16[512,512]{1,0:T(8,128)(2,1)S(1)}, bf16[512,512]{1,0:T(8,128)(2,1)S(1)}, u32[]{:S(2)}, u32[]{:S(2)}) collective-permute-start(bf16[512,512]{1,0:T(8,128)(2,1)S(1)} %outer.8), channel_id=1, source_target_pairs={{0,1},{1,0},{2,3},{3,2},{4,5},{5,4},{6,7},{7,6},{8,9},{9,8},{10,11... | collective-permute-start | bytes 1572872 | tf_op jit(solution)/shard_map/ppermute | solution.py:51
  129.3 2.1 %collective-permute-start.22 = (bf16[512,512]{1,0:T(8,128)(2,1)S(1)}, bf16[512,512]{1,0:T(8,128)(2,1)S(1)}, u32[]{:S(2)}, u32[]{:S(2)}) collective-permute-start(bf16[512,512]{1,0:T(8,128)(2,1)S(1)} %outer.7), channel_id=1, source_target_pairs={{0,1},{1,0},{2,3},{3,2},{4,5},{5,4},{6,7},{7,6},{8,9},{9,8},{10,11... | collective-permute-start | bytes 1572872 | tf_op jit(solution)/shard_map/ppermute | solution.py:51

commit v3 on v2

--- a/solution.py
+++ b/solution.py
@@ -334,7 +334,7 @@
     place = jnp.stack([at // CORES, at % CORES]).astype(jnp.int32)
     middle = chips // 2
     near = [by for by in range(1, chips) if by != middle]
-    spread = tokens // 4
+    spread = tokens // 8
 
     rows = [kv_grad[0]] + [along_chips(kv_grad[0], chips - by, 1) for by in range(1, chips)]
     other_weight = swap_cores(kv_weight[0])

time: 139 us -> 142 us (1.022)
  the two profiles are of different devices: /device:TPU:10 before, /device:TPU:31 now
where the time goes in v3:
time: 142 us; the launch traced here: 141 us
  waiting for transfers between devices  69.5 us (49%)
  starting transfers between devices  37.3 us (26%)
  Pallas kernels  28.7 us (20%)
  local copies, waits for them, and re-layouts  4.83 us (3%)
    ppermute x12, waiting for transfers between devices, along_chips(): return lax.ppermute(array, ('pipe', 'dp'), pairs)  61.1 us
    ppermute x12, starting transfers between devices, along_chips(): return lax.ppermute(array, ('pipe', 'dp'), pairs)  19.6 us
    pallas_call x5, Pallas kernels, outer(): call(functools.partial(outer_kernel, [len(group) for group in groups], le...  7.68 us
    ppermute x6, waiting for transfers between devices, between_lines(): return lax.ppermute(array, ('pipe', 'dp'), pairs)  6.53 us
    ppermute x2, starting transfers between devices, from_behind(): return lax.ppermute(array, axis, pairs)  5.9 us
    ppermute x3, starting transfers between devices, swap_cores(): return lax.ppermute(array, 'dp', [(i, i ^ 1) for i in range(length)])  5.88 us
    pallas_call x4, Pallas kernels, normalize(): call(functools.partial(norm_kernel, chips, ahead), 'norm_forward', 4 * co...  5.6 us
    ppermute x6, starting transfers between devices, between_lines(): return lax.ppermute(array, ('pipe', 'dp'), pairs)  5.25 us
  transfers between devices with their start and end apart: 24, of which 9 were waited for; matrix products, arithmetic and copies ran while one was open for 1% of the time, Pallas kernels for 19%

profile of v3, /device:TPU:31, one launch (start us, length us, event | category | flops | bytes accessed | tf_op | source)
XLA Modules:
  0.0 141.4 jit_solution(4130966708259467744)
XLA Ops:
  0.6 0.7 collective-permute-start
  1.4 0.2 collective-permute-start.1
  1.6 3.0 %collective-permute-start.3 = (bf16[128,1024]{1,0:T(8,128)(2,1)}, bf16[128,1024]{1,0:T(8,128)(2,1)S(1)}, u32[]{:S(2)}, u32[]{:S(2)}) collective-permute-start(bf16[128,1024]{1,0:T(8,128)(2,1)} %bitcast.29), channel_id=1, source_target_pairs={{0,1},{1,0},{2,3},{3,2},{4,5},{5,4},{6,7},{7,6},{8,10},{9,11},{10,... | collective-permute-start | bytes 786440 | tf_op jit(solution)/shard_map/ppermute | solution.py:34
  4.6 0.8 copy.13.col_seg_ref
  5.4 1.2 copy-done.3
  6.7 1.2 copy-done.4
  7.9 0.9 copy-done.7
  8.8 0.7 copy-done.8
  9.4 4.5 %attend.1.cot_ref = bf16[128,512]{1,0:T(8,128)(2,1)S(1)} custom-call(bf16[128,4096]{1,0:T(8,128)(2,1)S(1)} %bitcast.21, bf16[128,512]{1,0:T(8,128)(2,1)S(1)} %bitcast.23, bf16[128,4096]{1,0:T(8,128)(2,1)S(1)} %bitcast.22, s32[1,128]{1,0:T(1,128)S(1)} %copy-done.8, s32[128,1]{1,0:T(8,128)S(1)} %copy.13.col_seg_ref), custom_call_target="tpu_custom_call" | custom-call | flops 268435456 | bytes 2097152 | tf_op jit(solution)/shard_map/attend/pallas_call | solution.py:155
  14.0 7.5 %collective-permute-done.2.rest_1_.rest_2_ = bf16[128,1024]{1,0:T(8,128)(2,1)S(1)} collective-permute-done((bf16[128,1024]{1,0:T(8,128)(2,1)}, bf16[128,1024]{1,0:T(8,128)(2,1)S(1)}, u32[]{:S(2)}, u32[]{:S(2)}) %collective-permute-start.2) | collective-permute-done | bytes 262176 | tf_op jit(solution)/shard_map/ppermute | solution.py:34
  21.5 1.6 %norm_forward.5 = (bf16[128,2560]{1,0:T(8,128)(2,1)S(1)}, bf16[128,2560]{1,0:T(8,128)(2,1)S(1)}) custom-call(s32[2]{0:T(128)S(1)} %pad_add_fusion.place_ref, bf16[128,8192]{1,0:T(8,128)(2,1)S(1)} %bitcast.13, bf16[1,8192]{1,0:T(2,128)(2,1)S(1)} %copy-done.5, bf16[128,512]{1,0:T(8,128)(2,1)S(1)} %attend.1.cot_ref, ...), custom_call_target="tpu_custom_call" | custom-call | flops 4194304 | bytes 3407872 | tf_op jit(solution)/shard_map/norm_forward/pallas_call | solution.py:92
  23.1 5.8 %collective-permute-start.10 = (bf16[128,2560]{1,0:T(8,128)(2,1)S(1)}, bf16[128,2560]{1,0:T(8,128)(2,1)S(1)}, u32[]{:S(2)}, u32[]{:S(2)}) collective-permute-start(bf16[128,2560]{1,0:T(8,128)(2,1)S(1)} %get-tuple-element.17), channel_id=1, source_target_pairs={{0,2},{1,3},{2,4},{3,5},{4,6},{5,7},{6,0},{7,1},{8,10},{9,11},{10,... | collective-permute-start | bytes 1966088 | tf_op jit(solution)/shard_map/ppermute | solution.py:34
  28.9 0.7 norm_forward.4.refs_0_
  29.6 0.7 collective-permute-start.4
  30.3 0.7 collective-permute-start.5
  31.0 1.3 collective-permute-start.6
  32.3 1.4 %collective-permute-done.6.refs_3_ = bf16[16,2560]{1,0:T(8,128)(2,1)S(1)} collective-permute-done((bf16[16,2560]{1,0:T(8,128)(2,1)S(1)}, bf16[16,2560]{1,0:T(8,128)(2,1)S(1)}, u32[]{:S(2)}, u32[]{:S(2)}) %collective-permute-start.6) | collective-permute-done | bytes 81952 | tf_op jit(solution)/shard_map/ppermute | solution.py:40
  33.8 5.2 %project.1 = (bf16[80,2048]{1,0:T(8,128)(2,1)S(1)}, bf16[80,2048]{1,0:T(8,128)(2,1)S(1)}, bf16[80,2048]{1,0:T(8,128)(2,1)S(1)}, bf16[80,2048]{1,0:T(8,128)(2,1)S...) custom-call(bf16[1024,1024]{1,0:T(8,128)(2,1)S(1)} %bitcast.26, ...), custom_call_target="tpu_custom_call" | custom-call | flops 2147483648 | bytes 7340032 | tf_op jit(solution)/shard_map/project/pallas_call | solution.py:206
  39.0 0.4 collective-permute-start.7
  39.4 1.0 collective-permute-start.8
  40.4 1.4 collective-permute-start.9
  41.8 0.7 collective-permute-start.18
  42.5 0.4 collective-permute-done.10.rest_4_.refs_1_.refs_7_
  42.9 3.2 %collective-permute-start.12 = (bf16[48,2048]{1,0:T(8,128)(2,1)S(1)}, bf16[48,2048]{1,0:T(8,128)(2,1)S(1)}, u32[]{:S(2)}, u32[]{:S(2)}) collective-permute-start(bf16[48,2048]{1,0:T(8,128)(2,1)S(1)} %get-tuple-element.19), channel_id=1, source_target_pairs={{0,1},{1,0},{2,3},{3,2},{4,5},{5,4},{6,7},{7,6},{8,10},{9,11},{10,... | collective-permute-start | bytes 589832 | tf_op jit(solution)/shard_map/ppermute | solution.py:34
  46.1 3.8 %collective-permute-done.7.rest_1_ = bf16[80,2048]{1,0:T(8,128)(2,1)S(1)} collective-permute-done((bf16[80,2048]{1,0:T(8,128)(2,1)S(1)}, bf16[80,2048]{1,0:T(8,128)(2,1)S(1)}, u32[]{:S(2)}, u32[]{:S(2)}) %collective-permute-start.7) | collective-permute-done | bytes 327712 | tf_op jit(solution)/shard_map/ppermute | solution.py:34
  50.0 2.1 %collective-permute-start.14 = (bf16[48,2048]{1,0:T(8,128)(2,1)S(1)}, bf16[48,2048]{1,0:T(8,128)(2,1)S(1)}, u32[]{:S(2)}, u32[]{:S(2)}) collective-permute-start(bf16[48,2048]{1,0:T(8,128)(2,1)S(1)} %get-tuple-element.21), channel_id=1, source_target_pairs={{0,1},{1,0},{2,3},{3,2},{4,5},{5,4},{6,7},{7,6},{8,14},{9,15},{10,... | collective-permute-start | bytes 589832 | tf_op jit(solution)/shard_map/ppermute | solution.py:34
  52.0 28.3 %collective-permute-done.8.rest_2_ = bf16[80,2048]{1,0:T(8,128)(2,1)S(1)} collective-permute-done((bf16[80,2048]{1,0:T(8,128)(2,1)S(1)}, bf16[80,2048]{1,0:T(8,128)(2,1)S(1)}, u32[]{:S(2)}, u32[]{:S(2)}) %collective-permute-start.8) | collective-permute-done | bytes 327712 | tf_op jit(solution)/shard_map/ppermute | solution.py:34
  80.4 2.5 %norm_backward.2.rest_0_ = bf16[80,8192]{1,0:T(8,128)(2,1)S(1)} custom-call(s32[2]{0:T(128)S(1)} %pad_add_fusion.place_ref, bf16[128,8192]{1,0:T(8,128)(2,1)S(1)} %bitcast.17, bf16[1,8192]{1,0:T(2,128)(2,1)S(1)} %copy-done.6, bf16[128,8192]{1,0:T(8,128)(2,1)S(1)} %bitcast.19, bf16[80,2048]{1,0:T(8,128)(2,1)S(1)} %get-tuple-element.13.rest_0_, ...), custom_call_target="tpu_custom_call" | custom-call | flops 6553600 | bytes 5242880 | tf_op jit(solution)/shard_map/norm_backward/pallas_call | solution.py:253
  82.9 2.2 %collective-permute-start.11 = (bf16[80,8192]{1,0:T(8,128)(2,1)S(1)}, bf16[80,8192]{1,0:T(8,128)(2,1)S(1)}, u32[]{:S(2)}, u32[]{:S(2)}) collective-permute-start(bf16[80,8192]{1,0:T(8,128)(2,1)S(1)} %norm_backward.2.rest_0_), channel_id=1, source_target_pairs={{8,0},{16,8},{24,16},{9,1},{17,9},{25,17},{10,2},{18,10},{26,18},{... | collective-permute-start | bytes 3932168 | tf_op jit(solution)/shard_map/ppermute | solution.py:25
  85.2 1.9 %norm_forward.6.rest_0_ = bf16[112,2560]{1,0:T(8,128)(2,1)S(1)} custom-call(s32[2]{0:T(128)S(1)} %pad_add_fusion.place_ref, bf16[128,8192]{1,0:T(8,128)(2,1)S(1)} %bitcast.15, bf16[1,8192]{1,0:T(2,128)(2,1)S(1)} %copy-done.5, bf16[128,512]{1,0:T(8,128)(2,1)S(1)} %attend.1.cot_ref, bf16[80,8192]{1,0:T(8,128)(2,1)S(1)} %norm_backward.2.rest_0_, ...), custom_call_target="tpu_custom_call" | custom-call | flops 3670016 | bytes 2408448 | tf_op jit(solution)/shard_map/norm_forward/pallas_call | solution.py:92
  87.0 2.4 %collective-permute-start.17 = (bf16[112,2560]{1,0:T(8,128)(2,1)S(1)}, bf16[112,2560]{1,0:T(8,128)(2,1)S(1)}, u32[]{:S(2)}, u32[]{:S(2)}) collective-permute-start(bf16[112,2560]{1,0:T(8,128)(2,1)S(1)} %norm_forward.6.rest_0_), channel_id=1, source_target_pairs={{0,4},{1,5},{2,6},{3,7},{4,0},{5,1},{6,2},{7,3},{8,12},{9,13},{10,... | collective-permute-start | bytes 1720328 | tf_op jit(solution)/shard_map/ppermute | solution.py:34
  89.4 1.5 %norm_forward.7.rest_4_ = bf16[128,2560]{1,0:T(8,128)(2,1)S(1)} custom-call(s32[2]{0:T(128)S(1)} %pad_add_fusion.place_ref, bf16[128,8192]{1,0:T(8,128)(2,1)S(1)} %bitcast.16, bf16[1,8192]{1,0:T(2,128)(2,1)S(1)} %copy-done.5, bf16[128,512]{1,0:T(8,128)(2,1)S(1)} %attend.1.cot_ref, bf16[112,2560]{1,0:T(8,128)(2,1)S(1)} %norm_forward.6.rest_0_), custom_call_target="tpu_custom_call" | custom-call | flops 4194304 | bytes 2752512 | tf_op jit(solution)/shard_map/norm_forward/pallas_call | solution.py:92
  91.0 0.7 collective-permute-start.19
  91.7 0.7 collective-permute-start.20
  92.4 1.7 %norm_backward.3.refs_12_ = bf16[48,8192]{1,0:T(8,128)(2,1)S(1)} custom-call(s32[2]{0:T(128)S(1)} %pad_add_fusion.place_ref, bf16[128,8192]{1,0:T(8,128)(2,1)S(1)} %bitcast.18, bf16[1,8192]{1,0:T(2,128)(2,1)S(1)} %copy-done.6, bf16[128,8192]{1,0:T(8,128)(2,1)S(1)} %bitcast.20, bf16[48,2048]{1,0:T(8,128)(2,1)S(1)} %get-tuple-element.18.rest_0_, ...), custom_call_target="tpu_custom_call" | custom-call | flops 3932160 | bytes 3145728 | tf_op jit(solution)/shard_map/norm_backward/pallas_call | solution.py:253
  94.2 3.7 %collective-permute-start.15 = (bf16[48,8192]{1,0:T(8,128)(2,1)S(1)}, bf16[48,8192]{1,0:T(8,128)(2,1)S(1)}, u32[]{:S(2)}, u32[]{:S(2)}) collective-permute-start(bf16[48,8192]{1,0:T(8,128)(2,1)S(1)} %norm_backward.3.refs_12_), channel_id=1, source_target_pairs={{8,0},{16,8},{24,16},{9,1},{17,9},{25,17},{10,2},{18,10},{26,18},{... | collective-permute-start | bytes 2359304 | tf_op jit(solution)/shard_map/ppermute | solution.py:25
  97.8 1.3 collective-permute-start.21
  99.1 5.1 %collective-permute-done.21.refs_5_.refs_11_ = bf16[16,2560]{1,0:T(8,128)(2,1)S(1)} collective-permute-done((bf16[16,2560]{1,0:T(8,128)(2,1)S(1)}, bf16[16,2560]{1,0:T(8,128)(2,1)S(1)}, u32[]{:S(2)}, u32[]{:S(2)}) %collective-permute-start.21) | collective-permute-done | bytes 81952 | tf_op jit(solution)/shard_map/ppermute | solution.py:40
  104.2 1.8 %outer.6.refs_4_ = f32[1024,512]{1,0:T(8,128)S(1)} custom-call(bf16[128,2560]{1,0:T(8,128)(2,1)S(1)} %get-tuple-element.12.refs_4_.refs_0_.refs_6_, bf16[128,2560]{1,0:T(8,128)(2,1)S(1)} %collective-permute-done.10.rest_4_.refs_1_.refs_7_, bf16[16,2560]{1,0:T(8,128)(2,1)S(1)} %get-tuple-element.25.refs_2_.refs_8_, ...), custom_call_target="tpu_custom_call" | custom-call | flops 335544320 | bytes 2752512 | tf_op jit(solution)/shard_map/outer/pallas_call | solution.py:300
  106.0 1.8 %outer.5.refs_5_.refs_4_ = f32[1024,512]{1,0:T(8,128)S(1)} custom-call(bf16[128,2560]{1,0:T(8,128)(2,1)S(1)} %get-tuple-element.12.refs_4_.refs_0_.refs_6_, bf16[128,2560]{1,0:T(8,128)(2,1)S(1)} %collective-permute-done.10.rest_4_.refs_1_.refs_7_, bf16[16,2560]{1,0:T(8,128)(2,1)S(1)} %get-tuple-element.25.refs_2_.refs_8_, ...), custom_call_target="tpu_custom_call" | custom-call | flops 335544320 | bytes 2752512 | tf_op jit(solution)/shard_map/outer/pallas_call | solution.py:300
  107.8 21.0 %collective-permute-done.17.refs_1_.refs_3_ = bf16[112,2560]{1,0:T(8,128)(2,1)S(1)} collective-permute-done((bf16[112,2560]{1,0:T(8,128)(2,1)S(1)}, bf16[112,2560]{1,0:T(8,128)(2,1)S(1)}, u32[]{:S(2)}, u32[]{:S(2)}) %collective-permute-start.17) | collective-permute-done | bytes 573472 | tf_op jit(solution)/shard_map/ppermute | solution.py:34
  128.8 0.7 outer.8
  129.6 5.0 %collective-permute-start.23 = (bf16[512,512]{1,0:T(8,128)(2,1)S(1)}, bf16[512,512]{1,0:T(8,128)(2,1)S(1)}, u32[]{:S(2)}, u32[]{:S(2)}) collective-permute-start(bf16[512,512]{1,0:T(8,128)(2,1)S(1)} %outer.8), channel_id=1, source_target_pairs={{0,1},{1,0},{2,3},{3,2},{4,5},{5,4},{6,7},{7,6},{8,9},{9,8},{10,11... | collective-permute-start | bytes 1572872 | tf_op jit(solution)/shard_map/ppermute | solution.py:51
  134.6 0.7 outer.7
  135.5 0.7 collective-permute-done.23.refs_6_
  136.2 1.2 collective-permute-done.22.refs_5_
  137.3 2.6 %outer.9 = f32[1024,512]{1,0:T(8,128)} custom-call(bf16[128,2560]{1,0:T(8,128)(2,1)S(1)} %collective-permute-done.16.refs_0_.refs_2_, bf16[112,2560]{1,0:T(8,128)(2,1)S(1)} %collective-permute-done.17.refs_1_.refs_3_, bf16[128,2560]{1,0:T(8,128)(2,1)S(1)} %collective-permute-done.16.refs_0_.refs_2_, ...), custom_call_target="tpu_custom_call" | custom-call | flops 251658240 | bytes 2588672 | tf_op jit(solution)/shard_map/outer/pallas_call | solution.py:300
  140.0 1.5 %stack_rows.3 = bf16[128,8192]{1,0:T(8,128)(2,1)} custom-call(bf16[80,8192]{1,0:T(8,128)(2,1)S(1)} %collective-permute-done.11.refs_0_, bf16[48,8192]{1,0:T(8,128)(2,1)S(1)} %collective-permute-done.15.refs_1_), custom_call_target="tpu_custom_call" | custom-call | bytes 4194304 | tf_op jit(solution)/shard_map/stack_rows/pallas_call | solution.py:117
  (40 shorter events, 0.4 us)
Async XLA Ops:
  0.6 20.9 %copy-start = (bf16[1,128,8192]{2,1,0:T(8,128)(2,1)S(1)}, bf16[1,128,8192]{2,1,0:T(8,128)(2,1)}, u32[]{:S(2)}) copy-start(bf16[1,128,8192]{2,1,0:T(8,128)(2,1)} %param.11) | copy-start | bytes 6291460
  0.6 28.3 %collective-permute-start = (bf16[1024,1024]{1,0:T(8,128)(2,1)}, bf16[1024,1024]{1,0:T(8,128)(2,1)}, u32[]{:S(2)}, u32[]{:S(2)}) collective-permute-start(bf16[1024,1024]{1,0:T(8,128)(2,1)} %bitcast.25), channel_id=1, source_target_pairs={{0,1},{1,0},{2,3},{3,2},{4,5},{5,4},{6,7},{7,6},{8,9},{9,8},{10,11... | collective-permute-start | bytes 6291464 | tf_op jit(solution)/shard_map/ppermute | solution.py:51
  1.4 12.6 %collective-permute-start.1 = (bf16[128,1024]{1,0:T(8,128)(2,1)}, bf16[128,1024]{1,0:T(8,128)(2,1)S(1)}, u32[]{:S(2)}, u32[]{:S(2)}) collective-permute-start(bf16[128,1024]{1,0:T(8,128)(2,1)} %bitcast.27), channel_id=1, source_target_pairs={{0,1},{1,0},{2,3},{3,2},{4,5},{5,4},{6,7},{7,6},{8,14},{9,15},{10,... | collective-permute-start | bytes 786440 | tf_op jit(solution)/shard_map/ppermute | solution.py:34
  1.5 19.9 %collective-permute-start.2 = (bf16[128,1024]{1,0:T(8,128)(2,1)}, bf16[128,1024]{1,0:T(8,128)(2,1)S(1)}, u32[]{:S(2)}, u32[]{:S(2)}) collective-permute-start(bf16[128,1024]{1,0:T(8,128)(2,1)} %bitcast.28), channel_id=1, source_target_pairs={{0,1},{1,0},{2,3},{3,2},{4,5},{5,4},{6,7},{7,6},{8,12},{9,13},{10,... | collective-permute-start | bytes 786440 | tf_op jit(solution)/shard_map/ppermute | solution.py:34
  1.6 19.9 %collective-permute-start.3 = (bf16[128,1024]{1,0:T(8,128)(2,1)}, bf16[128,1024]{1,0:T(8,128)(2,1)S(1)}, u32[]{:S(2)}, u32[]{:S(2)}) collective-permute-start(bf16[128,1024]{1,0:T(8,128)(2,1)} %bitcast.29), channel_id=1, source_target_pairs={{0,1},{1,0},{2,3},{3,2},{4,5},{5,4},{6,7},{7,6},{8,10},{9,11},{10,... | collective-permute-start | bytes 786440 | tf_op jit(solution)/shard_map/ppermute | solution.py:34
  5.4 1.2 copy-start.3
  6.6 1.2 copy-start.4
  7.9 0.9 copy-start.7
  8.8 0.7 copy-start.8
  9.4 12.1 %copy-start.5 = (bf16[1,8192]{1,0:T(2,128)(2,1)S(1)}, bf16[1,8192]{1,0:T(2,128)(2,1)}, u32[]{:S(2)}) copy-start(bf16[1,8192]{1,0:T(2,128)(2,1)} %gain_ref.10) | copy-start | bytes 49156
  23.1 10.7 %copy-start.9 = (bf16[1,1024,1024]{2,1,0:T(8,128)(2,1)S(1)}, bf16[1,1024,1024]{2,1,0:T(8,128)(2,1)}, u32[]{:S(2)}) copy-start(bf16[1,1024,1024]{2,1,0:T(8,128)(2,1)} %param.21) | copy-start | bytes 6291460
  23.1 10.7 %copy-start.10 = (bf16[1,128,1024]{2,1,0:T(8,128)(2,1)S(1)}, bf16[1,128,1024]{2,1,0:T(8,128)(2,1)}, u32[]{:S(2)}) copy-start(bf16[1,128,1024]{2,1,0:T(8,128)(2,1)} %param.20) | copy-start | bytes 786436
  23.1 19.8 %collective-permute-start.10 = (bf16[128,2560]{1,0:T(8,128)(2,1)S(1)}, bf16[128,2560]{1,0:T(8,128)(2,1)S(1)}, u32[]{:S(2)}, u32[]{:S(2)}) collective-permute-start(bf16[128,2560]{1,0:T(8,128)(2,1)S(1)} %get-tuple-element.17), channel_id=1, source_target_pairs={{0,2},{1,3},{2,4},{3,5},{4,6},{5,7},{6,0},{7,1},{8,10},{9,11},{10,... | collective-permute-start | bytes 1966088 | tf_op jit(solution)/shard_map/ppermute | solution.py:34
  29.6 2.7 %collective-permute-start.4 = (bf16[16,2560]{1,0:T(8,128)(2,1)S(1)}, bf16[16,2560]{1,0:T(8,128)(2,1)S(1)}, u32[]{:S(2)}, u32[]{:S(2)}) collective-permute-start(bf16[16,2560]{1,0:T(8,128)(2,1)S(1)} %norm_forward.4.refs_0_), channel_id=1, source_target_pairs={{8,0},{9,1},{10,2},{11,3},{12,4},{13,5},{14,6},{15,7}} | collective-permute-start | bytes 245768 | tf_op jit(solution)/shard_map/ppermute | solution.py:40
  30.3 2.0 %collective-permute-start.5 = (bf16[16,2560]{1,0:T(8,128)(2,1)S(1)}, bf16[16,2560]{1,0:T(8,128)(2,1)S(1)}, u32[]{:S(2)}, u32[]{:S(2)}) collective-permute-start(bf16[16,2560]{1,0:T(8,128)(2,1)S(1)} %norm_forward.4.refs_0_), channel_id=1, source_target_pairs={{16,0},{17,1},{18,2},{19,3},{20,4},{21,5},{22,6},{23,7}} | collective-permute-start | bytes 245768 | tf_op jit(solution)/shard_map/ppermute | solution.py:40
  31.0 2.8 %collective-permute-start.6 = (bf16[16,2560]{1,0:T(8,128)(2,1)S(1)}, bf16[16,2560]{1,0:T(8,128)(2,1)S(1)}, u32[]{:S(2)}, u32[]{:S(2)}) collective-permute-start(bf16[16,2560]{1,0:T(8,128)(2,1)S(1)} %norm_forward.4.refs_0_), channel_id=1, source_target_pairs={{24,0},{25,1},{26,2},{27,3},{28,4},{29,5},{30,6},{31,7}} | collective-permute-start | bytes 245768 | tf_op jit(solution)/shard_map/ppermute | solution.py:40
  33.8 46.5 %copy-start.1 = (bf16[1,128,8192]{2,1,0:T(8,128)(2,1)S(1)}, bf16[1,128,8192]{2,1,0:T(8,128)(2,1)}, u32[]{:S(2)}) copy-start(bf16[1,128,8192]{2,1,0:T(8,128)(2,1)} %param.17) | copy-start | bytes 6291460
  33.8 46.5 %copy-start.2 = (bf16[1,128,8192]{2,1,0:T(8,128)(2,1)S(1)}, bf16[1,128,8192]{2,1,0:T(8,128)(2,1)}, u32[]{:S(2)}) copy-start(bf16[1,128,8192]{2,1,0:T(8,128)(2,1)} %param.19) | copy-start | bytes 6291460
  33.8 46.5 %copy-start.6 = (bf16[1,8192]{1,0:T(2,128)(2,1)S(1)}, bf16[1,8192]{1,0:T(2,128)(2,1)}, u32[]{:S(2)}) copy-start(bf16[1,8192]{1,0:T(2,128)(2,1)} %gain_ref.11) | copy-start | bytes 49156
  39.0 10.9 %collective-permute-start.7 = (bf16[80,2048]{1,0:T(8,128)(2,1)S(1)}, bf16[80,2048]{1,0:T(8,128)(2,1)S(1)}, u32[]{:S(2)}, u32[]{:S(2)}) collective-permute-start(bf16[80,2048]{1,0:T(8,128)(2,1)S(1)} %get-tuple-element.14), channel_id=1, source_target_pairs={{0,1},{1,0},{2,3},{3,2},{4,5},{5,4},{6,7},{7,6},{8,10},{9,11},{10,... | collective-permute-start | bytes 983048 | tf_op jit(solution)/shard_map/ppermute | solution.py:34
  39.4 40.9 %collective-permute-start.8 = (bf16[80,2048]{1,0:T(8,128)(2,1)S(1)}, bf16[80,2048]{1,0:T(8,128)(2,1)S(1)}, u32[]{:S(2)}, u32[]{:S(2)}) collective-permute-start(bf16[80,2048]{1,0:T(8,128)(2,1)S(1)} %get-tuple-element.15), channel_id=1, source_target_pairs={{0,1},{1,0},{2,3},{3,2},{4,5},{5,4},{6,7},{7,6},{8,12},{9,13},{10,... | collective-permute-start | bytes 983048 | tf_op jit(solution)/shard_map/ppermute | solution.py:34
  40.4 39.9 %collective-permute-start.9 = (bf16[80,2048]{1,0:T(8,128)(2,1)S(1)}, bf16[80,2048]{1,0:T(8,128)(2,1)S(1)}, u32[]{:S(2)}, u32[]{:S(2)}) collective-permute-start(bf16[80,2048]{1,0:T(8,128)(2,1)S(1)} %get-tuple-element.16), channel_id=1, source_target_pairs={{0,1},{1,0},{2,3},{3,2},{4,5},{5,4},{6,7},{7,6},{8,14},{9,15},{10,... | collective-permute-start | bytes 983048 | tf_op jit(solution)/shard_map/ppermute | solution.py:34
  41.8 49.2 %collective-permute-start.18 = (bf16[64,2560]{1,0:T(8,128)(2,1)S(1)}, bf16[64,2560]{1,0:T(8,128)(2,1)S(1)}, u32[]{:S(2)}, u32[]{:S(2)}) collective-permute-start(bf16[64,2560]{1,0:T(8,128)(2,1)S(1)} %stack_rows.2.rest_4_), channel_id=1, source_target_pairs={{0,4},{1,5},{2,6},{3,7},{4,0},{5,1},{6,2},{7,3}} | collective-permute-start | bytes 983048 | tf_op jit(solution)/shard_map/ppermute | solution.py:46
  42.9 42.2 %collective-permute-start.12 = (bf16[48,2048]{1,0:T(8,128)(2,1)S(1)}, bf16[48,2048]{1,0:T(8,128)(2,1)S(1)}, u32[]{:S(2)}, u32[]{:S(2)}) collective-permute-start(bf16[48,2048]{1,0:T(8,128)(2,1)S(1)} %get-tuple-element.19), channel_id=1, source_target_pairs={{0,1},{1,0},{2,3},{3,2},{4,5},{5,4},{6,7},{7,6},{8,10},{9,11},{10,... | collective-permute-start | bytes 589832 | tf_op jit(solution)/shard_map/ppermute | solution.py:34
  50.0 35.2 %collective-permute-start.14 = (bf16[48,2048]{1,0:T(8,128)(2,1)S(1)}, bf16[48,2048]{1,0:T(8,128)(2,1)S(1)}, u32[]{:S(2)}, u32[]{:S(2)}) collective-permute-start(bf16[48,2048]{1,0:T(8,128)(2,1)S(1)} %get-tuple-element.21), channel_id=1, source_target_pairs={{0,1},{1,0},{2,3},{3,2},{4,5},{5,4},{6,7},{7,6},{8,14},{9,15},{10,... | collective-permute-start | bytes 589832 | tf_op jit(solution)/shard_map/ppermute | solution.py:34
  80.3 11.4 %collective-permute-start.13 = (bf16[48,2048]{1,0:T(8,128)(2,1)S(1)}, bf16[48,2048]{1,0:T(8,128)(2,1)S(1)}, u32[]{:S(2)}, u32[]{:S(2)}) collective-permute-start(bf16[48,2048]{1,0:T(8,128)(2,1)S(1)} %get-tuple-element.20), channel_id=1, source_target_pairs={{0,1},{1,0},{2,3},{3,2},{4,5},{5,4},{6,7},{7,6},{8,12},{9,13},{10,... | collective-permute-start | bytes 589832 | tf_op jit(solution)/shard_map/ppermute | solution.py:34
  82.9 57.1 %collective-permute-start.11 = (bf16[80,8192]{1,0:T(8,128)(2,1)S(1)}, bf16[80,8192]{1,0:T(8,128)(2,1)S(1)}, u32[]{:S(2)}, u32[]{:S(2)}) collective-permute-start(bf16[80,8192]{1,0:T(8,128)(2,1)S(1)} %norm_backward.2.rest_0_), channel_id=1, source_target_pairs={{8,0},{16,8},{24,16},{9,1},{17,9},{25,17},{10,2},{18,10},{26,18},{... | collective-permute-start | bytes 3932168 | tf_op jit(solution)/shard_map/ppermute | solution.py:25
  87.0 41.8 %collective-permute-start.17 = (bf16[112,2560]{1,0:T(8,128)(2,1)S(1)}, bf16[112,2560]{1,0:T(8,128)(2,1)S(1)}, u32[]{:S(2)}, u32[]{:S(2)}) collective-permute-start(bf16[112,2560]{1,0:T(8,128)(2,1)S(1)} %norm_forward.6.rest_0_), channel_id=1, source_target_pairs={{0,4},{1,5},{2,6},{3,7},{4,0},{5,1},{6,2},{7,3},{8,12},{9,13},{10,... | collective-permute-start | bytes 1720328 | tf_op jit(solution)/shard_map/ppermute | solution.py:34
  90.9 37.9 %collective-permute-start.16 = (bf16[128,2560]{1,0:T(8,128)(2,1)S(1)}, bf16[128,2560]{1,0:T(8,128)(2,1)S(1)}, u32[]{:S(2)}, u32[]{:S(2)}) collective-permute-start(bf16[128,2560]{1,0:T(8,128)(2,1)S(1)} %norm_forward.7.rest_4_), channel_id=1, source_target_pairs={{0,6},{1,7},{2,0},{3,1},{4,2},{5,3},{6,4},{7,5},{8,14},{9,15},{10,... | collective-permute-start | bytes 1966088 | tf_op jit(solution)/shard_map/ppermute | solution.py:34
  91.0 3.1 %collective-permute-start.19 = (bf16[16,2560]{1,0:T(8,128)(2,1)S(1)}, bf16[16,2560]{1,0:T(8,128)(2,1)S(1)}, u32[]{:S(2)}, u32[]{:S(2)}) collective-permute-start(bf16[16,2560]{1,0:T(8,128)(2,1)S(1)} %get-tuple-element.24), channel_id=1, source_target_pairs={{0,8},{1,9},{2,10},{3,11},{4,12},{5,13},{6,14},{7,15}} | collective-permute-start | bytes 245768 | tf_op jit(solution)/shard_map/ppermute | solution.py:40
  91.7 6.1 %collective-permute-start.20 = (bf16[16,2560]{1,0:T(8,128)(2,1)S(1)}, bf16[16,2560]{1,0:T(8,128)(2,1)S(1)}, u32[]{:S(2)}, u32[]{:S(2)}) collective-permute-start(bf16[16,2560]{1,0:T(8,128)(2,1)S(1)} %get-tuple-element.23), channel_id=1, source_target_pairs={{0,16},{1,17},{2,18},{3,19},{4,20},{5,21},{6,22},{7,23}} | collective-permute-start | bytes 245768 | tf_op jit(solution)/shard_map/ppermute | solution.py:40
  94.2 45.8 %collective-permute-start.15 = (bf16[48,8192]{1,0:T(8,128)(2,1)S(1)}, bf16[48,8192]{1,0:T(8,128)(2,1)S(1)}, u32[]{:S(2)}, u32[]{:S(2)}) collective-permute-start(bf16[48,8192]{1,0:T(8,128)(2,1)S(1)} %norm_backward.3.refs_12_), channel_id=1, source_target_pairs={{8,0},{16,8},{24,16},{9,1},{17,9},{25,17},{10,2},{18,10},{26,18},{... | collective-permute-start | bytes 2359304 | tf_op jit(solution)/shard_map/ppermute | solution.py:25
  97.8 6.4 %collective-permute-start.21 = (bf16[16,2560]{1,0:T(8,128)(2,1)S(1)}, bf16[16,2560]{1,0:T(8,128)(2,1)S(1)}, u32[]{:S(2)}, u32[]{:S(2)}) collective-permute-start(bf16[16,2560]{1,0:T(8,128)(2,1)S(1)} %get-tuple-element.22), channel_id=1, source_target_pairs={{0,24},{1,25},{2,26},{3,27},{4,28},{5,29},{6,30},{7,31}} | collective-permute-start | bytes 245768 | tf_op jit(solution)/shard_map/ppermute | solution.py:40
  129.6 6.6 %collective-permute-start.23 = (bf16[512,512]{1,0:T(8,128)(2,1)S(1)}, bf16[512,512]{1,0:T(8,128)(2,1)S(1)}, u32[]{:S(2)}, u32[]{:S(2)}) collective-permute-start(bf16[512,512]{1,0:T(8,128)(2,1)S(1)} %outer.8), channel_id=1, source_target_pairs={{0,1},{1,0},{2,3},{3,2},{4,5},{5,4},{6,7},{7,6},{8,9},{9,8},{10,11... | collective-permute-start | bytes 1572872 | tf_op jit(solution)/shard_map/ppermute | solution.py:51
  135.4 2.0 %collective-permute-start.22 = (bf16[512,512]{1,0:T(8,128)(2,1)S(1)}, bf16[512,512]{1,0:T(8,128)(2,1)S(1)}, u32[]{:S(2)}, u32[]{:S(2)}) collective-permute-start(bf16[512,512]{1,0:T(8,128)(2,1)S(1)} %outer.7), channel_id=1, source_target_pairs={{0,1},{1,0},{2,3},{3,2},{4,5},{5,4},{6,7},{7,6},{8,9},{9,8},{10,11... | collective-permute-start | bytes 1572872 | tf_op jit(solution)/shard_map/ppermute | solution.py:51

commit v4 on v2

--- a/solution.py
+++ b/solution.py
@@ -121,6 +121,31 @@
         out_specs=pl.BlockSpec((tall, width), lambda i: (0, 0)),
         out_shape=jax.ShapeDtypeStruct((tall, width), arrays[0].dtype),
     )(*arrays, *after)
+
+
+def join_kernel(count, *refs):
+    out_ref, semaphores = refs[-2], refs[-1]
+    at, copies = 0, []
+    for index, ref in enumerate(refs[:count]):
+        tall = ref.shape[0]
+        copies.append(pltpu.make_async_copy(ref, out_ref.at[at:at + tall], semaphores.at[index]))
+        at += tall
+    for copy in copies:
+        copy.start()
+    for copy in copies:
+        copy.wait()
+
+
+def join_rows(arrays):
+    width = arrays[0].shape[1]
+    tall = sum(array.shape[0] for array in arrays)
+    return call(
+        functools.partial(join_kernel, len(arrays)), "join_rows", 0, 4 * tall * width,
+        in_specs=[whole] * len(arrays),
+        out_specs=pl.BlockSpec(memory_space=pltpu.HBM),
+        out_shape=jax.ShapeDtypeStruct((tall, width), arrays[0].dtype),
+        scratch_shapes=[pltpu.SemaphoreType.DMA((len(arrays),))],
+    )(*arrays)
 
 
 def attend_kernel(query_ref, key_ref, grad_ref, row_seg_ref, col_seg_ref, out_ref):
@@ -362,7 +387,7 @@
     late = apply(near[1:], 0, tokens, kept)
     above = [above, backward(arrived[1], start=cuts[1], after=late[:1])]
     below = [from_behind(half, "pipe", -1) for half in above]
-    cot_below = stack_rows(below, [])
+    cot_below = join_rows(below)
 
     groups = [[column] for column in columns] + [returned]
     last = [[along_chips(block, by)] for block, by in zip(late + kept, near[1:] + [middle])]

time: 139 us -> 138 us (level)
    pallas_call x2 -> x1, Pallas kernels: 1.5 us -> 0.05 us  [stack_rows(): call(functools.partial(stack_kernel, len(arrays)), 'stack_rows', 0, 4 * t...]
where the time goes in v4:
time: 138 us; the launch traced here: 137 us
  waiting for transfers between devices  70.2 us (51%)
  starting transfers between devices  32.2 us (23%)
  Pallas kernels  28.3 us (21%)
  local copies, waits for them, and re-layouts  4.85 us (4%)
    ppermute x12, waiting for transfers between devices, along_chips(): return lax.ppermute(array, ('pipe', 'dp'), pairs)  67.3 us
    ppermute x12, starting transfers between devices, along_chips(): return lax.ppermute(array, ('pipe', 'dp'), pairs)  17.2 us
    ppermute x2, starting transfers between devices, from_behind(): return lax.ppermute(array, axis, pairs)  8.05 us
    pallas_call x5, Pallas kernels, outer(): call(functools.partial(outer_kernel, [len(group) for group in groups], le...  7.79 us
    ppermute x6, starting transfers between devices, between_lines(): return lax.ppermute(array, ('pipe', 'dp'), pairs)  5.4 us
    pallas_call x1, Pallas kernels, project(): call(functools.partial(project_kernel, chips, steps, cuts), 'project', 4...  5.38 us
    pallas_call x4, Pallas kernels, normalize(): call(functools.partial(norm_kernel, chips, ahead), 'norm_forward', 4 * co...  5.06 us
    pallas_call x1, Pallas kernels, attend(): call(attend_kernel, 'attend', 4 * tokens * tokens * queries.shape[1], 4 *...  4.48 us
  transfers between devices with their start and end apart: 24, of which 9 were waited for; matrix products, arithmetic and copies ran while one was open for 1% of the time, Pallas kernels for 20%

profile of v4, /device:TPU:10, one launch (start us, length us, event | category | flops | bytes accessed | tf_op | source)
XLA Modules:
  0.0 136.6 jit_solution(10563333762371294018)
XLA Ops:
  0.7 0.5 collective-permute-start.1
  1.2 2.6 %collective-permute-start.2 = (bf16[128,1024]{1,0:T(8,128)(2,1)}, bf16[128,1024]{1,0:T(8,128)(2,1)S(1)}, u32[]{:S(2)}, u32[]{:S(2)}) collective-permute-start(bf16[128,1024]{1,0:T(8,128)(2,1)} %bitcast.28), channel_id=1, source_target_pairs={{0,1},{1,0},{2,3},{3,2},{4,5},{5,4},{6,7},{7,6},{8,12},{9,13},{10,... | collective-permute-start | bytes 786440 | tf_op jit(solution)/shard_map/ppermute | solution.py:34
  3.8 2.5 %collective-permute-start.3 = (bf16[128,1024]{1,0:T(8,128)(2,1)}, bf16[128,1024]{1,0:T(8,128)(2,1)S(1)}, u32[]{:S(2)}, u32[]{:S(2)}) collective-permute-start(bf16[128,1024]{1,0:T(8,128)(2,1)} %bitcast.29), channel_id=1, source_target_pairs={{0,1},{1,0},{2,3},{3,2},{4,5},{5,4},{6,7},{7,6},{8,10},{9,11},{10,... | collective-permute-start | bytes 786440 | tf_op jit(solution)/shard_map/ppermute | solution.py:34
  6.3 0.8 copy.13.col_seg_ref
  7.1 1.2 copy-done.3
  8.3 1.2 copy-done.4
  9.5 0.9 copy-done.7
  10.4 0.7 copy-done.8
  11.1 4.5 %attend.1.cot_ref = bf16[128,512]{1,0:T(8,128)(2,1)S(1)} custom-call(bf16[128,4096]{1,0:T(8,128)(2,1)S(1)} %bitcast.21, bf16[128,512]{1,0:T(8,128)(2,1)S(1)} %bitcast.23, bf16[128,4096]{1,0:T(8,128)(2,1)S(1)} %bitcast.22, s32[1,128]{1,0:T(1,128)S(1)} %copy-done.8, s32[128,1]{1,0:T(8,128)S(1)} %copy.13.col_seg_ref), custom_call_target="tpu_custom_call" | custom-call | flops 268435456 | bytes 2097152 | tf_op jit(solution)/shard_map/attend/pallas_call | solution.py:180
  15.6 0.8 norm_forward.4.refs_0_
  16.4 1.4 %collective-permute-start.4 = (bf16[32,2560]{1,0:T(8,128)(2,1)S(1)}, bf16[32,2560]{1,0:T(8,128)(2,1)S(1)}, u32[]{:S(2)}, u32[]{:S(2)}) collective-permute-start(bf16[32,2560]{1,0:T(8,128)(2,1)S(1)} %norm_forward.4.refs_0_), channel_id=1, source_target_pairs={{8,0},{9,1},{10,2},{11,3},{12,4},{13,5},{14,6},{15,7}} | collective-permute-start | bytes 491528 | tf_op jit(solution)/shard_map/ppermute | solution.py:40
  17.9 0.7 collective-permute-start.5
  18.6 0.7 collective-permute-start.6
  19.2 2.8 %collective-permute-done.2.rest_1_.rest_2_ = bf16[128,1024]{1,0:T(8,128)(2,1)S(1)} collective-permute-done((bf16[128,1024]{1,0:T(8,128)(2,1)}, bf16[128,1024]{1,0:T(8,128)(2,1)S(1)}, u32[]{:S(2)}, u32[]{:S(2)}) %collective-permute-start.2) | collective-permute-done | bytes 262176 | tf_op jit(solution)/shard_map/ppermute | solution.py:34
  22.1 4.8 %collective-permute-done.3.rest_2_.rest_3_ = bf16[128,1024]{1,0:T(8,128)(2,1)S(1)} collective-permute-done((bf16[128,1024]{1,0:T(8,128)(2,1)}, bf16[128,1024]{1,0:T(8,128)(2,1)S(1)}, u32[]{:S(2)}, u32[]{:S(2)}) %collective-permute-start.3) | collective-permute-done | bytes 262176 | tf_op jit(solution)/shard_map/ppermute | solution.py:34
  26.9 1.5 %norm_forward.5 = (bf16[128,2560]{1,0:T(8,128)(2,1)S(1)}, bf16[128,2560]{1,0:T(8,128)(2,1)S(1)}) custom-call(s32[2]{0:T(128)S(1)} %pad_add_fusion.place_ref, bf16[128,8192]{1,0:T(8,128)(2,1)S(1)} %bitcast.14, bf16[1,8192]{1,0:T(2,128)(2,1)S(1)} %copy-done.5, bf16[128,512]{1,0:T(8,128)(2,1)S(1)} %attend.1.cot_ref, ...), custom_call_target="tpu_custom_call" | custom-call | flops 4194304 | bytes 3407872 | tf_op jit(solution)/shard_map/norm_forward/pallas_call | solution.py:92
  28.5 2.4 %collective-permute-start.10 = (bf16[128,2560]{1,0:T(8,128)(2,1)S(1)}, bf16[128,2560]{1,0:T(8,128)(2,1)S(1)}, u32[]{:S(2)}, u32[]{:S(2)}) collective-permute-start(bf16[128,2560]{1,0:T(8,128)(2,1)S(1)} %get-tuple-element.17), channel_id=1, source_target_pairs={{0,2},{1,3},{2,4},{3,5},{4,6},{5,7},{6,0},{7,1},{8,10},{9,11},{10,... | collective-permute-start | bytes 1966088 | tf_op jit(solution)/shard_map/ppermute | solution.py:34
  31.0 0.8 collective-permute-start.18
  31.9 5.4 %project.1 = (bf16[80,2048]{1,0:T(8,128)(2,1)S(1)}, bf16[80,2048]{1,0:T(8,128)(2,1)S(1)}, bf16[80,2048]{1,0:T(8,128)(2,1)S(1)}, bf16[80,2048]{1,0:T(8,128)(2,1)S...) custom-call(bf16[1024,1024]{1,0:T(8,128)(2,1)S(1)} %bitcast.26, ...), custom_call_target="tpu_custom_call" | custom-call | flops 2147483648 | bytes 7340032 | tf_op jit(solution)/shard_map/project/pallas_call | solution.py:231
  37.2 0.1 collective-permute-start.7
  37.3 2.0 %collective-permute-start.8 = (bf16[80,2048]{1,0:T(8,128)(2,1)S(1)}, bf16[80,2048]{1,0:T(8,128)(2,1)S(1)}, u32[]{:S(2)}, u32[]{:S(2)}) collective-permute-start(bf16[80,2048]{1,0:T(8,128)(2,1)S(1)} %get-tuple-element.15), channel_id=1, source_target_pairs={{0,1},{1,0},{2,3},{3,2},{4,5},{5,4},{6,7},{7,6},{8,12},{9,13},{10,... | collective-permute-start | bytes 983048 | tf_op jit(solution)/shard_map/ppermute | solution.py:34
  39.3 1.0 collective-permute-start.9
  40.4 5.8 %collective-permute-done.10.rest_4_.refs_1_.refs_7_ = bf16[128,2560]{1,0:T(8,128)(2,1)S(1)} collective-permute-done((bf16[128,2560]{1,0:T(8,128)(2,1)S(1)}, bf16[128,2560]{1,0:T(8,128)(2,1)S(1)}, u32[]{:S(2)}, u32[]{:S(2)}) %collective-permute-start.10) | collective-permute-done | bytes 655392 | tf_op jit(solution)/shard_map/ppermute | solution.py:34
  46.2 2.4 %collective-permute-start.12 = (bf16[48,2048]{1,0:T(8,128)(2,1)S(1)}, bf16[48,2048]{1,0:T(8,128)(2,1)S(1)}, u32[]{:S(2)}, u32[]{:S(2)}) collective-permute-start(bf16[48,2048]{1,0:T(8,128)(2,1)S(1)} %get-tuple-element.19), channel_id=1, source_target_pairs={{0,1},{1,0},{2,3},{3,2},{4,5},{5,4},{6,7},{7,6},{8,10},{9,11},{10,... | collective-permute-start | bytes 589832 | tf_op jit(solution)/shard_map/ppermute | solution.py:34
  48.6 18.6 %collective-permute-done.7.rest_1_ = bf16[80,2048]{1,0:T(8,128)(2,1)S(1)} collective-permute-done((bf16[80,2048]{1,0:T(8,128)(2,1)S(1)}, bf16[80,2048]{1,0:T(8,128)(2,1)S(1)}, u32[]{:S(2)}, u32[]{:S(2)}) %collective-permute-start.7) | collective-permute-done | bytes 327712 | tf_op jit(solution)/shard_map/ppermute | solution.py:34
  67.2 15.4 %collective-permute-done.8.rest_2_ = bf16[80,2048]{1,0:T(8,128)(2,1)S(1)} collective-permute-done((bf16[80,2048]{1,0:T(8,128)(2,1)S(1)}, bf16[80,2048]{1,0:T(8,128)(2,1)S(1)}, u32[]{:S(2)}, u32[]{:S(2)}) %collective-permute-start.8) | collective-permute-done | bytes 327712 | tf_op jit(solution)/shard_map/ppermute | solution.py:34
  82.6 3.4 %collective-permute-start.13 = (bf16[48,2048]{1,0:T(8,128)(2,1)S(1)}, bf16[48,2048]{1,0:T(8,128)(2,1)S(1)}, u32[]{:S(2)}, u32[]{:S(2)}) collective-permute-start(bf16[48,2048]{1,0:T(8,128)(2,1)S(1)} %get-tuple-element.20), channel_id=1, source_target_pairs={{0,1},{1,0},{2,3},{3,2},{4,5},{5,4},{6,7},{7,6},{8,12},{9,13},{10,... | collective-permute-start | bytes 589832 | tf_op jit(solution)/shard_map/ppermute | solution.py:34
  86.0 2.5 %norm_backward.2.rest_0_ = bf16[80,8192]{1,0:T(8,128)(2,1)S(1)} custom-call(s32[2]{0:T(128)S(1)} %pad_add_fusion.place_ref, bf16[128,8192]{1,0:T(8,128)(2,1)S(1)} %bitcast.17, bf16[1,8192]{1,0:T(2,128)(2,1)S(1)} %copy-done.6, bf16[128,8192]{1,0:T(8,128)(2,1)S(1)} %bitcast.19, bf16[80,2048]{1,0:T(8,128)(2,1)S(1)} %get-tuple-element.13.rest_0_, ...), custom_call_target="tpu_custom_call" | custom-call | flops 6553600 | bytes 5242880 | tf_op jit(solution)/shard_map/norm_backward/pallas_call | solution.py:278
  88.5 1.9 %collective-permute-start.11 = (bf16[80,8192]{1,0:T(8,128)(2,1)S(1)}, bf16[80,8192]{1,0:T(8,128)(2,1)S(1)}, u32[]{:S(2)}, u32[]{:S(2)}) collective-permute-start(bf16[80,8192]{1,0:T(8,128)(2,1)S(1)} %norm_backward.2.rest_0_), channel_id=1, source_target_pairs={{8,0},{16,8},{24,16},{9,1},{17,9},{25,17},{10,2},{18,10},{26,18},{... | collective-permute-start | bytes 3932168 | tf_op jit(solution)/shard_map/ppermute | solution.py:25
  90.5 1.3 norm_forward.6.rest_0_
  91.8 1.5 %norm_forward.7.rest_4_ = bf16[128,2560]{1,0:T(8,128)(2,1)S(1)} custom-call(s32[2]{0:T(128)S(1)} %pad_add_fusion.place_ref, bf16[128,8192]{1,0:T(8,128)(2,1)S(1)} %bitcast.16, bf16[1,8192]{1,0:T(2,128)(2,1)S(1)} %copy-done.5, bf16[128,512]{1,0:T(8,128)(2,1)S(1)} %attend.1.cot_ref, bf16[96,2560]{1,0:T(8,128)(2,1)S(1)} %norm_forward.6.rest_0_), custom_call_target="tpu_custom_call" | custom-call | flops 4194304 | bytes 2752512 | tf_op jit(solution)/shard_map/norm_forward/pallas_call | solution.py:92
  93.3 0.3 collective-permute-start.16
  93.7 1.3 collective-permute-start.19
  95.0 19.8 %collective-permute-done.13.rest_2_ = bf16[48,2048]{1,0:T(8,128)(2,1)S(1)} collective-permute-done((bf16[48,2048]{1,0:T(8,128)(2,1)S(1)}, bf16[48,2048]{1,0:T(8,128)(2,1)S(1)}, u32[]{:S(2)}, u32[]{:S(2)}) %collective-permute-start.13) | collective-permute-done | bytes 196640 | tf_op jit(solution)/shard_map/ppermute | solution.py:34
  114.7 0.7 collective-permute-start.20
  115.4 0.7 collective-permute-start.21
  116.1 1.7 %norm_backward.3.refs_12_ = bf16[48,8192]{1,0:T(8,128)(2,1)S(1)} custom-call(s32[2]{0:T(128)S(1)} %pad_add_fusion.place_ref, bf16[128,8192]{1,0:T(8,128)(2,1)S(1)} %bitcast.18, bf16[1,8192]{1,0:T(2,128)(2,1)S(1)} %copy-done.6, bf16[128,8192]{1,0:T(8,128)(2,1)S(1)} %bitcast.20, bf16[48,2048]{1,0:T(8,128)(2,1)S(1)} %get-tuple-element.18.rest_0_, ...), custom_call_target="tpu_custom_call" | custom-call | flops 3932160 | bytes 3145728 | tf_op jit(solution)/shard_map/norm_backward/pallas_call | solution.py:278
  117.8 6.1 %collective-permute-start.15 = (bf16[48,8192]{1,0:T(8,128)(2,1)S(1)}, bf16[48,8192]{1,0:T(8,128)(2,1)S(1)}, u32[]{:S(2)}, u32[]{:S(2)}) collective-permute-start(bf16[48,8192]{1,0:T(8,128)(2,1)S(1)} %norm_backward.3.refs_12_), channel_id=1, source_target_pairs={{8,0},{16,8},{24,16},{9,1},{17,9},{25,17},{10,2},{18,10},{26,18},{... | collective-permute-start | bytes 2359304 | tf_op jit(solution)/shard_map/ppermute | solution.py:25
  124.0 1.8 %outer.6.refs_4_ = f32[1024,512]{1,0:T(8,128)S(1)} custom-call(bf16[128,2560]{1,0:T(8,128)(2,1)S(1)} %get-tuple-element.12.refs_4_.refs_0_.refs_6_, bf16[128,2560]{1,0:T(8,128)(2,1)S(1)} %collective-permute-done.10.rest_4_.refs_1_.refs_7_, bf16[32,2560]{1,0:T(8,128)(2,1)S(1)} %get-tuple-element.25.refs_2_.refs_8_, ...), custom_call_target="tpu_custom_call" | custom-call | flops 402653184 | bytes 2883584 | tf_op jit(solution)/shard_map/outer/pallas_call | solution.py:325
  125.8 1.8 %outer.5.refs_5_.refs_4_ = f32[1024,512]{1,0:T(8,128)S(1)} custom-call(bf16[128,2560]{1,0:T(8,128)(2,1)S(1)} %get-tuple-element.12.refs_4_.refs_0_.refs_6_, bf16[128,2560]{1,0:T(8,128)(2,1)S(1)} %collective-permute-done.10.rest_4_.refs_1_.refs_7_, bf16[32,2560]{1,0:T(8,128)(2,1)S(1)} %get-tuple-element.25.refs_2_.refs_8_, ...), custom_call_target="tpu_custom_call" | custom-call | flops 402653184 | bytes 2883584 | tf_op jit(solution)/shard_map/outer/pallas_call | solution.py:325
  127.7 0.7 outer.8
  128.5 0.7 outer.7
  129.3 0.5 collective-permute-start.22
  129.8 0.6 collective-permute-done.23.refs_6_
  130.4 0.9 collective-permute-done.22.refs_5_
  131.4 2.6 %outer.9 = f32[1024,512]{1,0:T(8,128)} custom-call(bf16[128,2560]{1,0:T(8,128)(2,1)S(1)} %collective-permute-done.16.refs_0_.refs_2_, bf16[96,2560]{1,0:T(8,128)(2,1)S(1)} %collective-permute-done.17.refs_1_.refs_3_, bf16[128,2560]{1,0:T(8,128)(2,1)S(1)} %collective-permute-done.16.refs_0_.refs_2_, ...), custom_call_target="tpu_custom_call" | custom-call | flops 234881024 | bytes 2555904 | tf_op jit(solution)/shard_map/outer/pallas_call | solution.py:325
  134.0 1.3 collective-permute-done.15.refs_1_
  135.3 1.3 join_rows.1
  (40 shorter events, 0.5 us)
Async XLA Ops:
  0.6 15.0 %copy-start = (bf16[1,128,8192]{2,1,0:T(8,128)(2,1)S(1)}, bf16[1,128,8192]{2,1,0:T(8,128)(2,1)}, u32[]{:S(2)}) copy-start(bf16[1,128,8192]{2,1,0:T(8,128)(2,1)} %param.11) | copy-start | bytes 6291460
  0.6 15.0 %collective-permute-start = (bf16[1024,1024]{1,0:T(8,128)(2,1)}, bf16[1024,1024]{1,0:T(8,128)(2,1)}, u32[]{:S(2)}, u32[]{:S(2)}) collective-permute-start(bf16[1024,1024]{1,0:T(8,128)(2,1)} %bitcast.25), channel_id=1, source_target_pairs={{0,1},{1,0},{2,3},{3,2},{4,5},{5,4},{6,7},{7,6},{8,9},{9,8},{10,11... | collective-permute-start | bytes 6291464 | tf_op jit(solution)/shard_map/ppermute | solution.py:51
  0.7 17.8 %collective-permute-start.1 = (bf16[128,1024]{1,0:T(8,128)(2,1)}, bf16[128,1024]{1,0:T(8,128)(2,1)S(1)}, u32[]{:S(2)}, u32[]{:S(2)}) collective-permute-start(bf16[128,1024]{1,0:T(8,128)(2,1)} %bitcast.27), channel_id=1, source_target_pairs={{0,1},{1,0},{2,3},{3,2},{4,5},{5,4},{6,7},{7,6},{8,14},{9,15},{10,... | collective-permute-start | bytes 786440 | tf_op jit(solution)/shard_map/ppermute | solution.py:34
  1.2 20.8 %collective-permute-start.2 = (bf16[128,1024]{1,0:T(8,128)(2,1)}, bf16[128,1024]{1,0:T(8,128)(2,1)S(1)}, u32[]{:S(2)}, u32[]{:S(2)}) collective-permute-start(bf16[128,1024]{1,0:T(8,128)(2,1)} %bitcast.28), channel_id=1, source_target_pairs={{0,1},{1,0},{2,3},{3,2},{4,5},{5,4},{6,7},{7,6},{8,12},{9,13},{10,... | collective-permute-start | bytes 786440 | tf_op jit(solution)/shard_map/ppermute | solution.py:34
  3.8 23.1 %collective-permute-start.3 = (bf16[128,1024]{1,0:T(8,128)(2,1)}, bf16[128,1024]{1,0:T(8,128)(2,1)S(1)}, u32[]{:S(2)}, u32[]{:S(2)}) collective-permute-start(bf16[128,1024]{1,0:T(8,128)(2,1)} %bitcast.29), channel_id=1, source_target_pairs={{0,1},{1,0},{2,3},{3,2},{4,5},{5,4},{6,7},{7,6},{8,10},{9,11},{10,... | collective-permute-start | bytes 786440 | tf_op jit(solution)/shard_map/ppermute | solution.py:34
  7.1 1.2 copy-start.3
  8.3 1.2 copy-start.4
  9.5 0.9 copy-start.7
  10.4 0.7 copy-start.8
  11.1 4.6 %copy-start.5 = (bf16[1,8192]{1,0:T(2,128)(2,1)S(1)}, bf16[1,8192]{1,0:T(2,128)(2,1)}, u32[]{:S(2)}) copy-start(bf16[1,8192]{1,0:T(2,128)(2,1)} %gain_ref.10) | copy-start | bytes 49156
  16.4 15.4 %copy-start.9 = (bf16[1,1024,1024]{2,1,0:T(8,128)(2,1)S(1)}, bf16[1,1024,1024]{2,1,0:T(8,128)(2,1)}, u32[]{:S(2)}) copy-start(bf16[1,1024,1024]{2,1,0:T(8,128)(2,1)} %param.21) | copy-start | bytes 6291460
  16.4 15.4 %copy-start.10 = (bf16[1,128,1024]{2,1,0:T(8,128)(2,1)S(1)}, bf16[1,128,1024]{2,1,0:T(8,128)(2,1)}, u32[]{:S(2)}) copy-start(bf16[1,128,1024]{2,1,0:T(8,128)(2,1)} %param.20) | copy-start | bytes 786436
  16.4 14.5 %collective-permute-start.4 = (bf16[32,2560]{1,0:T(8,128)(2,1)S(1)}, bf16[32,2560]{1,0:T(8,128)(2,1)S(1)}, u32[]{:S(2)}, u32[]{:S(2)}) collective-permute-start(bf16[32,2560]{1,0:T(8,128)(2,1)S(1)} %norm_forward.4.refs_0_), channel_id=1, source_target_pairs={{8,0},{9,1},{10,2},{11,3},{12,4},{13,5},{14,6},{15,7}} | collective-permute-start | bytes 491528 | tf_op jit(solution)/shard_map/ppermute | solution.py:40
  17.9 13.0 %collective-permute-start.5 = (bf16[32,2560]{1,0:T(8,128)(2,1)S(1)}, bf16[32,2560]{1,0:T(8,128)(2,1)S(1)}, u32[]{:S(2)}, u32[]{:S(2)}) collective-permute-start(bf16[32,2560]{1,0:T(8,128)(2,1)S(1)} %norm_forward.4.refs_0_), channel_id=1, source_target_pairs={{16,0},{17,1},{18,2},{19,3},{20,4},{21,5},{22,6},{23,7}} | collective-permute-start | bytes 491528 | tf_op jit(solution)/shard_map/ppermute | solution.py:40
  18.6 12.3 %collective-permute-start.6 = (bf16[32,2560]{1,0:T(8,128)(2,1)S(1)}, bf16[32,2560]{1,0:T(8,128)(2,1)S(1)}, u32[]{:S(2)}, u32[]{:S(2)}) collective-permute-start(bf16[32,2560]{1,0:T(8,128)(2,1)S(1)} %norm_forward.4.refs_0_), channel_id=1, source_target_pairs={{24,0},{25,1},{26,2},{27,3},{28,4},{29,5},{30,6},{31,7}} | collective-permute-start | bytes 491528 | tf_op jit(solution)/shard_map/ppermute | solution.py:40
  28.5 17.7 %collective-permute-start.10 = (bf16[128,2560]{1,0:T(8,128)(2,1)S(1)}, bf16[128,2560]{1,0:T(8,128)(2,1)S(1)}, u32[]{:S(2)}, u32[]{:S(2)}) collective-permute-start(bf16[128,2560]{1,0:T(8,128)(2,1)S(1)} %get-tuple-element.17), channel_id=1, source_target_pairs={{0,2},{1,3},{2,4},{3,5},{4,6},{5,7},{6,0},{7,1},{8,10},{9,11},{10,... | collective-permute-start | bytes 1966088 | tf_op jit(solution)/shard_map/ppermute | solution.py:34
  31.0 55.0 %copy-start.1 = (bf16[1,128,8192]{2,1,0:T(8,128)(2,1)S(1)}, bf16[1,128,8192]{2,1,0:T(8,128)(2,1)}, u32[]{:S(2)}) copy-start(bf16[1,128,8192]{2,1,0:T(8,128)(2,1)} %param.17) | copy-start | bytes 6291460
  31.0 55.0 %copy-start.2 = (bf16[1,128,8192]{2,1,0:T(8,128)(2,1)S(1)}, bf16[1,128,8192]{2,1,0:T(8,128)(2,1)}, u32[]{:S(2)}) copy-start(bf16[1,128,8192]{2,1,0:T(8,128)(2,1)} %param.19) | copy-start | bytes 6291460
  31.0 55.0 %copy-start.6 = (bf16[1,8192]{1,0:T(2,128)(2,1)S(1)}, bf16[1,8192]{1,0:T(2,128)(2,1)}, u32[]{:S(2)}) copy-start(bf16[1,8192]{1,0:T(2,128)(2,1)} %gain_ref.11) | copy-start | bytes 49156
  31.0 62.6 %collective-permute-start.18 = (bf16[128,2560]{1,0:T(8,128)(2,1)S(1)}, bf16[128,2560]{1,0:T(8,128)(2,1)S(1)}, u32[]{:S(2)}, u32[]{:S(2)}) collective-permute-start(bf16[128,2560]{1,0:T(8,128)(2,1)S(1)} %stack_rows.1.rest_4_), channel_id=1, source_target_pairs={{0,4},{1,5},{2,6},{3,7},{4,0},{5,1},{6,2},{7,3}} | collective-permute-start | bytes 1966088 | tf_op jit(solution)/shard_map/ppermute | solution.py:46
  37.2 29.9 %collective-permute-start.7 = (bf16[80,2048]{1,0:T(8,128)(2,1)S(1)}, bf16[80,2048]{1,0:T(8,128)(2,1)S(1)}, u32[]{:S(2)}, u32[]{:S(2)}) collective-permute-start(bf16[80,2048]{1,0:T(8,128)(2,1)S(1)} %get-tuple-element.14), channel_id=1, source_target_pairs={{0,1},{1,0},{2,3},{3,2},{4,5},{5,4},{6,7},{7,6},{8,10},{9,11},{10,... | collective-permute-start | bytes 983048 | tf_op jit(solution)/shard_map/ppermute | solution.py:34
  37.3 45.3 %collective-permute-start.8 = (bf16[80,2048]{1,0:T(8,128)(2,1)S(1)}, bf16[80,2048]{1,0:T(8,128)(2,1)S(1)}, u32[]{:S(2)}, u32[]{:S(2)}) collective-permute-start(bf16[80,2048]{1,0:T(8,128)(2,1)S(1)} %get-tuple-element.15), channel_id=1, source_target_pairs={{0,1},{1,0},{2,3},{3,2},{4,5},{5,4},{6,7},{7,6},{8,12},{9,13},{10,... | collective-permute-start | bytes 983048 | tf_op jit(solution)/shard_map/ppermute | solution.py:34
  39.3 46.7 %collective-permute-start.9 = (bf16[80,2048]{1,0:T(8,128)(2,1)S(1)}, bf16[80,2048]{1,0:T(8,128)(2,1)S(1)}, u32[]{:S(2)}, u32[]{:S(2)}) collective-permute-start(bf16[80,2048]{1,0:T(8,128)(2,1)S(1)} %get-tuple-element.16), channel_id=1, source_target_pairs={{0,1},{1,0},{2,3},{3,2},{4,5},{5,4},{6,7},{7,6},{8,14},{9,15},{10,... | collective-permute-start | bytes 983048 | tf_op jit(solution)/shard_map/ppermute | solution.py:34
  46.2 44.3 %collective-permute-start.12 = (bf16[48,2048]{1,0:T(8,128)(2,1)S(1)}, bf16[48,2048]{1,0:T(8,128)(2,1)S(1)}, u32[]{:S(2)}, u32[]{:S(2)}) collective-permute-start(bf16[48,2048]{1,0:T(8,128)(2,1)S(1)} %get-tuple-element.19), channel_id=1, source_target_pairs={{0,1},{1,0},{2,3},{3,2},{4,5},{5,4},{6,7},{7,6},{8,10},{9,11},{10,... | collective-permute-start | bytes 589832 | tf_op jit(solution)/shard_map/ppermute | solution.py:34
  67.2 23.3 %collective-permute-start.14 = (bf16[48,2048]{1,0:T(8,128)(2,1)S(1)}, bf16[48,2048]{1,0:T(8,128)(2,1)S(1)}, u32[]{:S(2)}, u32[]{:S(2)}) collective-permute-start(bf16[48,2048]{1,0:T(8,128)(2,1)S(1)} %get-tuple-element.21), channel_id=1, source_target_pairs={{0,1},{1,0},{2,3},{3,2},{4,5},{5,4},{6,7},{7,6},{8,14},{9,15},{10,... | collective-permute-start | bytes 589832 | tf_op jit(solution)/shard_map/ppermute | solution.py:34
  82.6 32.1 %collective-permute-start.13 = (bf16[48,2048]{1,0:T(8,128)(2,1)S(1)}, bf16[48,2048]{1,0:T(8,128)(2,1)S(1)}, u32[]{:S(2)}, u32[]{:S(2)}) collective-permute-start(bf16[48,2048]{1,0:T(8,128)(2,1)S(1)} %get-tuple-element.20), channel_id=1, source_target_pairs={{0,1},{1,0},{2,3},{3,2},{4,5},{5,4},{6,7},{7,6},{8,12},{9,13},{10,... | collective-permute-start | bytes 589832 | tf_op jit(solution)/shard_map/ppermute | solution.py:34
  88.5 46.8 %collective-permute-start.11 = (bf16[80,8192]{1,0:T(8,128)(2,1)S(1)}, bf16[80,8192]{1,0:T(8,128)(2,1)S(1)}, u32[]{:S(2)}, u32[]{:S(2)}) collective-permute-start(bf16[80,8192]{1,0:T(8,128)(2,1)S(1)} %norm_backward.2.rest_0_), channel_id=1, source_target_pairs={{8,0},{16,8},{24,16},{9,1},{17,9},{25,17},{10,2},{18,10},{26,18},{... | collective-permute-start | bytes 3932168 | tf_op jit(solution)/shard_map/ppermute | solution.py:25
  91.8 35.9 %collective-permute-start.17 = (bf16[96,2560]{1,0:T(8,128)(2,1)S(1)}, bf16[96,2560]{1,0:T(8,128)(2,1)S(1)}, u32[]{:S(2)}, u32[]{:S(2)}) collective-permute-start(bf16[96,2560]{1,0:T(8,128)(2,1)S(1)} %norm_forward.6.rest_0_), channel_id=1, source_target_pairs={{0,4},{1,5},{2,6},{3,7},{4,0},{5,1},{6,2},{7,3},{8,12},{9,13},{10,... | collective-permute-start | bytes 1474568 | tf_op jit(solution)/shard_map/ppermute | solution.py:34
  93.3 34.4 %collective-permute-start.16 = (bf16[128,2560]{1,0:T(8,128)(2,1)S(1)}, bf16[128,2560]{1,0:T(8,128)(2,1)S(1)}, u32[]{:S(2)}, u32[]{:S(2)}) collective-permute-start(bf16[128,2560]{1,0:T(8,128)(2,1)S(1)} %norm_forward.7.rest_4_), channel_id=1, source_target_pairs={{0,6},{1,7},{2,0},{3,1},{4,2},{5,3},{6,4},{7,5},{8,14},{9,15},{10,... | collective-permute-start | bytes 1966088 | tf_op jit(solution)/shard_map/ppermute | solution.py:34
  93.7 21.7 %collective-permute-start.19 = (bf16[32,2560]{1,0:T(8,128)(2,1)S(1)}, bf16[32,2560]{1,0:T(8,128)(2,1)S(1)}, u32[]{:S(2)}, u32[]{:S(2)}) collective-permute-start(bf16[32,2560]{1,0:T(8,128)(2,1)S(1)} %get-tuple-element.24), channel_id=1, source_target_pairs={{0,8},{1,9},{2,10},{3,11},{4,12},{5,13},{6,14},{7,15}} | collective-permute-start | bytes 491528 | tf_op jit(solution)/shard_map/ppermute | solution.py:40
  114.7 3.1 %collective-permute-start.20 = (bf16[32,2560]{1,0:T(8,128)(2,1)S(1)}, bf16[32,2560]{1,0:T(8,128)(2,1)S(1)}, u32[]{:S(2)}, u32[]{:S(2)}) collective-permute-start(bf16[32,2560]{1,0:T(8,128)(2,1)S(1)} %get-tuple-element.23), channel_id=1, source_target_pairs={{0,16},{1,17},{2,18},{3,19},{4,20},{5,21},{6,22},{7,23}} | collective-permute-start | bytes 491528 | tf_op jit(solution)/shard_map/ppermute | solution.py:40
  115.4 8.6 %collective-permute-start.21 = (bf16[32,2560]{1,0:T(8,128)(2,1)S(1)}, bf16[32,2560]{1,0:T(8,128)(2,1)S(1)}, u32[]{:S(2)}, u32[]{:S(2)}) collective-permute-start(bf16[32,2560]{1,0:T(8,128)(2,1)S(1)} %get-tuple-element.22), channel_id=1, source_target_pairs={{0,24},{1,25},{2,26},{3,27},{4,28},{5,29},{6,30},{7,31}} | collective-permute-start | bytes 491528 | tf_op jit(solution)/shard_map/ppermute | solution.py:40
  117.8 17.5 %collective-permute-start.15 = (bf16[48,8192]{1,0:T(8,128)(2,1)S(1)}, bf16[48,8192]{1,0:T(8,128)(2,1)S(1)}, u32[]{:S(2)}, u32[]{:S(2)}) collective-permute-start(bf16[48,8192]{1,0:T(8,128)(2,1)S(1)} %norm_backward.3.refs_12_), channel_id=1, source_target_pairs={{8,0},{16,8},{24,16},{9,1},{17,9},{25,17},{10,2},{18,10},{26,18},{... | collective-permute-start | bytes 2359304 | tf_op jit(solution)/shard_map/ppermute | solution.py:25
  128.4 2.0 %collective-permute-start.23 = (bf16[512,512]{1,0:T(8,128)(2,1)S(1)}, bf16[512,512]{1,0:T(8,128)(2,1)S(1)}, u32[]{:S(2)}, u32[]{:S(2)}) collective-permute-start(bf16[512,512]{1,0:T(8,128)(2,1)S(1)} %outer.8), channel_id=1, source_target_pairs={{0,1},{1,0},{2,3},{3,2},{4,5},{5,4},{6,7},{7,6},{8,9},{9,8},{10,11... | collective-permute-start | bytes 1572872 | tf_op jit(solution)/shard_map/ppermute | solution.py:51
  129.3 2.1 %collective-permute-start.22 = (bf16[512,512]{1,0:T(8,128)(2,1)S(1)}, bf16[512,512]{1,0:T(8,128)(2,1)S(1)}, u32[]{:S(2)}, u32[]{:S(2)}) collective-permute-start(bf16[512,512]{1,0:T(8,128)(2,1)S(1)} %outer.7), channel_id=1, source_target_pairs={{0,1},{1,0},{2,3},{3,2},{4,5},{5,4},{6,7},{7,6},{8,9},{9,8},{10,11... | collective-permute-start | bytes 1572872 | tf_op jit(solution)/shard_map/ppermute | solution.py:51

commit v5 on v4

--- a/solution.py
+++ b/solution.py
@@ -383,7 +383,7 @@
     ]
     backward = functools.partial(norm_backward, place, rows=frozen_input[0], gain=frozen_gain, grads=output_grad[0])
     above = backward(arrived[0], start=cuts[0], after=columns[1:])
-    kept = apply([middle], spread, tokens - spread, [above] + [arrived[1][by] for by in near])
+    kept = apply([middle], spread, tokens - spread, [above] + arrived[1][1:])
     late = apply(near[1:], 0, tokens, kept)
     above = [above, backward(arrived[1], start=cuts[1], after=late[:1])]
     below = [from_behind(half, "pipe", -1) for half in above]

time: 138 us -> 137 us (level)
  waiting for transfers between devices: 70.2 us -> 76.7 us
  starting transfers between devices: 32.2 us -> 26.1 us
    ppermute x6, waiting for transfers between devices: 0.02 us -> 5.49 us  [between_lines(): return lax.ppermute(array, ('pipe', 'dp'), pairs)]
    ppermute x2, starting transfers between devices: 8.05 us -> 4 us  [from_behind(): return lax.ppermute(array, axis, pairs)]
    ppermute x12, starting transfers between devices: 17.2 us -> 15.1 us  [along_chips(): return lax.ppermute(array, ('pipe', 'dp'), pairs)]
  transfers between devices with their start and end apart: 24 -> 24, of which waited for: 9 -> 13; matrix products, arithmetic and copies ran while one was open for 1% -> 1% of each run, Pallas kernels for 20% -> 20%
where the time goes in v5:
time: 137 us
  waiting for transfers between devices  76.7 us (56%)
  Pallas kernels  28.3 us (21%)
  starting transfers between devices  26.1 us (19%)
  local copies, waits for them, and re-layouts  4.85 us (4%)
    ppermute x12, waiting for transfers between devices, along_chips(): return lax.ppermute(array, ('pipe', 'dp'), pairs)  68.4 us
    ppermute x12, starting transfers between devices, along_chips(): return lax.ppermute(array, ('pipe', 'dp'), pairs)  15.1 us
    pallas_call x5, Pallas kernels, outer(): call(functools.partial(outer_kernel, [len(group) for group in groups], le...  7.77 us
    ppermute x6, waiting for transfers between devices, between_lines(): return lax.ppermute(array, ('pipe', 'dp'), pairs)  5.49 us
    ppermute x6, starting transfers between devices, between_lines(): return lax.ppermute(array, ('pipe', 'dp'), pairs)  5.4 us
    pallas_call x1, Pallas kernels, project(): call(functools.partial(project_kernel, chips, steps, cuts), 'project', 4...  5.38 us
    pallas_call x4, Pallas kernels, normalize(): call(functools.partial(norm_kernel, chips, ahead), 'norm_forward', 4 * co...  5.03 us
    pallas_call x1, Pallas kernels, attend(): call(attend_kernel, 'attend', 4 * tokens * tokens * queries.shape[1], 4 *...  4.48 us
  transfers between devices with their start and end apart: 24, of which 13 were waited for; matrix products, arithmetic and copies ran while one was open for 1% of the time, Pallas kernels for 20%

profile of v5, /device:TPU:10, one launch (start us, length us, event | category | flops | bytes accessed | tf_op | source)
XLA Modules:
  0.0 137.0 jit_solution(14132835865764036373)
XLA Ops:
  1.2 2.6 %collective-permute-start.2 = (bf16[128,1024]{1,0:T(8,128)(2,1)}, bf16[128,1024]{1,0:T(8,128)(2,1)S(1)}, u32[]{:S(2)}, u32[]{:S(2)}) collective-permute-start(bf16[128,1024]{1,0:T(8,128)(2,1)} %bitcast.28), channel_id=1, source_target_pairs={{0,1},{1,0},{2,3},{3,2},{4,5},{5,4},{6,7},{7,6},{8,12},{9,13},{10,... | collective-permute-start | bytes 786440 | tf_op jit(solution)/shard_map/ppermute | solution.py:34
  3.8 2.5 %collective-permute-start.3 = (bf16[128,1024]{1,0:T(8,128)(2,1)}, bf16[128,1024]{1,0:T(8,128)(2,1)S(1)}, u32[]{:S(2)}, u32[]{:S(2)}) collective-permute-start(bf16[128,1024]{1,0:T(8,128)(2,1)} %bitcast.29), channel_id=1, source_target_pairs={{0,1},{1,0},{2,3},{3,2},{4,5},{5,4},{6,7},{7,6},{8,10},{9,11},{10,... | collective-permute-start | bytes 786440 | tf_op jit(solution)/shard_map/ppermute | solution.py:34
  6.3 0.8 copy.13.col_seg_ref
  7.1 1.2 copy-done.3
  8.3 1.2 copy-done.4
  9.5 0.9 copy-done.7
  10.4 0.7 copy-done.8
  11.1 4.5 %attend.1.cot_ref = bf16[128,512]{1,0:T(8,128)(2,1)S(1)} custom-call(bf16[128,4096]{1,0:T(8,128)(2,1)S(1)} %bitcast.21, bf16[128,512]{1,0:T(8,128)(2,1)S(1)} %bitcast.23, bf16[128,4096]{1,0:T(8,128)(2,1)S(1)} %bitcast.22, s32[1,128]{1,0:T(1,128)S(1)} %copy-done.8, s32[128,1]{1,0:T(8,128)S(1)} %copy.13.col_seg_ref), custom_call_target="tpu_custom_call" | custom-call | flops 268435456 | bytes 2097152 | tf_op jit(solution)/shard_map/attend/pallas_call | solution.py:180
  15.6 0.8 norm_forward.4.refs_0_
  16.4 1.4 %collective-permute-start.4 = (bf16[32,2560]{1,0:T(8,128)(2,1)S(1)}, bf16[32,2560]{1,0:T(8,128)(2,1)S(1)}, u32[]{:S(2)}, u32[]{:S(2)}) collective-permute-start(bf16[32,2560]{1,0:T(8,128)(2,1)S(1)} %norm_forward.4.refs_0_), channel_id=1, source_target_pairs={{8,0},{9,1},{10,2},{11,3},{12,4},{13,5},{14,6},{15,7}} | collective-permute-start | bytes 491528 | tf_op jit(solution)/shard_map/ppermute | solution.py:40
  17.9 0.7 collective-permute-start.5
  18.6 0.7 collective-permute-start.6
  19.2 2.8 %collective-permute-done.2.rest_1_.rest_2_ = bf16[128,1024]{1,0:T(8,128)(2,1)S(1)} collective-permute-done((bf16[128,1024]{1,0:T(8,128)(2,1)}, bf16[128,1024]{1,0:T(8,128)(2,1)S(1)}, u32[]{:S(2)}, u32[]{:S(2)}) %collective-permute-start.2) | collective-permute-done | bytes 262176 | tf_op jit(solution)/shard_map/ppermute | solution.py:34
  22.1 4.8 %collective-permute-done.3.rest_2_.rest_3_ = bf16[128,1024]{1,0:T(8,128)(2,1)S(1)} collective-permute-done((bf16[128,1024]{1,0:T(8,128)(2,1)}, bf16[128,1024]{1,0:T(8,128)(2,1)S(1)}, u32[]{:S(2)}, u32[]{:S(2)}) %collective-permute-start.3) | collective-permute-done | bytes 262176 | tf_op jit(solution)/shard_map/ppermute | solution.py:34
  26.9 1.5 %norm_forward.5 = (bf16[128,2560]{1,0:T(8,128)(2,1)S(1)}, bf16[128,2560]{1,0:T(8,128)(2,1)S(1)}) custom-call(s32[2]{0:T(128)S(1)} %pad_add_fusion.place_ref, bf16[128,8192]{1,0:T(8,128)(2,1)S(1)} %bitcast.14, bf16[1,8192]{1,0:T(2,128)(2,1)S(1)} %copy-done.5, bf16[128,512]{1,0:T(8,128)(2,1)S(1)} %attend.1.cot_ref, ...), custom_call_target="tpu_custom_call" | custom-call | flops 4194304 | bytes 3407872 | tf_op jit(solution)/shard_map/norm_forward/pallas_call | solution.py:92
  28.5 2.4 %collective-permute-start.10 = (bf16[128,2560]{1,0:T(8,128)(2,1)S(1)}, bf16[128,2560]{1,0:T(8,128)(2,1)S(1)}, u32[]{:S(2)}, u32[]{:S(2)}) collective-permute-start(bf16[128,2560]{1,0:T(8,128)(2,1)S(1)} %get-tuple-element.17), channel_id=1, source_target_pairs={{0,2},{1,3},{2,4},{3,5},{4,6},{5,7},{6,0},{7,1},{8,10},{9,11},{10,... | collective-permute-start | bytes 1966088 | tf_op jit(solution)/shard_map/ppermute | solution.py:34
  31.0 0.8 collective-permute-start.18
  31.9 5.4 %project.1 = (bf16[80,2048]{1,0:T(8,128)(2,1)S(1)}, bf16[80,2048]{1,0:T(8,128)(2,1)S(1)}, bf16[80,2048]{1,0:T(8,128)(2,1)S(1)}, bf16[80,2048]{1,0:T(8,128)(2,1)S...) custom-call(bf16[1024,1024]{1,0:T(8,128)(2,1)S(1)} %bitcast.26, ...), custom_call_target="tpu_custom_call" | custom-call | flops 2147483648 | bytes 7340032 | tf_op jit(solution)/shard_map/project/pallas_call | solution.py:231
  37.3 2.0 %collective-permute-start.8 = (bf16[80,2048]{1,0:T(8,128)(2,1)S(1)}, bf16[80,2048]{1,0:T(8,128)(2,1)S(1)}, u32[]{:S(2)}, u32[]{:S(2)}) collective-permute-start(bf16[80,2048]{1,0:T(8,128)(2,1)S(1)} %get-tuple-element.15), channel_id=1, source_target_pairs={{0,1},{1,0},{2,3},{3,2},{4,5},{5,4},{6,7},{7,6},{8,12},{9,13},{10,... | collective-permute-start | bytes 983048 | tf_op jit(solution)/shard_map/ppermute | solution.py:34
  39.3 1.0 collective-permute-start.9
  40.4 5.8 %collective-permute-done.10.rest_4_.refs_1_.refs_7_ = bf16[128,2560]{1,0:T(8,128)(2,1)S(1)} collective-permute-done((bf16[128,2560]{1,0:T(8,128)(2,1)S(1)}, bf16[128,2560]{1,0:T(8,128)(2,1)S(1)}, u32[]{:S(2)}, u32[]{:S(2)}) %collective-permute-start.10) | collective-permute-done | bytes 655392 | tf_op jit(solution)/shard_map/ppermute | solution.py:34
  46.2 2.4 %collective-permute-start.12 = (bf16[48,2048]{1,0:T(8,128)(2,1)S(1)}, bf16[48,2048]{1,0:T(8,128)(2,1)S(1)}, u32[]{:S(2)}, u32[]{:S(2)}) collective-permute-start(bf16[48,2048]{1,0:T(8,128)(2,1)S(1)} %get-tuple-element.19), channel_id=1, source_target_pairs={{0,1},{1,0},{2,3},{3,2},{4,5},{5,4},{6,7},{7,6},{8,10},{9,11},{10,... | collective-permute-start | bytes 589832 | tf_op jit(solution)/shard_map/ppermute | solution.py:34
  48.6 18.6 %collective-permute-done.7.rest_1_ = bf16[80,2048]{1,0:T(8,128)(2,1)S(1)} collective-permute-done((bf16[80,2048]{1,0:T(8,128)(2,1)S(1)}, bf16[80,2048]{1,0:T(8,128)(2,1)S(1)}, u32[]{:S(2)}, u32[]{:S(2)}) %collective-permute-start.7) | collective-permute-done | bytes 327712 | tf_op jit(solution)/shard_map/ppermute | solution.py:34
  67.2 11.2 %collective-permute-done.8.rest_2_ = bf16[80,2048]{1,0:T(8,128)(2,1)S(1)} collective-permute-done((bf16[80,2048]{1,0:T(8,128)(2,1)S(1)}, bf16[80,2048]{1,0:T(8,128)(2,1)S(1)}, u32[]{:S(2)}, u32[]{:S(2)}) %collective-permute-start.8) | collective-permute-done | bytes 327712 | tf_op jit(solution)/shard_map/ppermute | solution.py:34
  78.4 4.4 %collective-permute-done.9.rest_3_ = bf16[80,2048]{1,0:T(8,128)(2,1)S(1)} collective-permute-done((bf16[80,2048]{1,0:T(8,128)(2,1)S(1)}, bf16[80,2048]{1,0:T(8,128)(2,1)S(1)}, u32[]{:S(2)}, u32[]{:S(2)}) %collective-permute-start.9) | collective-permute-done | bytes 327712 | tf_op jit(solution)/shard_map/ppermute | solution.py:34
  82.8 2.5 %norm_backward.2.rest_0_ = bf16[80,8192]{1,0:T(8,128)(2,1)S(1)} custom-call(s32[2]{0:T(128)S(1)} %pad_add_fusion.place_ref, bf16[128,8192]{1,0:T(8,128)(2,1)S(1)} %bitcast.17, bf16[1,8192]{1,0:T(2,128)(2,1)S(1)} %copy-done.6, bf16[128,8192]{1,0:T(8,128)(2,1)S(1)} %bitcast.19, bf16[80,2048]{1,0:T(8,128)(2,1)S(1)} %get-tuple-element.13.rest_0_, ...), custom_call_target="tpu_custom_call" | custom-call | flops 6553600 | bytes 5242880 | tf_op jit(solution)/shard_map/norm_backward/pallas_call | solution.py:278
  85.4 1.9 %collective-permute-start.11 = (bf16[80,8192]{1,0:T(8,128)(2,1)S(1)}, bf16[80,8192]{1,0:T(8,128)(2,1)S(1)}, u32[]{:S(2)}, u32[]{:S(2)}) collective-permute-start(bf16[80,8192]{1,0:T(8,128)(2,1)S(1)} %norm_backward.2.rest_0_), channel_id=1, source_target_pairs={{8,0},{16,8},{24,16},{9,1},{17,9},{25,17},{10,2},{18,10},{26,18},{... | collective-permute-start | bytes 3932168 | tf_op jit(solution)/shard_map/ppermute | solution.py:25
  87.3 2.0 %collective-permute-done.13.rest_2_ = bf16[48,2048]{1,0:T(8,128)(2,1)S(1)} collective-permute-done((bf16[48,2048]{1,0:T(8,128)(2,1)S(1)}, bf16[48,2048]{1,0:T(8,128)(2,1)S(1)}, u32[]{:S(2)}, u32[]{:S(2)}) %collective-permute-start.13) | collective-permute-done | bytes 196640 | tf_op jit(solution)/shard_map/ppermute | solution.py:34
  89.3 1.8 %collective-permute-done.14.rest_3_ = bf16[48,2048]{1,0:T(8,128)(2,1)S(1)} collective-permute-done((bf16[48,2048]{1,0:T(8,128)(2,1)S(1)}, bf16[48,2048]{1,0:T(8,128)(2,1)S(1)}, u32[]{:S(2)}, u32[]{:S(2)}) %collective-permute-start.14) | collective-permute-done | bytes 196640 | tf_op jit(solution)/shard_map/ppermute | solution.py:34
  91.2 1.2 norm_forward.6.rest_0_
  92.4 1.6 %collective-permute-start.17 = (bf16[96,2560]{1,0:T(8,128)(2,1)S(1)}, bf16[96,2560]{1,0:T(8,128)(2,1)S(1)}, u32[]{:S(2)}, u32[]{:S(2)}) collective-permute-start(bf16[96,2560]{1,0:T(8,128)(2,1)S(1)} %norm_forward.6.rest_0_), channel_id=1, source_target_pairs={{0,4},{1,5},{2,6},{3,7},{4,0},{5,1},{6,2},{7,3},{8,12},{9,13},{10,... | collective-permute-start | bytes 1474568 | tf_op jit(solution)/shard_map/ppermute | solution.py:34
  94.0 1.5 %norm_forward.7.rest_4_ = bf16[128,2560]{1,0:T(8,128)(2,1)S(1)} custom-call(s32[2]{0:T(128)S(1)} %pad_add_fusion.place_ref, bf16[128,8192]{1,0:T(8,128)(2,1)S(1)} %bitcast.16, bf16[1,8192]{1,0:T(2,128)(2,1)S(1)} %copy-done.5, bf16[128,512]{1,0:T(8,128)(2,1)S(1)} %attend.1.cot_ref, bf16[96,2560]{1,0:T(8,128)(2,1)S(1)} %norm_forward.6.rest_0_), custom_call_target="tpu_custom_call" | custom-call | flops 4194304 | bytes 2752512 | tf_op jit(solution)/shard_map/norm_forward/pallas_call | solution.py:92
  95.7 1.3 collective-permute-start.19
  97.0 0.7 collective-permute-start.20
  97.6 5.5 %collective-permute-done.19.refs_3_.refs_9_ = bf16[32,2560]{1,0:T(8,128)(2,1)S(1)} collective-permute-done((bf16[32,2560]{1,0:T(8,128)(2,1)S(1)}, bf16[32,2560]{1,0:T(8,128)(2,1)S(1)}, u32[]{:S(2)}, u32[]{:S(2)}) %collective-permute-start.19) | collective-permute-done | bytes 163872 | tf_op jit(solution)/shard_map/ppermute | solution.py:40
  103.1 0.7 collective-permute-start.21
  103.8 1.7 %norm_backward.3.refs_12_ = bf16[48,8192]{1,0:T(8,128)(2,1)S(1)} custom-call(s32[2]{0:T(128)S(1)} %pad_add_fusion.place_ref, bf16[128,8192]{1,0:T(8,128)(2,1)S(1)} %bitcast.18, bf16[1,8192]{1,0:T(2,128)(2,1)S(1)} %copy-done.6, bf16[128,8192]{1,0:T(8,128)(2,1)S(1)} %bitcast.20, bf16[48,2048]{1,0:T(8,128)(2,1)S(1)} %get-tuple-element.18.rest_0_, ...), custom_call_target="tpu_custom_call" | custom-call | flops 3932160 | bytes 3145728 | tf_op jit(solution)/shard_map/norm_backward/pallas_call | solution.py:278
  105.5 2.1 %collective-permute-start.15 = (bf16[48,8192]{1,0:T(8,128)(2,1)S(1)}, bf16[48,8192]{1,0:T(8,128)(2,1)S(1)}, u32[]{:S(2)}, u32[]{:S(2)}) collective-permute-start(bf16[48,8192]{1,0:T(8,128)(2,1)S(1)} %norm_backward.3.refs_12_), channel_id=1, source_target_pairs={{8,0},{16,8},{24,16},{9,1},{17,9},{25,17},{10,2},{18,10},{26,18},{... | collective-permute-start | bytes 2359304 | tf_op jit(solution)/shard_map/ppermute | solution.py:25
  107.6 1.8 %outer.6.refs_4_ = f32[1024,512]{1,0:T(8,128)S(1)} custom-call(bf16[128,2560]{1,0:T(8,128)(2,1)S(1)} %get-tuple-element.12.refs_4_.refs_0_.refs_6_, bf16[128,2560]{1,0:T(8,128)(2,1)S(1)} %collective-permute-done.10.rest_4_.refs_1_.refs_7_, bf16[32,2560]{1,0:T(8,128)(2,1)S(1)} %get-tuple-element.25.refs_2_.refs_8_, ...), custom_call_target="tpu_custom_call" | custom-call | flops 402653184 | bytes 2883584 | tf_op jit(solution)/shard_map/outer/pallas_call | solution.py:325
  109.5 1.8 %outer.5.refs_5_.refs_4_ = f32[1024,512]{1,0:T(8,128)S(1)} custom-call(bf16[128,2560]{1,0:T(8,128)(2,1)S(1)} %get-tuple-element.12.refs_4_.refs_0_.refs_6_, bf16[128,2560]{1,0:T(8,128)(2,1)S(1)} %collective-permute-done.10.rest_4_.refs_1_.refs_7_, bf16[32,2560]{1,0:T(8,128)(2,1)S(1)} %get-tuple-element.25.refs_2_.refs_8_, ...), custom_call_target="tpu_custom_call" | custom-call | flops 402653184 | bytes 2883584 | tf_op jit(solution)/shard_map/outer/pallas_call | solution.py:325
  111.3 16.7 %collective-permute-done.17.refs_1_.refs_3_ = bf16[96,2560]{1,0:T(8,128)(2,1)S(1)} collective-permute-done((bf16[96,2560]{1,0:T(8,128)(2,1)S(1)}, bf16[96,2560]{1,0:T(8,128)(2,1)S(1)}, u32[]{:S(2)}, u32[]{:S(2)}) %collective-permute-start.17) | collective-permute-done | bytes 491552 | tf_op jit(solution)/shard_map/ppermute | solution.py:34
  128.1 0.7 outer.8
  128.9 0.7 outer.7
  130.2 0.6 collective-permute-done.23.refs_6_
  130.8 0.9 collective-permute-done.22.refs_5_
  131.7 2.6 %outer.9 = f32[1024,512]{1,0:T(8,128)} custom-call(bf16[128,2560]{1,0:T(8,128)(2,1)S(1)} %collective-permute-done.16.refs_0_.refs_2_, bf16[96,2560]{1,0:T(8,128)(2,1)S(1)} %collective-permute-done.17.refs_1_.refs_3_, bf16[128,2560]{1,0:T(8,128)(2,1)S(1)} %collective-permute-done.16.refs_0_.refs_2_, ...), custom_call_target="tpu_custom_call" | custom-call | flops 234881024 | bytes 2555904 | tf_op jit(solution)/shard_map/outer/pallas_call | solution.py:325
  134.3 1.3 collective-permute-done.15.refs_1_
  135.6 1.3 join_rows.1
  (40 shorter events, 1.6 us)
Async XLA Ops:
  0.6 15.0 %copy-start = (bf16[1,128,8192]{2,1,0:T(8,128)(2,1)S(1)}, bf16[1,128,8192]{2,1,0:T(8,128)(2,1)}, u32[]{:S(2)}) copy-start(bf16[1,128,8192]{2,1,0:T(8,128)(2,1)} %param.11) | copy-start | bytes 6291460
  0.6 15.0 %collective-permute-start = (bf16[1024,1024]{1,0:T(8,128)(2,1)}, bf16[1024,1024]{1,0:T(8,128)(2,1)}, u32[]{:S(2)}, u32[]{:S(2)}) collective-permute-start(bf16[1024,1024]{1,0:T(8,128)(2,1)} %bitcast.25), channel_id=1, source_target_pairs={{0,1},{1,0},{2,3},{3,2},{4,5},{5,4},{6,7},{7,6},{8,9},{9,8},{10,11... | collective-permute-start | bytes 6291464 | tf_op jit(solution)/shard_map/ppermute | solution.py:51
  0.7 17.8 %collective-permute-start.1 = (bf16[128,1024]{1,0:T(8,128)(2,1)}, bf16[128,1024]{1,0:T(8,128)(2,1)S(1)}, u32[]{:S(2)}, u32[]{:S(2)}) collective-permute-start(bf16[128,1024]{1,0:T(8,128)(2,1)} %bitcast.27), channel_id=1, source_target_pairs={{0,1},{1,0},{2,3},{3,2},{4,5},{5,4},{6,7},{7,6},{8,14},{9,15},{10,... | collective-permute-start | bytes 786440 | tf_op jit(solution)/shard_map/ppermute | solution.py:34
  1.2 20.8 %collective-permute-start.2 = (bf16[128,1024]{1,0:T(8,128)(2,1)}, bf16[128,1024]{1,0:T(8,128)(2,1)S(1)}, u32[]{:S(2)}, u32[]{:S(2)}) collective-permute-start(bf16[128,1024]{1,0:T(8,128)(2,1)} %bitcast.28), channel_id=1, source_target_pairs={{0,1},{1,0},{2,3},{3,2},{4,5},{5,4},{6,7},{7,6},{8,12},{9,13},{10,... | collective-permute-start | bytes 786440 | tf_op jit(solution)/shard_map/ppermute | solution.py:34
  3.8 23.1 %collective-permute-start.3 = (bf16[128,1024]{1,0:T(8,128)(2,1)}, bf16[128,1024]{1,0:T(8,128)(2,1)S(1)}, u32[]{:S(2)}, u32[]{:S(2)}) collective-permute-start(bf16[128,1024]{1,0:T(8,128)(2,1)} %bitcast.29), channel_id=1, source_target_pairs={{0,1},{1,0},{2,3},{3,2},{4,5},{5,4},{6,7},{7,6},{8,10},{9,11},{10,... | collective-permute-start | bytes 786440 | tf_op jit(solution)/shard_map/ppermute | solution.py:34
  7.1 1.2 copy-start.3
  8.3 1.2 copy-start.4
  9.5 0.9 copy-start.7
  10.4 0.7 copy-start.8
  11.1 4.6 %copy-start.5 = (bf16[1,8192]{1,0:T(2,128)(2,1)S(1)}, bf16[1,8192]{1,0:T(2,128)(2,1)}, u32[]{:S(2)}) copy-start(bf16[1,8192]{1,0:T(2,128)(2,1)} %gain_ref.10) | copy-start | bytes 49156
  16.4 15.4 %copy-start.9 = (bf16[1,1024,1024]{2,1,0:T(8,128)(2,1)S(1)}, bf16[1,1024,1024]{2,1,0:T(8,128)(2,1)}, u32[]{:S(2)}) copy-start(bf16[1,1024,1024]{2,1,0:T(8,128)(2,1)} %param.21) | copy-start | bytes 6291460
  16.4 15.4 %copy-start.10 = (bf16[1,128,1024]{2,1,0:T(8,128)(2,1)S(1)}, bf16[1,128,1024]{2,1,0:T(8,128)(2,1)}, u32[]{:S(2)}) copy-start(bf16[1,128,1024]{2,1,0:T(8,128)(2,1)} %param.20) | copy-start | bytes 786436
  16.4 14.5 %collective-permute-start.4 = (bf16[32,2560]{1,0:T(8,128)(2,1)S(1)}, bf16[32,2560]{1,0:T(8,128)(2,1)S(1)}, u32[]{:S(2)}, u32[]{:S(2)}) collective-permute-start(bf16[32,2560]{1,0:T(8,128)(2,1)S(1)} %norm_forward.4.refs_0_), channel_id=1, source_target_pairs={{8,0},{9,1},{10,2},{11,3},{12,4},{13,5},{14,6},{15,7}} | collective-permute-start | bytes 491528 | tf_op jit(solution)/shard_map/ppermute | solution.py:40
  17.9 13.0 %collective-permute-start.5 = (bf16[32,2560]{1,0:T(8,128)(2,1)S(1)}, bf16[32,2560]{1,0:T(8,128)(2,1)S(1)}, u32[]{:S(2)}, u32[]{:S(2)}) collective-permute-start(bf16[32,2560]{1,0:T(8,128)(2,1)S(1)} %norm_forward.4.refs_0_), channel_id=1, source_target_pairs={{16,0},{17,1},{18,2},{19,3},{20,4},{21,5},{22,6},{23,7}} | collective-permute-start | bytes 491528 | tf_op jit(solution)/shard_map/ppermute | solution.py:40
  18.6 12.3 %collective-permute-start.6 = (bf16[32,2560]{1,0:T(8,128)(2,1)S(1)}, bf16[32,2560]{1,0:T(8,128)(2,1)S(1)}, u32[]{:S(2)}, u32[]{:S(2)}) collective-permute-start(bf16[32,2560]{1,0:T(8,128)(2,1)S(1)} %norm_forward.4.refs_0_), channel_id=1, source_target_pairs={{24,0},{25,1},{26,2},{27,3},{28,4},{29,5},{30,6},{31,7}} | collective-permute-start | bytes 491528 | tf_op jit(solution)/shard_map/ppermute | solution.py:40
  28.5 17.7 %collective-permute-start.10 = (bf16[128,2560]{1,0:T(8,128)(2,1)S(1)}, bf16[128,2560]{1,0:T(8,128)(2,1)S(1)}, u32[]{:S(2)}, u32[]{:S(2)}) collective-permute-start(bf16[128,2560]{1,0:T(8,128)(2,1)S(1)} %get-tuple-element.17), channel_id=1, source_target_pairs={{0,2},{1,3},{2,4},{3,5},{4,6},{5,7},{6,0},{7,1},{8,10},{9,11},{10,... | collective-permute-start | bytes 1966088 | tf_op jit(solution)/shard_map/ppermute | solution.py:34
  31.0 51.9 %copy-start.1 = (bf16[1,128,8192]{2,1,0:T(8,128)(2,1)S(1)}, bf16[1,128,8192]{2,1,0:T(8,128)(2,1)}, u32[]{:S(2)}) copy-start(bf16[1,128,8192]{2,1,0:T(8,128)(2,1)} %param.17) | copy-start | bytes 6291460
  31.0 51.9 %copy-start.2 = (bf16[1,128,8192]{2,1,0:T(8,128)(2,1)S(1)}, bf16[1,128,8192]{2,1,0:T(8,128)(2,1)}, u32[]{:S(2)}) copy-start(bf16[1,128,8192]{2,1,0:T(8,128)(2,1)} %param.19) | copy-start | bytes 6291460
  31.0 51.9 %copy-start.6 = (bf16[1,8192]{1,0:T(2,128)(2,1)S(1)}, bf16[1,8192]{1,0:T(2,128)(2,1)}, u32[]{:S(2)}) copy-start(bf16[1,8192]{1,0:T(2,128)(2,1)} %gain_ref.11) | copy-start | bytes 49156
  31.0 64.6 %collective-permute-start.18 = (bf16[128,2560]{1,0:T(8,128)(2,1)S(1)}, bf16[128,2560]{1,0:T(8,128)(2,1)S(1)}, u32[]{:S(2)}, u32[]{:S(2)}) collective-permute-start(bf16[128,2560]{1,0:T(8,128)(2,1)S(1)} %stack_rows.1.rest_4_), channel_id=1, source_target_pairs={{0,4},{1,5},{2,6},{3,7},{4,0},{5,1},{6,2},{7,3}} | collective-permute-start | bytes 1966088 | tf_op jit(solution)/shard_map/ppermute | solution.py:46
  37.2 29.9 %collective-permute-start.7 = (bf16[80,2048]{1,0:T(8,128)(2,1)S(1)}, bf16[80,2048]{1,0:T(8,128)(2,1)S(1)}, u32[]{:S(2)}, u32[]{:S(2)}) collective-permute-start(bf16[80,2048]{1,0:T(8,128)(2,1)S(1)} %get-tuple-element.14), channel_id=1, source_target_pairs={{0,1},{1,0},{2,3},{3,2},{4,5},{5,4},{6,7},{7,6},{8,10},{9,11},{10,... | collective-permute-start | bytes 983048 | tf_op jit(solution)/shard_map/ppermute | solution.py:34
  37.3 41.1 %collective-permute-start.8 = (bf16[80,2048]{1,0:T(8,128)(2,1)S(1)}, bf16[80,2048]{1,0:T(8,128)(2,1)S(1)}, u32[]{:S(2)}, u32[]{:S(2)}) collective-permute-start(bf16[80,2048]{1,0:T(8,128)(2,1)S(1)} %get-tuple-element.15), channel_id=1, source_target_pairs={{0,1},{1,0},{2,3},{3,2},{4,5},{5,4},{6,7},{7,6},{8,12},{9,13},{10,... | collective-permute-start | bytes 983048 | tf_op jit(solution)/shard_map/ppermute | solution.py:34
  39.3 43.5 %collective-permute-start.9 = (bf16[80,2048]{1,0:T(8,128)(2,1)S(1)}, bf16[80,2048]{1,0:T(8,128)(2,1)S(1)}, u32[]{:S(2)}, u32[]{:S(2)}) collective-permute-start(bf16[80,2048]{1,0:T(8,128)(2,1)S(1)} %get-tuple-element.16), channel_id=1, source_target_pairs={{0,1},{1,0},{2,3},{3,2},{4,5},{5,4},{6,7},{7,6},{8,14},{9,15},{10,... | collective-permute-start | bytes 983048 | tf_op jit(solution)/shard_map/ppermute | solution.py:34
  46.2 41.1 %collective-permute-start.12 = (bf16[48,2048]{1,0:T(8,128)(2,1)S(1)}, bf16[48,2048]{1,0:T(8,128)(2,1)S(1)}, u32[]{:S(2)}, u32[]{:S(2)}) collective-permute-start(bf16[48,2048]{1,0:T(8,128)(2,1)S(1)} %get-tuple-element.19), channel_id=1, source_target_pairs={{0,1},{1,0},{2,3},{3,2},{4,5},{5,4},{6,7},{7,6},{8,10},{9,11},{10,... | collective-permute-start | bytes 589832 | tf_op jit(solution)/shard_map/ppermute | solution.py:34
  67.2 22.2 %collective-permute-start.13 = (bf16[48,2048]{1,0:T(8,128)(2,1)S(1)}, bf16[48,2048]{1,0:T(8,128)(2,1)S(1)}, u32[]{:S(2)}, u32[]{:S(2)}) collective-permute-start(bf16[48,2048]{1,0:T(8,128)(2,1)S(1)} %get-tuple-element.20), channel_id=1, source_target_pairs={{0,1},{1,0},{2,3},{3,2},{4,5},{5,4},{6,7},{7,6},{8,12},{9,13},{10,... | collective-permute-start | bytes 589832 | tf_op jit(solution)/shard_map/ppermute | solution.py:34
  78.4 12.8 %collective-permute-start.14 = (bf16[48,2048]{1,0:T(8,128)(2,1)S(1)}, bf16[48,2048]{1,0:T(8,128)(2,1)S(1)}, u32[]{:S(2)}, u32[]{:S(2)}) collective-permute-start(bf16[48,2048]{1,0:T(8,128)(2,1)S(1)} %get-tuple-element.21), channel_id=1, source_target_pairs={{0,1},{1,0},{2,3},{3,2},{4,5},{5,4},{6,7},{7,6},{8,14},{9,15},{10,... | collective-permute-start | bytes 589832 | tf_op jit(solution)/shard_map/ppermute | solution.py:34
  85.4 50.3 %collective-permute-start.11 = (bf16[80,8192]{1,0:T(8,128)(2,1)S(1)}, bf16[80,8192]{1,0:T(8,128)(2,1)S(1)}, u32[]{:S(2)}, u32[]{:S(2)}) collective-permute-start(bf16[80,8192]{1,0:T(8,128)(2,1)S(1)} %norm_backward.2.rest_0_), channel_id=1, source_target_pairs={{8,0},{16,8},{24,16},{9,1},{17,9},{25,17},{10,2},{18,10},{26,18},{... | collective-permute-start | bytes 3932168 | tf_op jit(solution)/shard_map/ppermute | solution.py:25
  92.4 35.6 %collective-permute-start.17 = (bf16[96,2560]{1,0:T(8,128)(2,1)S(1)}, bf16[96,2560]{1,0:T(8,128)(2,1)S(1)}, u32[]{:S(2)}, u32[]{:S(2)}) collective-permute-start(bf16[96,2560]{1,0:T(8,128)(2,1)S(1)} %norm_forward.6.rest_0_), channel_id=1, source_target_pairs={{0,4},{1,5},{2,6},{3,7},{4,0},{5,1},{6,2},{7,3},{8,12},{9,13},{10,... | collective-permute-start | bytes 1474568 | tf_op jit(solution)/shard_map/ppermute | solution.py:34
  95.5 32.5 %collective-permute-start.16 = (bf16[128,2560]{1,0:T(8,128)(2,1)S(1)}, bf16[128,2560]{1,0:T(8,128)(2,1)S(1)}, u32[]{:S(2)}, u32[]{:S(2)}) collective-permute-start(bf16[128,2560]{1,0:T(8,128)(2,1)S(1)} %norm_forward.7.rest_4_), channel_id=1, source_target_pairs={{0,6},{1,7},{2,0},{3,1},{4,2},{5,3},{6,4},{7,5},{8,14},{9,15},{10,... | collective-permute-start | bytes 1966088 | tf_op jit(solution)/shard_map/ppermute | solution.py:34
  95.7 7.5 %collective-permute-start.19 = (bf16[32,2560]{1,0:T(8,128)(2,1)S(1)}, bf16[32,2560]{1,0:T(8,128)(2,1)S(1)}, u32[]{:S(2)}, u32[]{:S(2)}) collective-permute-start(bf16[32,2560]{1,0:T(8,128)(2,1)S(1)} %get-tuple-element.24), channel_id=1, source_target_pairs={{0,8},{1,9},{2,10},{3,11},{4,12},{5,13},{6,14},{7,15}} | collective-permute-start | bytes 491528 | tf_op jit(solution)/shard_map/ppermute | solution.py:40
  97.0 8.6 %collective-permute-start.20 = (bf16[32,2560]{1,0:T(8,128)(2,1)S(1)}, bf16[32,2560]{1,0:T(8,128)(2,1)S(1)}, u32[]{:S(2)}, u32[]{:S(2)}) collective-permute-start(bf16[32,2560]{1,0:T(8,128)(2,1)S(1)} %get-tuple-element.23), channel_id=1, source_target_pairs={{0,16},{1,17},{2,18},{3,19},{4,20},{5,21},{6,22},{7,23}} | collective-permute-start | bytes 491528 | tf_op jit(solution)/shard_map/ppermute | solution.py:40
  103.1 4.5 %collective-permute-start.21 = (bf16[32,2560]{1,0:T(8,128)(2,1)S(1)}, bf16[32,2560]{1,0:T(8,128)(2,1)S(1)}, u32[]{:S(2)}, u32[]{:S(2)}) collective-permute-start(bf16[32,2560]{1,0:T(8,128)(2,1)S(1)} %get-tuple-element.22), channel_id=1, source_target_pairs={{0,24},{1,25},{2,26},{3,27},{4,28},{5,29},{6,30},{7,31}} | collective-permute-start | bytes 491528 | tf_op jit(solution)/shard_map/ppermute | solution.py:40
  105.5 30.1 %collective-permute-start.15 = (bf16[48,8192]{1,0:T(8,128)(2,1)S(1)}, bf16[48,8192]{1,0:T(8,128)(2,1)S(1)}, u32[]{:S(2)}, u32[]{:S(2)}) collective-permute-start(bf16[48,8192]{1,0:T(8,128)(2,1)S(1)} %norm_backward.3.refs_12_), channel_id=1, source_target_pairs={{8,0},{16,8},{24,16},{9,1},{17,9},{25,17},{10,2},{18,10},{26,18},{... | collective-permute-start | bytes 2359304 | tf_op jit(solution)/shard_map/ppermute | solution.py:25
  128.8 2.0 %collective-permute-start.23 = (bf16[512,512]{1,0:T(8,128)(2,1)S(1)}, bf16[512,512]{1,0:T(8,128)(2,1)S(1)}, u32[]{:S(2)}, u32[]{:S(2)}) collective-permute-start(bf16[512,512]{1,0:T(8,128)(2,1)S(1)} %outer.8), channel_id=1, source_target_pairs={{0,1},{1,0},{2,3},{3,2},{4,5},{5,4},{6,7},{7,6},{8,9},{9,8},{10,11... | collective-permute-start | bytes 1572872 | tf_op jit(solution)/shard_map/ppermute | solution.py:51
  129.6 2.1 %collective-permute-start.22 = (bf16[512,512]{1,0:T(8,128)(2,1)S(1)}, bf16[512,512]{1,0:T(8,128)(2,1)S(1)}, u32[]{:S(2)}, u32[]{:S(2)}) collective-permute-start(bf16[512,512]{1,0:T(8,128)(2,1)S(1)} %outer.7), channel_id=1, source_target_pairs={{0,1},{1,0},{2,3},{3,2},{4,5},{5,4},{6,7},{7,6},{8,9},{9,8},{10,11... | collective-permute-start | bytes 1572872 | tf_op jit(solution)/shard_map/ppermute | solution.py:51

commit v6 on v5

--- a/solution.py
+++ b/solution.py
@@ -383,9 +383,9 @@
     ]
     backward = functools.partial(norm_backward, place, rows=frozen_input[0], gain=frozen_gain, grads=output_grad[0])
     above = backward(arrived[0], start=cuts[0], after=columns[1:])
-    kept = apply([middle], spread, tokens - spread, [above] + arrived[1][1:])
-    late = apply(near[1:], 0, tokens, kept)
-    above = [above, backward(arrived[1], start=cuts[1], after=late[:1])]
+    late = apply(near[1:], 0, tokens, [above] + [arrived[1][by] for by in near])
+    kept = apply([middle], spread, tokens - spread, late + arrived[1][1:])
+    above = [above, backward(arrived[1], start=cuts[1], after=kept)]
     below = [from_behind(half, "pipe", -1) for half in above]
     cot_below = join_rows(below)
 

time: 137 us -> 137 us (level)
  waiting for transfers between devices: 76.7 us -> 73.9 us
  starting transfers between devices: 26.1 us -> 28.5 us
    ppermute x12, waiting for transfers between devices: 68.4 us -> 61.5 us  [along_chips(): return lax.ppermute(array, ('pipe', 'dp'), pairs)]
    ppermute x2, waiting for transfers between devices: 1.3 us -> 4.1 us  [from_behind(): return lax.ppermute(array, axis, pairs)]
    ppermute x12, starting transfers between devices: 15.1 us -> 17.6 us  [along_chips(): return lax.ppermute(array, ('pipe', 'dp'), pairs)]
  transfers between devices with their start and end apart: 24 -> 24, of which waited for: 13 -> 10; matrix products, arithmetic and copies ran while one was open for 1% -> 1% of each run, Pallas kernels for 20% -> 20%
where the time goes in v6:
time: 137 us
  waiting for transfers between devices  73.9 us (54%)
  starting transfers between devices  28.5 us (21%)
  Pallas kernels  28.4 us (21%)
  local copies, waits for them, and re-layouts  4.85 us (4%)
    ppermute x12, waiting for transfers between devices, along_chips(): return lax.ppermute(array, ('pipe', 'dp'), pairs)  61.5 us
    ppermute x12, starting transfers between devices, along_chips(): return lax.ppermute(array, ('pipe', 'dp'), pairs)  17.6 us
    pallas_call x5, Pallas kernels, outer(): call(functools.partial(outer_kernel, [len(group) for group in groups], le...  7.79 us
    ppermute x6, waiting for transfers between devices, between_lines(): return lax.ppermute(array, ('pipe', 'dp'), pairs)  6.7 us
    ppermute x6, starting transfers between devices, between_lines(): return lax.ppermute(array, ('pipe', 'dp'), pairs)  5.4 us
    pallas_call x1, Pallas kernels, project(): call(functools.partial(project_kernel, chips, steps, cuts), 'project', 4...  5.38 us
    pallas_call x4, Pallas kernels, normalize(): call(functools.partial(norm_kernel, chips, ahead), 'norm_forward', 4 * co...  5.06 us
    pallas_call x1, Pallas kernels, attend(): call(attend_kernel, 'attend', 4 * tokens * tokens * queries.shape[1], 4 *...  4.48 us
  transfers between devices with their start and end apart: 24, of which 10 were waited for; matrix products, arithmetic and copies ran while one was open for 1% of the time, Pallas kernels for 20%

profile of v6, /device:TPU:10, one launch (start us, length us, event | category | flops | bytes accessed | tf_op | source)
XLA Modules:
  0.0 136.7 jit_solution(15729474451015255445)
XLA Ops:
  0.7 0.5 collective-permute-start.1
  1.2 2.6 %collective-permute-start.2 = (bf16[128,1024]{1,0:T(8,128)(2,1)}, bf16[128,1024]{1,0:T(8,128)(2,1)S(1)}, u32[]{:S(2)}, u32[]{:S(2)}) collective-permute-start(bf16[128,1024]{1,0:T(8,128)(2,1)} %bitcast.28), channel_id=1, source_target_pairs={{0,1},{1,0},{2,3},{3,2},{4,5},{5,4},{6,7},{7,6},{8,12},{9,13},{10,... | collective-permute-start | bytes 786440 | tf_op jit(solution)/shard_map/ppermute | solution.py:34
  3.8 2.5 %collective-permute-start.3 = (bf16[128,1024]{1,0:T(8,128)(2,1)}, bf16[128,1024]{1,0:T(8,128)(2,1)S(1)}, u32[]{:S(2)}, u32[]{:S(2)}) collective-permute-start(bf16[128,1024]{1,0:T(8,128)(2,1)} %bitcast.29), channel_id=1, source_target_pairs={{0,1},{1,0},{2,3},{3,2},{4,5},{5,4},{6,7},{7,6},{8,10},{9,11},{10,... | collective-permute-start | bytes 786440 | tf_op jit(solution)/shard_map/ppermute | solution.py:34
  6.3 0.8 copy.13.col_seg_ref
  7.1 1.2 copy-done.3
  8.3 1.2 copy-done.4
  9.5 0.9 copy-done.7
  10.4 0.7 copy-done.8
  11.1 4.5 %attend.1.cot_ref = bf16[128,512]{1,0:T(8,128)(2,1)S(1)} custom-call(bf16[128,4096]{1,0:T(8,128)(2,1)S(1)} %bitcast.21, bf16[128,512]{1,0:T(8,128)(2,1)S(1)} %bitcast.23, bf16[128,4096]{1,0:T(8,128)(2,1)S(1)} %bitcast.22, s32[1,128]{1,0:T(1,128)S(1)} %copy-done.8, s32[128,1]{1,0:T(8,128)S(1)} %copy.13.col_seg_ref), custom_call_target="tpu_custom_call" | custom-call | flops 268435456 | bytes 2097152 | tf_op jit(solution)/shard_map/attend/pallas_call | solution.py:180
  15.6 0.8 norm_forward.4.refs_0_
  16.4 1.4 %collective-permute-start.4 = (bf16[32,2560]{1,0:T(8,128)(2,1)S(1)}, bf16[32,2560]{1,0:T(8,128)(2,1)S(1)}, u32[]{:S(2)}, u32[]{:S(2)}) collective-permute-start(bf16[32,2560]{1,0:T(8,128)(2,1)S(1)} %norm_forward.4.refs_0_), channel_id=1, source_target_pairs={{8,0},{9,1},{10,2},{11,3},{12,4},{13,5},{14,6},{15,7}} | collective-permute-start | bytes 491528 | tf_op jit(solution)/shard_map/ppermute | solution.py:40
  17.9 0.7 collective-permute-start.5
  18.6 0.7 collective-permute-start.6
  19.2 2.8 %collective-permute-done.2.rest_1_.rest_2_ = bf16[128,1024]{1,0:T(8,128)(2,1)S(1)} collective-permute-done((bf16[128,1024]{1,0:T(8,128)(2,1)}, bf16[128,1024]{1,0:T(8,128)(2,1)S(1)}, u32[]{:S(2)}, u32[]{:S(2)}) %collective-permute-start.2) | collective-permute-done | bytes 262176 | tf_op jit(solution)/shard_map/ppermute | solution.py:34
  22.1 4.8 %collective-permute-done.3.rest_2_.rest_3_ = bf16[128,1024]{1,0:T(8,128)(2,1)S(1)} collective-permute-done((bf16[128,1024]{1,0:T(8,128)(2,1)}, bf16[128,1024]{1,0:T(8,128)(2,1)S(1)}, u32[]{:S(2)}, u32[]{:S(2)}) %collective-permute-start.3) | collective-permute-done | bytes 262176 | tf_op jit(solution)/shard_map/ppermute | solution.py:34
  26.9 1.5 %norm_forward.5 = (bf16[128,2560]{1,0:T(8,128)(2,1)S(1)}, bf16[128,2560]{1,0:T(8,128)(2,1)S(1)}) custom-call(s32[2]{0:T(128)S(1)} %pad_add_fusion.place_ref, bf16[128,8192]{1,0:T(8,128)(2,1)S(1)} %bitcast.14, bf16[1,8192]{1,0:T(2,128)(2,1)S(1)} %copy-done.5, bf16[128,512]{1,0:T(8,128)(2,1)S(1)} %attend.1.cot_ref, ...), custom_call_target="tpu_custom_call" | custom-call | flops 4194304 | bytes 3407872 | tf_op jit(solution)/shard_map/norm_forward/pallas_call | solution.py:92
  28.5 2.4 %collective-permute-start.10 = (bf16[128,2560]{1,0:T(8,128)(2,1)S(1)}, bf16[128,2560]{1,0:T(8,128)(2,1)S(1)}, u32[]{:S(2)}, u32[]{:S(2)}) collective-permute-start(bf16[128,2560]{1,0:T(8,128)(2,1)S(1)} %get-tuple-element.17), channel_id=1, source_target_pairs={{0,2},{1,3},{2,4},{3,5},{4,6},{5,7},{6,0},{7,1},{8,10},{9,11},{10,... | collective-permute-start | bytes 1966088 | tf_op jit(solution)/shard_map/ppermute | solution.py:34
  31.0 0.8 collective-permute-start.18
  31.9 5.4 %project.1 = (bf16[80,2048]{1,0:T(8,128)(2,1)S(1)}, bf16[80,2048]{1,0:T(8,128)(2,1)S(1)}, bf16[80,2048]{1,0:T(8,128)(2,1)S(1)}, bf16[80,2048]{1,0:T(8,128)(2,1)S...) custom-call(bf16[1024,1024]{1,0:T(8,128)(2,1)S(1)} %bitcast.26, ...), custom_call_target="tpu_custom_call" | custom-call | flops 2147483648 | bytes 7340032 | tf_op jit(solution)/shard_map/project/pallas_call | solution.py:231
  37.3 2.0 %collective-permute-start.8 = (bf16[80,2048]{1,0:T(8,128)(2,1)S(1)}, bf16[80,2048]{1,0:T(8,128)(2,1)S(1)}, u32[]{:S(2)}, u32[]{:S(2)}) collective-permute-start(bf16[80,2048]{1,0:T(8,128)(2,1)S(1)} %get-tuple-element.15), channel_id=1, source_target_pairs={{0,1},{1,0},{2,3},{3,2},{4,5},{5,4},{6,7},{7,6},{8,12},{9,13},{10,... | collective-permute-start | bytes 983048 | tf_op jit(solution)/shard_map/ppermute | solution.py:34
  39.3 1.0 collective-permute-start.9
  40.3 5.8 %collective-permute-done.10.rest_4_.refs_1_.refs_7_ = bf16[128,2560]{1,0:T(8,128)(2,1)S(1)} collective-permute-done((bf16[128,2560]{1,0:T(8,128)(2,1)S(1)}, bf16[128,2560]{1,0:T(8,128)(2,1)S(1)}, u32[]{:S(2)}, u32[]{:S(2)}) %collective-permute-start.10) | collective-permute-done | bytes 655392 | tf_op jit(solution)/shard_map/ppermute | solution.py:34
  46.2 2.4 %collective-permute-start.12 = (bf16[48,2048]{1,0:T(8,128)(2,1)S(1)}, bf16[48,2048]{1,0:T(8,128)(2,1)S(1)}, u32[]{:S(2)}, u32[]{:S(2)}) collective-permute-start(bf16[48,2048]{1,0:T(8,128)(2,1)S(1)} %get-tuple-element.19), channel_id=1, source_target_pairs={{0,1},{1,0},{2,3},{3,2},{4,5},{5,4},{6,7},{7,6},{8,10},{9,11},{10,... | collective-permute-start | bytes 589832 | tf_op jit(solution)/shard_map/ppermute | solution.py:34
  48.6 18.6 %collective-permute-done.7.rest_1_ = bf16[80,2048]{1,0:T(8,128)(2,1)S(1)} collective-permute-done((bf16[80,2048]{1,0:T(8,128)(2,1)S(1)}, bf16[80,2048]{1,0:T(8,128)(2,1)S(1)}, u32[]{:S(2)}, u32[]{:S(2)}) %collective-permute-start.7) | collective-permute-done | bytes 327712 | tf_op jit(solution)/shard_map/ppermute | solution.py:34
  67.2 15.4 %collective-permute-done.8.rest_2_ = bf16[80,2048]{1,0:T(8,128)(2,1)S(1)} collective-permute-done((bf16[80,2048]{1,0:T(8,128)(2,1)S(1)}, bf16[80,2048]{1,0:T(8,128)(2,1)S(1)}, u32[]{:S(2)}, u32[]{:S(2)}) %collective-permute-start.8) | collective-permute-done | bytes 327712 | tf_op jit(solution)/shard_map/ppermute | solution.py:34
  82.6 3.4 %collective-permute-start.13 = (bf16[48,2048]{1,0:T(8,128)(2,1)S(1)}, bf16[48,2048]{1,0:T(8,128)(2,1)S(1)}, u32[]{:S(2)}, u32[]{:S(2)}) collective-permute-start(bf16[48,2048]{1,0:T(8,128)(2,1)S(1)} %get-tuple-element.20), channel_id=1, source_target_pairs={{0,1},{1,0},{2,3},{3,2},{4,5},{5,4},{6,7},{7,6},{8,12},{9,13},{10,... | collective-permute-start | bytes 589832 | tf_op jit(solution)/shard_map/ppermute | solution.py:34
  86.0 2.5 %norm_backward.2.rest_0_ = bf16[80,8192]{1,0:T(8,128)(2,1)S(1)} custom-call(s32[2]{0:T(128)S(1)} %pad_add_fusion.place_ref, bf16[128,8192]{1,0:T(8,128)(2,1)S(1)} %bitcast.17, bf16[1,8192]{1,0:T(2,128)(2,1)S(1)} %copy-done.6, bf16[128,8192]{1,0:T(8,128)(2,1)S(1)} %bitcast.19, bf16[80,2048]{1,0:T(8,128)(2,1)S(1)} %get-tuple-element.13.rest_0_, ...), custom_call_target="tpu_custom_call" | custom-call | flops 6553600 | bytes 5242880 | tf_op jit(solution)/shard_map/norm_backward/pallas_call | solution.py:278
  88.5 1.9 %collective-permute-start.11 = (bf16[80,8192]{1,0:T(8,128)(2,1)S(1)}, bf16[80,8192]{1,0:T(8,128)(2,1)S(1)}, u32[]{:S(2)}, u32[]{:S(2)}) collective-permute-start(bf16[80,8192]{1,0:T(8,128)(2,1)S(1)} %norm_backward.2.rest_0_), channel_id=1, source_target_pairs={{8,0},{16,8},{24,16},{9,1},{17,9},{25,17},{10,2},{18,10},{26,18},{... | collective-permute-start | bytes 3932168 | tf_op jit(solution)/shard_map/ppermute | solution.py:25
  90.5 1.5 %norm_forward.6.rest_0_ = bf16[128,2560]{1,0:T(8,128)(2,1)S(1)} custom-call(s32[2]{0:T(128)S(1)} %pad_add_fusion.place_ref, bf16[128,8192]{1,0:T(8,128)(2,1)S(1)} %bitcast.15, bf16[1,8192]{1,0:T(2,128)(2,1)S(1)} %copy-done.5, bf16[128,512]{1,0:T(8,128)(2,1)S(1)} %attend.1.cot_ref, bf16[80,8192]{1,0:T(8,128)(2,1)S(1)} %norm_backward.2.rest_0_, ...), custom_call_target="tpu_custom_call" | custom-call | flops 4194304 | bytes 2752512 | tf_op jit(solution)/shard_map/norm_forward/pallas_call | solution.py:92
  92.1 1.3 norm_forward.7.rest_4_
  93.3 0.7 collective-permute-start.17
  94.1 1.3 collective-permute-start.19
  95.4 0.7 collective-permute-start.20
  96.1 6.7 %collective-permute-done.19.refs_3_.refs_9_ = bf16[32,2560]{1,0:T(8,128)(2,1)S(1)} collective-permute-done((bf16[32,2560]{1,0:T(8,128)(2,1)S(1)}, bf16[32,2560]{1,0:T(8,128)(2,1)S(1)}, u32[]{:S(2)}, u32[]{:S(2)}) %collective-permute-start.19) | collective-permute-done | bytes 163872 | tf_op jit(solution)/shard_map/ppermute | solution.py:40
  102.8 0.7 collective-permute-start.21
  103.4 1.7 %norm_backward.3.refs_12_ = bf16[48,8192]{1,0:T(8,128)(2,1)S(1)} custom-call(s32[2]{0:T(128)S(1)} %pad_add_fusion.place_ref, bf16[128,8192]{1,0:T(8,128)(2,1)S(1)} %bitcast.18, bf16[1,8192]{1,0:T(2,128)(2,1)S(1)} %copy-done.6, bf16[128,8192]{1,0:T(8,128)(2,1)S(1)} %bitcast.20, bf16[48,2048]{1,0:T(8,128)(2,1)S(1)} %get-tuple-element.18.rest_0_, ...), custom_call_target="tpu_custom_call" | custom-call | flops 3932160 | bytes 3145728 | tf_op jit(solution)/shard_map/norm_backward/pallas_call | solution.py:278
  105.2 2.1 %collective-permute-start.15 = (bf16[48,8192]{1,0:T(8,128)(2,1)S(1)}, bf16[48,8192]{1,0:T(8,128)(2,1)S(1)}, u32[]{:S(2)}, u32[]{:S(2)}) collective-permute-start(bf16[48,8192]{1,0:T(8,128)(2,1)S(1)} %norm_backward.3.refs_12_), channel_id=1, source_target_pairs={{8,0},{16,8},{24,16},{9,1},{17,9},{25,17},{10,2},{18,10},{26,18},{... | collective-permute-start | bytes 2359304 | tf_op jit(solution)/shard_map/ppermute | solution.py:25
  107.3 1.8 %outer.6.refs_4_ = f32[1024,512]{1,0:T(8,128)S(1)} custom-call(bf16[128,2560]{1,0:T(8,128)(2,1)S(1)} %get-tuple-element.12.refs_4_.refs_0_.refs_6_, bf16[128,2560]{1,0:T(8,128)(2,1)S(1)} %collective-permute-done.10.rest_4_.refs_1_.refs_7_, bf16[32,2560]{1,0:T(8,128)(2,1)S(1)} %get-tuple-element.25.refs_2_.refs_8_, ...), custom_call_target="tpu_custom_call" | custom-call | flops 402653184 | bytes 2883584 | tf_op jit(solution)/shard_map/outer/pallas_call | solution.py:325
  109.1 1.8 %outer.5.refs_5_.refs_4_ = f32[1024,512]{1,0:T(8,128)S(1)} custom-call(bf16[128,2560]{1,0:T(8,128)(2,1)S(1)} %get-tuple-element.12.refs_4_.refs_0_.refs_6_, bf16[128,2560]{1,0:T(8,128)(2,1)S(1)} %collective-permute-done.10.rest_4_.refs_1_.refs_7_, bf16[32,2560]{1,0:T(8,128)(2,1)S(1)} %get-tuple-element.25.refs_2_.refs_8_, ...), custom_call_target="tpu_custom_call" | custom-call | flops 402653184 | bytes 2883584 | tf_op jit(solution)/shard_map/outer/pallas_call | solution.py:325
  111.0 13.9 %collective-permute-done.17.refs_1_.refs_3_ = bf16[96,2560]{1,0:T(8,128)(2,1)S(1)} collective-permute-done((bf16[96,2560]{1,0:T(8,128)(2,1)S(1)}, bf16[96,2560]{1,0:T(8,128)(2,1)S(1)}, u32[]{:S(2)}, u32[]{:S(2)}) %collective-permute-start.17) | collective-permute-done | bytes 491552 | tf_op jit(solution)/shard_map/ppermute | solution.py:34
  124.9 0.7 outer.8
  125.7 0.7 outer.7
  126.5 0.5 collective-permute-start.22
  127.0 0.6 collective-permute-done.23.refs_6_
  127.6 0.9 collective-permute-done.22.refs_5_
  128.6 2.7 %outer.9 = f32[1024,512]{1,0:T(8,128)} custom-call(bf16[128,2560]{1,0:T(8,128)(2,1)S(1)} %collective-permute-done.16.refs_0_.refs_2_, bf16[96,2560]{1,0:T(8,128)(2,1)S(1)} %collective-permute-done.17.refs_1_.refs_3_, bf16[128,2560]{1,0:T(8,128)(2,1)S(1)} %collective-permute-done.16.refs_0_.refs_2_, ...), custom_call_target="tpu_custom_call" | custom-call | flops 234881024 | bytes 2555904 | tf_op jit(solution)/shard_map/outer/pallas_call | solution.py:325
  131.2 4.1 %collective-permute-done.15.refs_1_ = bf16[48,8192]{1,0:T(8,128)(2,1)S(1)} collective-permute-done((bf16[48,8192]{1,0:T(8,128)(2,1)S(1)}, bf16[48,8192]{1,0:T(8,128)(2,1)S(1)}, u32[]{:S(2)}, u32[]{:S(2)}) %collective-permute-start.15) | collective-permute-done | bytes 786464 | tf_op jit(solution)/shard_map/ppermute | solution.py:25
  135.3 1.3 join_rows.1
  (40 shorter events, 0.5 us)
Async XLA Ops:
  0.6 15.0 %copy-start = (bf16[1,128,8192]{2,1,0:T(8,128)(2,1)S(1)}, bf16[1,128,8192]{2,1,0:T(8,128)(2,1)}, u32[]{:S(2)}) copy-start(bf16[1,128,8192]{2,1,0:T(8,128)(2,1)} %param.11) | copy-start | bytes 6291460
  0.6 15.0 %collective-permute-start = (bf16[1024,1024]{1,0:T(8,128)(2,1)}, bf16[1024,1024]{1,0:T(8,128)(2,1)}, u32[]{:S(2)}, u32[]{:S(2)}) collective-permute-start(bf16[1024,1024]{1,0:T(8,128)(2,1)} %bitcast.25), channel_id=1, source_target_pairs={{0,1},{1,0},{2,3},{3,2},{4,5},{5,4},{6,7},{7,6},{8,9},{9,8},{10,11... | collective-permute-start | bytes 6291464 | tf_op jit(solution)/shard_map/ppermute | solution.py:51
  0.7 17.8 %collective-permute-start.1 = (bf16[128,1024]{1,0:T(8,128)(2,1)}, bf16[128,1024]{1,0:T(8,128)(2,1)S(1)}, u32[]{:S(2)}, u32[]{:S(2)}) collective-permute-start(bf16[128,1024]{1,0:T(8,128)(2,1)} %bitcast.27), channel_id=1, source_target_pairs={{0,1},{1,0},{2,3},{3,2},{4,5},{5,4},{6,7},{7,6},{8,14},{9,15},{10,... | collective-permute-start | bytes 786440 | tf_op jit(solution)/shard_map/ppermute | solution.py:34
  1.2 20.8 %collective-permute-start.2 = (bf16[128,1024]{1,0:T(8,128)(2,1)}, bf16[128,1024]{1,0:T(8,128)(2,1)S(1)}, u32[]{:S(2)}, u32[]{:S(2)}) collective-permute-start(bf16[128,1024]{1,0:T(8,128)(2,1)} %bitcast.28), channel_id=1, source_target_pairs={{0,1},{1,0},{2,3},{3,2},{4,5},{5,4},{6,7},{7,6},{8,12},{9,13},{10,... | collective-permute-start | bytes 786440 | tf_op jit(solution)/shard_map/ppermute | solution.py:34
  3.8 23.1 %collective-permute-start.3 = (bf16[128,1024]{1,0:T(8,128)(2,1)}, bf16[128,1024]{1,0:T(8,128)(2,1)S(1)}, u32[]{:S(2)}, u32[]{:S(2)}) collective-permute-start(bf16[128,1024]{1,0:T(8,128)(2,1)} %bitcast.29), channel_id=1, source_target_pairs={{0,1},{1,0},{2,3},{3,2},{4,5},{5,4},{6,7},{7,6},{8,10},{9,11},{10,... | collective-permute-start | bytes 786440 | tf_op jit(solution)/shard_map/ppermute | solution.py:34
  7.1 1.2 copy-start.3
  8.3 1.2 copy-start.4
  9.5 0.9 copy-start.7
  10.4 0.7 copy-start.8
  11.1 4.6 %copy-start.5 = (bf16[1,8192]{1,0:T(2,128)(2,1)S(1)}, bf16[1,8192]{1,0:T(2,128)(2,1)}, u32[]{:S(2)}) copy-start(bf16[1,8192]{1,0:T(2,128)(2,1)} %gain_ref.10) | copy-start | bytes 49156
  16.4 15.4 %copy-start.9 = (bf16[1,1024,1024]{2,1,0:T(8,128)(2,1)S(1)}, bf16[1,1024,1024]{2,1,0:T(8,128)(2,1)}, u32[]{:S(2)}) copy-start(bf16[1,1024,1024]{2,1,0:T(8,128)(2,1)} %param.21) | copy-start | bytes 6291460
  16.4 15.4 %copy-start.10 = (bf16[1,128,1024]{2,1,0:T(8,128)(2,1)S(1)}, bf16[1,128,1024]{2,1,0:T(8,128)(2,1)}, u32[]{:S(2)}) copy-start(bf16[1,128,1024]{2,1,0:T(8,128)(2,1)} %param.20) | copy-start | bytes 786436
  16.4 14.5 %collective-permute-start.4 = (bf16[32,2560]{1,0:T(8,128)(2,1)S(1)}, bf16[32,2560]{1,0:T(8,128)(2,1)S(1)}, u32[]{:S(2)}, u32[]{:S(2)}) collective-permute-start(bf16[32,2560]{1,0:T(8,128)(2,1)S(1)} %norm_forward.4.refs_0_), channel_id=1, source_target_pairs={{8,0},{9,1},{10,2},{11,3},{12,4},{13,5},{14,6},{15,7}} | collective-permute-start | bytes 491528 | tf_op jit(solution)/shard_map/ppermute | solution.py:40
  17.9 13.0 %collective-permute-start.5 = (bf16[32,2560]{1,0:T(8,128)(2,1)S(1)}, bf16[32,2560]{1,0:T(8,128)(2,1)S(1)}, u32[]{:S(2)}, u32[]{:S(2)}) collective-permute-start(bf16[32,2560]{1,0:T(8,128)(2,1)S(1)} %norm_forward.4.refs_0_), channel_id=1, source_target_pairs={{16,0},{17,1},{18,2},{19,3},{20,4},{21,5},{22,6},{23,7}} | collective-permute-start | bytes 491528 | tf_op jit(solution)/shard_map/ppermute | solution.py:40
  18.6 12.3 %collective-permute-start.6 = (bf16[32,2560]{1,0:T(8,128)(2,1)S(1)}, bf16[32,2560]{1,0:T(8,128)(2,1)S(1)}, u32[]{:S(2)}, u32[]{:S(2)}) collective-permute-start(bf16[32,2560]{1,0:T(8,128)(2,1)S(1)} %norm_forward.4.refs_0_), channel_id=1, source_target_pairs={{24,0},{25,1},{26,2},{27,3},{28,4},{29,5},{30,6},{31,7}} | collective-permute-start | bytes 491528 | tf_op jit(solution)/shard_map/ppermute | solution.py:40
  28.5 17.7 %collective-permute-start.10 = (bf16[128,2560]{1,0:T(8,128)(2,1)S(1)}, bf16[128,2560]{1,0:T(8,128)(2,1)S(1)}, u32[]{:S(2)}, u32[]{:S(2)}) collective-permute-start(bf16[128,2560]{1,0:T(8,128)(2,1)S(1)} %get-tuple-element.17), channel_id=1, source_target_pairs={{0,2},{1,3},{2,4},{3,5},{4,6},{5,7},{6,0},{7,1},{8,10},{9,11},{10,... | collective-permute-start | bytes 1966088 | tf_op jit(solution)/shard_map/ppermute | solution.py:34
  31.0 55.0 %copy-start.1 = (bf16[1,128,8192]{2,1,0:T(8,128)(2,1)S(1)}, bf16[1,128,8192]{2,1,0:T(8,128)(2,1)}, u32[]{:S(2)}) copy-start(bf16[1,128,8192]{2,1,0:T(8,128)(2,1)} %param.17) | copy-start | bytes 6291460
  31.0 55.0 %copy-start.2 = (bf16[1,128,8192]{2,1,0:T(8,128)(2,1)S(1)}, bf16[1,128,8192]{2,1,0:T(8,128)(2,1)}, u32[]{:S(2)}) copy-start(bf16[1,128,8192]{2,1,0:T(8,128)(2,1)} %param.19) | copy-start | bytes 6291460
  31.0 55.0 %copy-start.6 = (bf16[1,8192]{1,0:T(2,128)(2,1)S(1)}, bf16[1,8192]{1,0:T(2,128)(2,1)}, u32[]{:S(2)}) copy-start(bf16[1,8192]{1,0:T(2,128)(2,1)} %gain_ref.11) | copy-start | bytes 49156
  31.0 63.0 %collective-permute-start.18 = (bf16[128,2560]{1,0:T(8,128)(2,1)S(1)}, bf16[128,2560]{1,0:T(8,128)(2,1)S(1)}, u32[]{:S(2)}, u32[]{:S(2)}) collective-permute-start(bf16[128,2560]{1,0:T(8,128)(2,1)S(1)} %stack_rows.1.rest_4_), channel_id=1, source_target_pairs={{0,4},{1,5},{2,6},{3,7},{4,0},{5,1},{6,2},{7,3}} | collective-permute-start | bytes 1966088 | tf_op jit(solution)/shard_map/ppermute | solution.py:46
  37.2 29.9 %collective-permute-start.7 = (bf16[80,2048]{1,0:T(8,128)(2,1)S(1)}, bf16[80,2048]{1,0:T(8,128)(2,1)S(1)}, u32[]{:S(2)}, u32[]{:S(2)}) collective-permute-start(bf16[80,2048]{1,0:T(8,128)(2,1)S(1)} %get-tuple-element.14), channel_id=1, source_target_pairs={{0,1},{1,0},{2,3},{3,2},{4,5},{5,4},{6,7},{7,6},{8,10},{9,11},{10,... | collective-permute-start | bytes 983048 | tf_op jit(solution)/shard_map/ppermute | solution.py:34
  37.3 45.3 %collective-permute-start.8 = (bf16[80,2048]{1,0:T(8,128)(2,1)S(1)}, bf16[80,2048]{1,0:T(8,128)(2,1)S(1)}, u32[]{:S(2)}, u32[]{:S(2)}) collective-permute-start(bf16[80,2048]{1,0:T(8,128)(2,1)S(1)} %get-tuple-element.15), channel_id=1, source_target_pairs={{0,1},{1,0},{2,3},{3,2},{4,5},{5,4},{6,7},{7,6},{8,12},{9,13},{10,... | collective-permute-start | bytes 983048 | tf_op jit(solution)/shard_map/ppermute | solution.py:34
  39.3 46.7 %collective-permute-start.9 = (bf16[80,2048]{1,0:T(8,128)(2,1)S(1)}, bf16[80,2048]{1,0:T(8,128)(2,1)S(1)}, u32[]{:S(2)}, u32[]{:S(2)}) collective-permute-start(bf16[80,2048]{1,0:T(8,128)(2,1)S(1)} %get-tuple-element.16), channel_id=1, source_target_pairs={{0,1},{1,0},{2,3},{3,2},{4,5},{5,4},{6,7},{7,6},{8,14},{9,15},{10,... | collective-permute-start | bytes 983048 | tf_op jit(solution)/shard_map/ppermute | solution.py:34
  46.2 44.3 %collective-permute-start.12 = (bf16[48,2048]{1,0:T(8,128)(2,1)S(1)}, bf16[48,2048]{1,0:T(8,128)(2,1)S(1)}, u32[]{:S(2)}, u32[]{:S(2)}) collective-permute-start(bf16[48,2048]{1,0:T(8,128)(2,1)S(1)} %get-tuple-element.19), channel_id=1, source_target_pairs={{0,1},{1,0},{2,3},{3,2},{4,5},{5,4},{6,7},{7,6},{8,10},{9,11},{10,... | collective-permute-start | bytes 589832 | tf_op jit(solution)/shard_map/ppermute | solution.py:34
  67.2 23.3 %collective-permute-start.14 = (bf16[48,2048]{1,0:T(8,128)(2,1)S(1)}, bf16[48,2048]{1,0:T(8,128)(2,1)S(1)}, u32[]{:S(2)}, u32[]{:S(2)}) collective-permute-start(bf16[48,2048]{1,0:T(8,128)(2,1)S(1)} %get-tuple-element.21), channel_id=1, source_target_pairs={{0,1},{1,0},{2,3},{3,2},{4,5},{5,4},{6,7},{7,6},{8,14},{9,15},{10,... | collective-permute-start | bytes 589832 | tf_op jit(solution)/shard_map/ppermute | solution.py:34
  82.6 9.5 %collective-permute-start.13 = (bf16[48,2048]{1,0:T(8,128)(2,1)S(1)}, bf16[48,2048]{1,0:T(8,128)(2,1)S(1)}, u32[]{:S(2)}, u32[]{:S(2)}) collective-permute-start(bf16[48,2048]{1,0:T(8,128)(2,1)S(1)} %get-tuple-element.20), channel_id=1, source_target_pairs={{0,1},{1,0},{2,3},{3,2},{4,5},{5,4},{6,7},{7,6},{8,12},{9,13},{10,... | collective-permute-start | bytes 589832 | tf_op jit(solution)/shard_map/ppermute | solution.py:34
  88.5 46.8 %collective-permute-start.11 = (bf16[80,8192]{1,0:T(8,128)(2,1)S(1)}, bf16[80,8192]{1,0:T(8,128)(2,1)S(1)}, u32[]{:S(2)}, u32[]{:S(2)}) collective-permute-start(bf16[80,8192]{1,0:T(8,128)(2,1)S(1)} %norm_backward.2.rest_0_), channel_id=1, source_target_pairs={{8,0},{16,8},{24,16},{9,1},{17,9},{25,17},{10,2},{18,10},{26,18},{... | collective-permute-start | bytes 3932168 | tf_op jit(solution)/shard_map/ppermute | solution.py:25
  92.0 32.9 %collective-permute-start.16 = (bf16[128,2560]{1,0:T(8,128)(2,1)S(1)}, bf16[128,2560]{1,0:T(8,128)(2,1)S(1)}, u32[]{:S(2)}, u32[]{:S(2)}) collective-permute-start(bf16[128,2560]{1,0:T(8,128)(2,1)S(1)} %norm_forward.6.rest_0_), channel_id=1, source_target_pairs={{0,6},{1,7},{2,0},{3,1},{4,2},{5,3},{6,4},{7,5},{8,14},{9,15},{10,... | collective-permute-start | bytes 1966088 | tf_op jit(solution)/shard_map/ppermute | solution.py:34
  93.3 31.6 %collective-permute-start.17 = (bf16[96,2560]{1,0:T(8,128)(2,1)S(1)}, bf16[96,2560]{1,0:T(8,128)(2,1)S(1)}, u32[]{:S(2)}, u32[]{:S(2)}) collective-permute-start(bf16[96,2560]{1,0:T(8,128)(2,1)S(1)} %norm_forward.7.rest_4_), channel_id=1, source_target_pairs={{0,4},{1,5},{2,6},{3,7},{4,0},{5,1},{6,2},{7,3},{8,12},{9,13},{10,... | collective-permute-start | bytes 1474568 | tf_op jit(solution)/shard_map/ppermute | solution.py:34
  94.1 8.7 %collective-permute-start.19 = (bf16[32,2560]{1,0:T(8,128)(2,1)S(1)}, bf16[32,2560]{1,0:T(8,128)(2,1)S(1)}, u32[]{:S(2)}, u32[]{:S(2)}) collective-permute-start(bf16[32,2560]{1,0:T(8,128)(2,1)S(1)} %get-tuple-element.24), channel_id=1, source_target_pairs={{0,8},{1,9},{2,10},{3,11},{4,12},{5,13},{6,14},{7,15}} | collective-permute-start | bytes 491528 | tf_op jit(solution)/shard_map/ppermute | solution.py:40
  95.4 9.8 %collective-permute-start.20 = (bf16[32,2560]{1,0:T(8,128)(2,1)S(1)}, bf16[32,2560]{1,0:T(8,128)(2,1)S(1)}, u32[]{:S(2)}, u32[]{:S(2)}) collective-permute-start(bf16[32,2560]{1,0:T(8,128)(2,1)S(1)} %get-tuple-element.23), channel_id=1, source_target_pairs={{0,16},{1,17},{2,18},{3,19},{4,20},{5,21},{6,22},{7,23}} | collective-permute-start | bytes 491528 | tf_op jit(solution)/shard_map/ppermute | solution.py:40
  102.8 4.5 %collective-permute-start.21 = (bf16[32,2560]{1,0:T(8,128)(2,1)S(1)}, bf16[32,2560]{1,0:T(8,128)(2,1)S(1)}, u32[]{:S(2)}, u32[]{:S(2)}) collective-permute-start(bf16[32,2560]{1,0:T(8,128)(2,1)S(1)} %get-tuple-element.22), channel_id=1, source_target_pairs={{0,24},{1,25},{2,26},{3,27},{4,28},{5,29},{6,30},{7,31}} | collective-permute-start | bytes 491528 | tf_op jit(solution)/shard_map/ppermute | solution.py:40
  105.2 30.1 %collective-permute-start.15 = (bf16[48,8192]{1,0:T(8,128)(2,1)S(1)}, bf16[48,8192]{1,0:T(8,128)(2,1)S(1)}, u32[]{:S(2)}, u32[]{:S(2)}) collective-permute-start(bf16[48,8192]{1,0:T(8,128)(2,1)S(1)} %norm_backward.3.refs_12_), channel_id=1, source_target_pairs={{8,0},{16,8},{24,16},{9,1},{17,9},{25,17},{10,2},{18,10},{26,18},{... | collective-permute-start | bytes 2359304 | tf_op jit(solution)/shard_map/ppermute | solution.py:25
  125.7 2.0 %collective-permute-start.23 = (bf16[512,512]{1,0:T(8,128)(2,1)S(1)}, bf16[512,512]{1,0:T(8,128)(2,1)S(1)}, u32[]{:S(2)}, u32[]{:S(2)}) collective-permute-start(bf16[512,512]{1,0:T(8,128)(2,1)S(1)} %outer.8), channel_id=1, source_target_pairs={{0,1},{1,0},{2,3},{3,2},{4,5},{5,4},{6,7},{7,6},{8,9},{9,8},{10,11... | collective-permute-start | bytes 1572872 | tf_op jit(solution)/shard_map/ppermute | solution.py:51
  126.5 2.1 %collective-permute-start.22 = (bf16[512,512]{1,0:T(8,128)(2,1)S(1)}, bf16[512,512]{1,0:T(8,128)(2,1)S(1)}, u32[]{:S(2)}, u32[]{:S(2)}) collective-permute-start(bf16[512,512]{1,0:T(8,128)(2,1)S(1)} %outer.7), channel_id=1, source_target_pairs={{0,1},{1,0},{2,3},{3,2},{4,5},{5,4},{6,7},{7,6},{8,9},{9,8},{10,11... | collective-permute-start | bytes 1572872 | tf_op jit(solution)/shard_map/ppermute | solution.py:51
